TPU v7x, 256 devices: a whole 4x4x8 slice. The times are simulated.
256 devices in a mesh: tile: 32 (over x, z_hi, core), mode: 8 (over z_lo, y).
Axes of the slice: x: 4, y: 4, z: 8 (z_hi: 4, z_lo: 2; z = z_hi * 2 + z_lo), core: 2. Of those that a mesh axis runs over, the one named last changes fastest.
Arguments:
- object_slices: bfloat16 [3, 2, 8192, 512], P(None, None, 'tile'), may hold values from -4 to 4
- probe_modes: bfloat16 [8, 2, 256, 256], P('mode'), may hold values from -2.09375 to 2.09375
- positions: int32 [128, 2], P('tile'), may hold values from 0 to 255
- measured: float32 [128, 256, 256], P('tile'), may hold values from 0.3 to 3
Outputs:
- object_grad: float32 [3, 2, 8192, 512], P(None, None, ('tile', 'mode'))
- probe_grad: float32 [8, 2, 256, 256], P('mode')
Inputs may be any that keep to these rules, and one draw needn't show every extreme that they name: `positions`: column 0 is a row offset from the top of the strip of 256 rows held by the listing tile index, column 1 a column offset; a window covers 256 x 256 cells.
All inputs are finite; a program needn't handle non-finite values.
Results may differ from a plain program's by a relative error of at most 0.035.
Values may be sent and summed in bfloat16 or wider, within the bound.
No kernel may reach another device: no remote copies, remote signals or barrier semaphores. Data moves between devices by JAX's collectives and lax.ppermute only.
A program may use at most 128 MiB of HBM per device.

v0:
```python
import math

import jax
import jax.numpy as jnp
from jax import lax
from jax.sharding import PartitionSpec as P

fresnel = 0.4


def from_behind(block, axis, distance):
    devices = range(lax.axis_size(axis))
    route = [((i - distance) % len(devices), i) for i in devices]
    return lax.ppermute(block, axis, route)


def tables(size):
    index = jnp.arange(size, dtype=jnp.int32)
    folded = index[:, None] * index[None, :] % size
    angle = 2.0 * math.pi / size * folded.astype(jnp.float32)
    scale = 1.0 / math.sqrt(size)
    table_real = (jnp.cos(angle) * scale).astype(jnp.bfloat16)
    table_imag = (-jnp.sin(angle) * scale).astype(jnp.bfloat16)
    freq = ((index + size // 2) % size - size // 2).astype(jnp.float32)
    phase = (
        -math.pi * fresnel / size * (freq[:, None] * freq[:, None] + freq[None, :] * freq[None, :])
    )
    return (table_real, table_imag, jnp.cos(phase), jnp.sin(phase))


def product(first, second, form):
    return jnp.einsum(form, first, second, preferred_element_type=jnp.float32)


def transform(real, imag, table_real, table_imag):
    left_form = "jk,pkl->pjl"
    right_form = "pjk,kl->pjl"
    mid_real = (product(table_real, real, left_form) - product(table_imag, imag, left_form)).astype(
        jnp.bfloat16
    )
    mid_imag = (product(table_real, imag, left_form) + product(table_imag, real, left_form)).astype(
        jnp.bfloat16
    )
    out_real = product(mid_real, table_real, right_form) - product(mid_imag, table_imag, right_form)
    out_imag = product(mid_real, table_imag, right_form) + product(mid_imag, table_real, right_form)
    return (out_real, out_imag)


def propagate(real, imag, tab, sign):
    table_real, table_imag, kernel_real, kernel_imag = tab
    freq_real, freq_imag = transform(real, imag, table_real, table_imag)
    turned = sign * kernel_imag
    mixed_real = (freq_real * kernel_real - freq_imag * turned).astype(jnp.bfloat16)
    mixed_imag = (freq_real * turned + freq_imag * kernel_real).astype(jnp.bfloat16)
    back_real, back_imag = transform(mixed_real, mixed_imag, table_real, -table_imag)
    return (back_real.astype(jnp.bfloat16), back_imag.astype(jnp.bfloat16))


def windows(region, rows, columns, patch):
    depth = region.shape[0]
    zero = jnp.zeros((), jnp.int32)

    def single(row, column):
        return lax.dynamic_slice(region, (zero, zero, row, column), (depth, 2, patch, patch))

    return jax.vmap(single)(rows, columns)


def forward(probe_real, probe_imag, patches, tab):
    count = patches.shape[0]
    depth = patches.shape[1]
    wave_real = jnp.broadcast_to(probe_real, (count,) + probe_real.shape)
    wave_imag = jnp.broadcast_to(probe_imag, (count,) + probe_imag.shape)
    waves = []
    for layer in range(depth):
        obj_real = patches[:, layer, 0].astype(jnp.float32)
        obj_imag = patches[:, layer, 1].astype(jnp.float32)
        waves.append((wave_real, wave_imag))
        cur_real = wave_real.astype(jnp.float32)
        cur_imag = wave_imag.astype(jnp.float32)
        exit_real = (cur_real * obj_real - cur_imag * obj_imag).astype(jnp.bfloat16)
        exit_imag = (cur_real * obj_imag + cur_imag * obj_real).astype(jnp.bfloat16)
        if layer + 1 < depth:
            wave_real, wave_imag = propagate(exit_real, exit_imag, tab, 1.0)
    far_real, far_imag = transform(exit_real, exit_imag, tab[0], tab[1])
    return (waves, far_real, far_imag)


def backward(waves, far_real, far_imag, residual, patches, tab):
    depth = patches.shape[1]
    grad_real = (residual * far_real).astype(jnp.bfloat16)
    grad_imag = (residual * far_imag).astype(jnp.bfloat16)
    back_real, back_imag = transform(grad_real, grad_imag, tab[0], -tab[1])
    back_real = back_real.astype(jnp.bfloat16)
    back_imag = back_imag.astype(jnp.bfloat16)
    pieces = [None] * depth
    probe_piece = None
    for layer in reversed(range(depth)):
        cur_real = waves[layer][0].astype(jnp.float32)
        cur_imag = waves[layer][1].astype(jnp.float32)
        obj_real = patches[:, layer, 0].astype(jnp.float32)
        obj_imag = patches[:, layer, 1].astype(jnp.float32)
        gin_real = back_real.astype(jnp.float32)
        gin_imag = back_imag.astype(jnp.float32)
        pieces[layer] = jnp.stack(
            [cur_real * gin_real + cur_imag * gin_imag, cur_real * gin_imag - cur_imag * gin_real],
            axis=1,
        )
        wave_grad_real = obj_real * gin_real + obj_imag * gin_imag
        wave_grad_imag = obj_real * gin_imag - obj_imag * gin_real
        if layer > 0:
            back_real, back_imag = propagate(
                wave_grad_real.astype(jnp.bfloat16), wave_grad_imag.astype(jnp.bfloat16), tab, -1.0
            )
        else:
            probe_piece = jnp.stack(
                [jnp.sum(wave_grad_real, axis=0), jnp.sum(wave_grad_imag, axis=0)]
            )
    return (jnp.stack(pieces, axis=1), probe_piece)


def on_device(object_slices, probe_modes, positions, measured):
    depth = object_slices.shape[0]
    strip = object_slices.shape[2]
    breadth = object_slices.shape[3]
    patch = probe_modes.shape[-1]
    count = positions.shape[0]
    tab = tables(patch)
    following = from_behind(object_slices, "tile", -1)
    region = jnp.concatenate([object_slices, following], axis=2)
    rows = positions[:, 0]
    columns = positions[:, 1]
    patches = windows(region, rows, columns, patch)
    mode_index = 0
    waves, far_real, far_imag = forward(
        probe_modes[mode_index, 0], probe_modes[mode_index, 1], patches, tab
    )
    states = [(waves, far_real, far_imag)]
    intensity = far_real * far_real + far_imag * far_imag
    residual = lax.psum(intensity.astype(jnp.bfloat16), "mode").astype(jnp.float32) - measured
    pieces = jnp.zeros((count, depth, 2, patch, patch), jnp.float32)
    mode_index = 0
    waves, far_real, far_imag = states[mode_index]
    mode_pieces, probe_piece = backward(waves, far_real, far_imag, residual, patches, tab)
    pieces = mode_pieces
    probe_list = [probe_piece]
    probe_grad = lax.psum(jnp.stack(probe_list).astype(jnp.bfloat16), "tile").astype(jnp.float32)
    zero = jnp.zeros((), jnp.int32)

    def place(index, total):
        begin = (zero, zero, rows[index], columns[index])
        current = lax.dynamic_slice(total, begin, (depth, 2, patch, patch))
        return lax.dynamic_update_slice(total, current + pieces[index], begin)

    grad = lax.fori_loop(0, count, place, jnp.zeros((depth, 2, 2 * strip, breadth), jnp.float32))
    spill = from_behind(grad[:, :, strip:].astype(jnp.bfloat16), "tile", 1).astype(jnp.float32)
    owned = grad[:, :, :strip] + spill
    object_grad = lax.psum_scatter(
        owned.astype(jnp.bfloat16), "mode", scatter_dimension=2, tiled=True
    ).astype(jnp.float32)
    return (object_grad, probe_grad)


def solution(mesh):
    placed = (
        P(None, None, "tile", None),
        P("mode", None, None, None),
        P("tile", None),
        P("tile", None, None),
    )
    return jax.shard_map(
        on_device,
        mesh=mesh,
        in_specs=placed,
        out_specs=(P(None, None, ("tile", "mode"), None), P("mode", None, None, None)),
        check_vma=False,
    )
```

profile of v0, /device:TPU:1, one launch (start us, length us, event | category | flops | bytes accessed | tf_op | source)
XLA Modules:
  0.0 703.6 jit_solution(949461631824141388)
XLA Ops:
  7.2 3.3 collective-permute-start
  11.6 1.8 bitcast_convert_fusion.1
  13.4 1.8 broadcast_multiply_fusion
  15.2 31.9 %collective-permute-done = bf16[3,2,256,512]{3,2,1,0:T(8,128)(2,1)} collective-permute-done((bf16[3,2,256,512]{3,2,1,0:T(8,128)(2,1)}, bf16[3,2,256,512]{3,2,1,0:T(8,128)(2,1)}, u32[]{:S(2)}, u32[]{:S(2)}) %collective-permute-start) | collective-permute-done | bytes 1572896 | tf_op jit(solution)/shard_map/ppermute | solution.py:14
  47.0 2.1 pad_maximum_fusion.1
  49.1 13.9 %while.15 = (s32[]{:T(128)}, bf16[3,2,512,512]{3,2,1,0:T(8,128)(2,1)S(1)}, s32[4,4]{1,0:T(4,128)S(1)}, bf16[4,3,2,256,256]{4,3,0,2,1:T(8,128)(2,1)}, s32[]{:T(128)}) while((s32[]{:T(128)}, bf16[3,2,512,512]{3,2,1,0:T(8,128)(2,1)S(1)}, s32[4,4]{1,0:T(4,128)S(1)}, bf16[4,3,2,256,256]{4,3,0,2,1:T(8,128)(2,1)}, s32[]{:T(128)}) %tuple.77), condition=%wide.while_cond, body=%wide.while_body.sunk | while | flops 2 | bytes 1574013 | solution.py:64
  49.8 2.7 bitcast_dynamic-update-slice_fusion.2
  53.2 2.8 bitcast_dynamic-update-slice_fusion.2
  56.6 2.8 bitcast_dynamic-update-slice_fusion.2
  60.1 2.8 bitcast_dynamic-update-slice_fusion.2
  63.1 2.9 fusion.213
  66.0 2.7 fusion.209
  68.7 1.4 fusion.49
  72.6 1.4 fusion.48
  75.3 1.4 add_convert_fusion.5
  78.0 1.8 fusion.202
  82.3 1.3 fusion.115
  84.8 1.3 fusion.4
  86.1 2.3 fusion.73
  90.9 1.4 fusion.45
  97.4 1.4 add_convert_fusion.4
  103.8 1.7 fusion.110
  106.7 1.3 fusion.10
  108.0 2.3 fusion.81
  115.3 1.3 fusion.130
  117.9 1.4 convolution_subtract_fusion.10
  119.3 2.1 add_convert_fusion.3
  121.5 78.7 %all-reduce.3.cloned.1.call-done = bf16[4,256,256]{2,1,0:T(8,128)(2,1)} async-done(((bf16[4,256,256]{2,1,0:T(8,128)(2,1)}), bf16[4,256,256]{2,1,0:T(8,128)(2,1)}) %all-reduce.3.cloned.1.call-update) | async-done | bytes 524304 | tf_op jit(solution)/shard_map/psum | solution.py:140
  200.2 1.3 multiply_convert_fusion
  206.6 1.3 fusion.105
  209.1 1.3 fusion.16
  210.4 1.8 fusion.85
  213.4 1.7 fusion.167
  217.6 1.3 fusion.125
  220.1 1.3 convolution_subtract_fusion.6
  221.4 1.5 add_convert_fusion.2
  225.4 1.4 fusion.35
  230.7 1.3 fusion.22
  232.0 1.8 fusion.77
  238.8 1.5 fusion.120
  241.5 1.3 convolution_subtract_fusion.2
  242.8 1.5 add_convert_fusion.1
  249.3 1.3 fusion.95
  252.4 1.3 fusion.28
  253.7 2.5 fusion.67
  256.3 3.3 pad_maximum_fusion
  259.6 3.4 broadcast_in_dim.6
  263.0 100.1 %while.14 = (s32[]{:T(128)}, f32[3,2,512,512]{3,2,1,0:T(8,128)}, s32[4]{0:T(128)S(1)}, s32[4]{0:T(128)S(1)}, f32[4,3,2,256,256]{4,3,0,2,1:T(8,128)}, /*index=5*/s32[]{:T(128)}, s32[]{:T(128)}, s32[]{:T(128)}) while((s32[]{:T(128)}, f32[3,2,512,512]{3,2,1,0:T(8,128)}, s32[4]{0:T(128)S(1)}, s32[4]{0:T(128)S(1)}, ...), condition=%wide.region_2.3_spmd, body=%wide.region_1.2_spmd.sunk | while | flops 393224 | bytes 7864521 | solution.py:155
  268.1 2.7 bitcast_add_fusion.2
  270.8 17.2 %dynamic_update_slice.8 = f32[3,2,512,512]{3,2,1,0:T(8,128)} dynamic-update-slice(f32[3,2,512,512]{3,2,1,0:T(8,128)} %get-tuple-element.266, f32[3,2,256,256]{3,2,1,0:T(8,128)S(1)} %bitcast_add_fusion.2, s32[]{:T(128)} %constant.62.clone.1..sunk, s32[]{:T(128)} %constant.62.clone.1..sunk, s32[]{:T(128)S(6)} %select_n.446, s32[]{:T(128)S(6)} %select_n.447) | dynamic-update-slice | bytes 3145732 | tf_op jit(solution)/shard_map/while/body/eval_jaxpr/dynamic_update_slice | solution.py:153
  293.0 2.7 bitcast_add_fusion.2
  295.7 17.1 %dynamic_update_slice.8 = f32[3,2,512,512]{3,2,1,0:T(8,128)} dynamic-update-slice(f32[3,2,512,512]{3,2,1,0:T(8,128)} %get-tuple-element.266, f32[3,2,256,256]{3,2,1,0:T(8,128)S(1)} %bitcast_add_fusion.2, s32[]{:T(128)} %constant.62.clone.1..sunk, s32[]{:T(128)} %constant.62.clone.1..sunk, s32[]{:T(128)S(6)} %select_n.446, s32[]{:T(128)S(6)} %select_n.447) | dynamic-update-slice | bytes 3145732 | tf_op jit(solution)/shard_map/while/body/eval_jaxpr/dynamic_update_slice | solution.py:153
  317.9 2.7 bitcast_add_fusion.2
  320.6 17.4 %dynamic_update_slice.8 = f32[3,2,512,512]{3,2,1,0:T(8,128)} dynamic-update-slice(f32[3,2,512,512]{3,2,1,0:T(8,128)} %get-tuple-element.266, f32[3,2,256,256]{3,2,1,0:T(8,128)S(1)} %bitcast_add_fusion.2, s32[]{:T(128)} %constant.62.clone.1..sunk, s32[]{:T(128)} %constant.62.clone.1..sunk, s32[]{:T(128)S(6)} %select_n.446, s32[]{:T(128)S(6)} %select_n.447) | dynamic-update-slice | bytes 3145732 | tf_op jit(solution)/shard_map/while/body/eval_jaxpr/dynamic_update_slice | solution.py:153
  343.0 2.7 bitcast_add_fusion.2
  345.7 17.5 %dynamic_update_slice.8 = f32[3,2,512,512]{3,2,1,0:T(8,128)} dynamic-update-slice(f32[3,2,512,512]{3,2,1,0:T(8,128)} %get-tuple-element.266, f32[3,2,256,256]{3,2,1,0:T(8,128)S(1)} %bitcast_add_fusion.2, s32[]{:T(128)} %constant.62.clone.1..sunk, s32[]{:T(128)} %constant.62.clone.1..sunk, s32[]{:T(128)S(6)} %select_n.446, s32[]{:T(128)S(6)} %select_n.447) | dynamic-update-slice | bytes 3145732 | tf_op jit(solution)/shard_map/while/body/eval_jaxpr/dynamic_update_slice | solution.py:153
  363.2 2.1 slice.113
  365.3 7.7 %collective-permute-start.1 = (bf16[3,2,256,512]{3,2,1,0:T(8,128)(2,1)S(1)}, bf16[3,2,256,512]{3,2,1,0:T(8,128)(2,1)S(1)}, u32[]{:S(2)}, u32[]{:S(2)}) collective-permute-start(bf16[3,2,256,512]{3,2,1,0:T(8,128)(2,1)S(1)} %slice.113), channel_id=1, source_target_pairs={{248,0},{0,8},{8,16},{16,24},{24,32},{32,40},{40,48},{48,56},{56,6... | collective-permute-start | bytes 4718600 | tf_op jit(solution)/shard_map/ppermute | solution.py:14
  373.8 24.9 %collective-permute-done.1 = bf16[3,2,256,512]{3,2,1,0:T(8,128)(2,1)S(1)} collective-permute-done((bf16[3,2,256,512]{3,2,1,0:T(8,128)(2,1)S(1)}, bf16[3,2,256,512]{3,2,1,0:T(8,128)(2,1)S(1)}, u32[]{:S(2)}, u32[]{:S(2)}) %collective-permute-start.1) | collective-permute-done | bytes 1572896 | tf_op jit(solution)/shard_map/ppermute | solution.py:14
  398.7 3.6 add_convert_fusion
  402.3 252.7 %all-reduce.5.cloned.1.call-done = bf16[1,2,256,256]{3,2,1,0:T(8,128)(2,1)} async-done(((bf16[1,2,256,256]{3,2,1,0:T(8,128)(2,1)}), bf16[1,2,256,256]{3,2,1,0:T(8,128)(2,1)}) %all-reduce.5.cloned.1.call-update) | async-done | bytes 262160 | tf_op jit(solution)/shard_map/psum | solution.py:147
  655.0 1.8 convert_element_type.799
  656.8 38.2 %reduce-scatter.2.cloned.1.call-done = bf16[3,2,32,512]{3,2,1,0:T(8,128)(2,1)} async-done(((bf16[3,2,256,512]{3,2,1,0:T(8,128)(2,1)}), bf16[3,2,32,512]{3,2,1,0:T(8,128)(2,1)}) %reduce-scatter.2.cloned.1.call-update) | async-done | bytes 196624 | tf_op jit(solution)/shard_map/reduce_scatter | solution.py:158
  695.1 1.7 convert_element_type.798
  (114 shorter events, 68.9 us)
Async XLA Ops:
  7.2 193.0 %all-reduce.3.cloned.1.call-start = ((), (), s32[]{:S(2)}) async-start(), calls=%async_computation.1 | async-start | bytes 1048576 | tf_op jit(solution)/shard_map/psum | solution.py:140
  7.2 39.8 %collective-permute-start = (bf16[3,2,256,512]{3,2,1,0:T(8,128)(2,1)}, bf16[3,2,256,512]{3,2,1,0:T(8,128)(2,1)}, u32[]{:S(2)}, u32[]{:S(2)}) collective-permute-start(bf16[3,2,256,512]{3,2,1,0:T(8,128)(2,1)} %param.6), channel_id=1, source_target_pairs={{8,0},{16,8},{24,16},{32,24},{40,32},{48,40},{56,48},{64,56},{72,6... | collective-permute-start | bytes 4718600 | tf_op jit(solution)/shard_map/ppermute | solution.py:14
  63.1 5.6 copy-start.3
  63.1 5.6 copy-start.5
  63.1 5.6 copy-start.8
  72.6 2.7 copy-start.1
  86.1 3.6 copy-start.10
  108.0 3.6 copy-start.13
  117.9 82.3 %copy-start.2 = (f32[4,256,256]{2,1,0:T(8,128)S(1)}, f32[4,256,256]{2,1,0:T(8,128)}, u32[]{:S(2)}) copy-start(f32[4,256,256]{2,1,0:T(8,128)} %param.9) | copy-start | bytes 3145732
  121.4 533.6 %all-reduce.5.cloned.1.call-start = ((), (), s32[]{:S(2)}) async-start(), calls=%async_computation.3 | async-start | bytes 524288 | tf_op jit(solution)/shard_map/psum | solution.py:147
  206.5 3.8 copy-start.9
  206.5 3.8 copy-start.14
  206.5 3.8 copy-start.15
  217.6 3.8 copy-start
  228.1 3.8 copy-start.11
  228.1 3.8 copy-start.12
  252.3 1.4 copy-start.4
  252.3 1.4 copy-start.6
  363.2 9.8 %copy-start.7 = (bf16[256,256]{1,0:T(8,128)(2,1)S(1)}, bf16[256,256]{1,0:T(8,128)(2,1)}, u32[]{:S(2)}) copy-start(bf16[256,256]{1,0:T(8,128)(2,1)} %get-tuple-element.116) | copy-start | bytes 393220
  365.3 33.3 %collective-permute-start.1 = (bf16[3,2,256,512]{3,2,1,0:T(8,128)(2,1)S(1)}, bf16[3,2,256,512]{3,2,1,0:T(8,128)(2,1)S(1)}, u32[]{:S(2)}, u32[]{:S(2)}) collective-permute-start(bf16[3,2,256,512]{3,2,1,0:T(8,128)(2,1)S(1)} %slice.113), channel_id=1, source_target_pairs={{248,0},{0,8},{8,16},{16,24},{24,32},{32,40},{40,48},{48,56},{56,6... | collective-permute-start | bytes 4718600 | tf_op jit(solution)/shard_map/ppermute | solution.py:14
  373.8 321.3 %reduce-scatter.2.cloned.1.call-start = ((), (), s32[]{:S(2)}) async-start(), calls=%async_computation.2 | async-start | bytes 1769472 | tf_op jit(solution)/shard_map/reduce_scatter | solution.py:158
Sparse Core Ops, SparseCore 0:
  121.6 78.5 all-reduce.2
  373.9 281.1 all-reduce.4
  657.6 37.3 reduce-scatter.1
where the time goes:
time: 713 us; the launch traced here: 704 us
  waiting for transfers between devices  426 us (60%)
  matrix products  112 us (16%)
  local copies, waits for them, and re-layouts  94.1 us (13%)
  other arithmetic  29.6 us (4%)
  loops' own time  15.9 us (2%)
  between operations  14.7 us (2%)
  starting transfers between devices  11.1 us (2%)
    psum x1, waiting for transfers between devices, on_device(): lax.psum(jnp.stack(probe_list).astype(jnp.bfloat16), 'tile')  253 us
    dot_general x80, matrix products, product(): return jnp.einsum(form, first, second, preferred_element_type=jnp.float32)  112 us
    psum x1, waiting for transfers between devices, on_device(): lax.psum(intensity.astype(jnp.bfloat16), 'mode').astype(jnp.float32)  78.7 us
    dynamic_update_slice x4, local copies, waits for them, and re-layouts, place(): return lax.dynamic_update_slice(total, current + pieces[index], begin)  69.1 us
    ppermute x2, waiting for transfers between devices, from_behind(): return lax.ppermute(block, axis, route)  56.7 us
    reduce_scatter x1, waiting for transfers between devices, on_device(): lax.psum_scatter(owned.astype(jnp.bfloat16), 'mode', scatter_dimension=2,...  38.2 us
    another operation x1, loops' own time, on_device(): lax.fori_loop(0, count, place, jnp.zeros((depth, 2, 2 * strip, breadth),...  15.6 us
  transfers between devices with their start and end apart: 5, of which 5 were waited for; matrix products, arithmetic and copies ran while one was open for 2% of the time, Pallas kernels for 0%

commit v1 on v0

v1 whole, which is shorter than its diff:
```python
import functools
import math

import jax
import jax.numpy as jnp
import numpy as np
from jax import lax
from jax.experimental import pallas as pl
from jax.experimental.pallas import tpu as pltpu
from jax.sharding import PartitionSpec as P

fresnel = 0.4
SIDE = 256
DEPTH = 3
SLOTS = 4
BF = jnp.bfloat16
F32 = jnp.float32
VMEM = pl.BlockSpec(memory_space=pltpu.VMEM)
SMEM = pl.BlockSpec(memory_space=pltpu.SMEM)
PARAMS = pltpu.CompilerParams(vmem_limit_bytes=48 * 1024 * 1024)


def constants():
    index = np.arange(SIDE)
    folded = index[:, None] * index[None, :] % SIDE
    angle = np.float32(2.0 * math.pi / SIDE) * folded.astype(np.float32)
    scale = np.float32(1.0 / math.sqrt(SIDE))
    real = (np.cos(angle) * scale).astype(jnp.bfloat16)
    imag = (-np.sin(angle) * scale).astype(jnp.bfloat16)
    table = np.block([[real, imag], [-imag, real]])
    freq = ((index + SIDE // 2) % SIDE - SIDE // 2).astype(np.float64)
    phase = -math.pi * fresnel / SIDE * (freq[:, None] ** 2 + freq[None, :] ** 2)
    kernel = np.stack([np.cos(phase), np.sin(phase)]).astype(np.float32)
    return table, kernel


def swap(block, axis, bits):
    route = [(i, i ^ bits) for i in range(lax.axis_size(axis))]
    return lax.ppermute(block, axis, route)


def shift(block, axis, distance):
    size = lax.axis_size(axis)
    return lax.ppermute(block, axis, [(i, (i + distance) % size) for i in range(size)])


def dot(first, second):
    return jnp.dot(first, second, preferred_element_type=F32)


def iotas():
    rows = lax.broadcasted_iota(jnp.int32, (SIDE, SIDE), 0)
    cols = lax.broadcasted_iota(jnp.int32, (SIDE, SIDE), 1)
    return rows, cols


def to_residues(offset):
    rows, cols = iotas()
    return jnp.where(((rows - offset) & (SIDE - 1)) == cols, 1.0, 0.0).astype(BF)


def from_residues(offset):
    rows, cols = iotas()
    return jnp.where(((cols - offset) & (SIDE - 1)) == rows, 1.0, 0.0).astype(BF)


def prepare_kernel(pos_ref, table_ref, table_t_ref, probe0, probe1, probe2, probe3, *outs):
    row_t, row_tt, col_t, col_tt, probe_out = outs
    for axis, plain, turned in ((0, row_t, row_tt), (1, col_t, col_tt)):
        offset = pos_ref[axis]
        there = to_residues(offset)
        back = from_residues(offset)
        for half in range(2):
            part = pl.ds(half * SIDE, SIDE)
            plain[part, :] = dot(there, table_ref[part, :]).astype(BF)
            turned[:, part] = dot(table_t_ref[:, part], back).astype(BF)
    rows = to_residues(pos_ref[0])
    cols = from_residues(pos_ref[1])
    for slot, probe in enumerate((probe0, probe1, probe2, probe3)):
        for part in range(2):
            moved = dot(rows, probe[part]).astype(BF)
            probe_out[slot, part] = dot(moved, cols).astype(BF)


def fill(field, slot, real, imag):
    field[slot, :SIDE, :] = real.astype(BF)
    field[slot, SIDE:, :] = imag.astype(BF)


def transform(field, mid, slot, left, right):
    turned = dot(left[...], field[slot])
    mid[slot, :, :SIDE] = turned[:SIDE].astype(BF)
    mid[slot, :, SIDE:] = turned[SIDE:].astype(BF)
    out = dot(mid[slot], right[...])
    return out[:, :SIDE], out[:, SIDE:]


def propagate(field, mid, slot, forth, back, kernel, sign):
    real, imag = transform(field, mid, slot, *forth)
    kernel_real = kernel[0]
    turned = sign * kernel[1]
    fill(field, slot, real * kernel_real - imag * turned, real * turned + imag * kernel_real)
    return transform(field, mid, slot, *back)


def forward_kernel(
    pos_ref, own, halo, probes, row_t, row_tt, col_t, col_tt, kernel,
    window, wave1, wave2, far, total, total_sent, field, mid,
):
    rows, cols = iotas()
    on_left = cols >= pos_ref[1]
    on_strip = rows >= pos_ref[0]
    for layer in range(DEPTH):
        for part in range(2):
            strip = own[layer, part].astype(F32)
            picked = jnp.where(on_left, strip[:, :SIDE], strip[:, SIDE:])
            below = halo[layer, part].astype(F32)
            window[layer, part] = jnp.where(on_strip, picked, below).astype(BF)
    forth = (row_tt, col_t)
    back = (row_t, col_tt)
    waves = (probes, wave1, wave2)
    for layer in range(DEPTH):
        for slot in range(SLOTS):
            obj_real = window[layer, 0].astype(F32)
            obj_imag = window[layer, 1].astype(F32)
            real = waves[layer][slot, 0].astype(F32)
            imag = waves[layer][slot, 1].astype(F32)
            fill(field, slot, real * obj_real - imag * obj_imag, real * obj_imag + imag * obj_real)
            if layer + 1 < DEPTH:
                real, imag = propagate(field, mid, slot, forth, back, kernel, 1.0)
                waves[layer + 1][slot, 0] = real.astype(BF)
                waves[layer + 1][slot, 1] = imag.astype(BF)
            else:
                real, imag = transform(field, mid, slot, *forth)
                far[slot, 0] = real
                far[slot, 1] = imag
                power = real * real + imag * imag
                total[...] = power if slot == 0 else total[...] + power
    total_sent[...] = total[...].astype(BF)


def backward_kernel(
    pos_ref, which_ref, window, probes, wave1, wave2, far, total, total_got, measured,
    row_t, row_tt, col_t, col_tt, kernel,
    grad_out, keep_out, send_out, field, mid, residual, grads, pieces,
):
    residual[...] = total[...] + total_got[...].astype(F32) - measured[0]
    forth = (row_tt, col_t)
    back = (row_t, col_tt)
    waves = (probes, wave1, wave2)
    rows = from_residues(pos_ref[0])
    cols = to_residues(pos_ref[1])
    backs = [None] * SLOTS
    for slot in range(SLOTS):
        fill(field, slot, residual[...] * far[slot, 0], residual[...] * far[slot, 1])
        backs[slot] = transform(field, mid, slot, *back)
    for layer in reversed(range(DEPTH)):
        for slot in range(SLOTS):
            gin_real, gin_imag = (part.astype(BF).astype(F32) for part in backs[slot])
            real = waves[layer][slot, 0].astype(F32)
            imag = waves[layer][slot, 1].astype(F32)
            grad_real = real * gin_real + imag * gin_imag
            grad_imag = real * gin_imag - imag * gin_real
            if slot > 0:
                grad_real += grads[0]
                grad_imag += grads[1]
            if slot + 1 < SLOTS:
                grads[0] = grad_real
                grads[1] = grad_imag
            else:
                shape = (8, SIDE // 8, SIDE)
                grad_out[:, layer, 0] = grad_real.astype(BF).reshape(shape)
                grad_out[:, layer, 1] = grad_imag.astype(BF).reshape(shape)
            obj_real = window[layer, 0].astype(F32)
            obj_imag = window[layer, 1].astype(F32)
            next_real = obj_real * gin_real + obj_imag * gin_imag
            next_imag = obj_real * gin_imag - obj_imag * gin_real
            if layer > 0:
                fill(field, slot, next_real, next_imag)
                backs[slot] = propagate(field, mid, slot, forth, back, kernel, -1.0)
            else:
                for part, value in enumerate((next_real, next_imag)):
                    moved = dot(rows, value.astype(BF)).astype(BF)
                    pieces[slot, part] = dot(moved, cols).astype(BF)
    half = SIDE // 2
    kept = which_ref[1]
    keep_out[...] = pieces[:, :, pl.ds(kept * half, half), :]
    send_out[...] = pieces[:, :, pl.ds((1 - kept) * half, half), :]


def gather_kernel(which_ref, positions, grads, own_out, spill_out):
    band = SIDE // 8
    top = which_ref[0] * band
    shape = (band, SIDE)
    rows = lax.broadcasted_iota(jnp.int32, shape, 0) + top
    cols = lax.broadcasted_iota(jnp.int32, shape, 1)
    for layer in range(DEPTH):
        for part in range(2):
            sums = [jnp.zeros(shape, F32) for _ in range(4)]
            for place in range(SLOTS):
                value = grads[place, layer, part].astype(F32)
                value += grads[SLOTS + place, layer, part].astype(F32)
                on_strip = rows >= positions[place, 0]
                on_left = cols >= positions[place, 1]
                for index, (here, left) in enumerate(
                    ((True, True), (True, False), (False, True), (False, False))
                ):
                    picked = on_strip if here else ~on_strip
                    picked &= on_left if left else ~on_left
                    sums[index] += jnp.where(picked, value, 0.0)
            own_out[layer, part, :, :SIDE] = sums[0]
            own_out[layer, part, :, SIDE:] = sums[1]
            spill_out[layer, part, :, :SIDE] = sums[2].astype(BF)
            spill_out[layer, part, :, SIDE:] = sums[3].astype(BF)


def quarter_kernel(which_ref, own, got1, got2, got3, *outs):
    total = own[...].astype(F32) + got1[...].astype(F32)
    total += got2[...].astype(F32) + got3[...].astype(F32)
    held = total.astype(BF)
    depth = held.shape[1] // 4
    scratch = outs[-1]
    scratch[...] = held
    for step in range(4):
        outs[step][...] = scratch[:, pl.ds((which_ref[2] ^ step) * depth, depth), :]


def merge_kernel(which_ref, part0, part1, part2, part3, out):
    depth = part0.shape[1]
    for step, part in enumerate((part0, part1, part2, part3)):
        out[:, pl.ds((which_ref[2] ^ step) * depth, depth), :] = part[...]


def finish_kernel(which_ref, own, got, out):
    half = SIDE // 2
    kept = which_ref[1]
    out[0, :, pl.ds(kept * half, half), :] = own[...].astype(F32)
    out[0, :, pl.ds((1 - kept) * half, half), :] = got[...].astype(F32)


def call(kernel, outs, arguments, scalars, scratch=()):
    return pl.pallas_call(
        kernel,
        out_shape=[jax.ShapeDtypeStruct(shape, dtype) for shape, dtype in outs],
        in_specs=[SMEM] * scalars + [VMEM] * (len(arguments) - scalars),
        out_specs=[VMEM] * len(outs),
        scratch_shapes=[pltpu.VMEM(shape, dtype) for shape, dtype in scratch],
        compiler_params=PARAMS,
    )(*arguments)


def on_device(object_slices, probe_modes, positions, measured):
    tile = lax.axis_index("tile")
    mode = lax.axis_index("mode")
    place = mode & (SLOTS - 1)
    half = SIDE // 2
    square = (SIDE, SIDE)
    table, kernel = constants()
    table_t = jnp.asarray(table.T)
    table = jnp.asarray(table)
    kernel = jnp.asarray(kernel)
    which = jnp.stack([mode, tile & 1, tile >> 3, place]).astype(jnp.int32)

    pos = lax.dynamic_index_in_dim(positions, place, 0, keepdims=False)
    above = shift(pos, "tile", 1)
    columns = lax.broadcasted_iota(jnp.int32, square, 1)
    chosen = jnp.where(columns >= above[1], object_slices[..., :SIDE], object_slices[..., SIDE:])
    halo = shift(chosen, "tile", -1)
    probes = [probe_modes[0]] + [swap(probe_modes[0], "mode", step) for step in range(1, 4)]

    wide = (2 * SIDE, 2 * SIDE)
    tables = call(
        prepare_kernel,
        [(wide, BF)] * 4 + [((SLOTS, 2) + square, BF)],
        (pos, table, table_t, *probes),
        1,
    )
    tables, rolled = tables[:4], tables[4]
    scratch = [((SLOTS, 2 * SIDE, SIDE), BF), ((SLOTS, SIDE, 2 * SIDE), BF)]
    window, wave1, wave2, far, total, total_sent = call(
        forward_kernel,
        [
            ((DEPTH, 2) + square, BF),
            ((SLOTS, 2) + square, BF),
            ((SLOTS, 2) + square, BF),
            ((SLOTS, 2) + square, F32),
            (square, F32),
            (square, BF),
        ],
        (pos, object_slices, halo, rolled, *tables, kernel),
        1,
        scratch,
    )
    total_got = swap(total_sent, "mode", 4)
    picked = lax.dynamic_index_in_dim(measured, place, 0, keepdims=True)
    grads, keep, send = call(
        backward_kernel,
        [
            ((8, DEPTH, 2, SIDE // 8, SIDE), BF),
            ((SLOTS, 2, half, SIDE), BF),
            ((SLOTS, 2, half, SIDE), BF),
        ],
        (pos, which, window, rolled, wave1, wave2, far, total, total_got, picked, *tables, kernel),
        2,
        scratch + [(square, F32), ((2,) + square, F32), ((SLOTS, 2) + square, BF)],
    )

    got = swap(send, "tile", 1)
    summed = (keep.astype(F32) + got.astype(F32)).astype(BF)
    parts = [summed[0]] + [swap(summed[step], "mode", step) for step in range(1, 4)]
    quarter = (2, half // 4, SIDE)
    quarters = call(
        quarter_kernel, [(quarter, BF)] * 4, (which, *parts), 1, [((2, half, SIDE), BF)]
    )
    parts = [quarters[0]] + [swap(quarters[step], "tile", step << 3) for step in range(1, 4)]
    part = ((parts[0].astype(F32) + parts[1]) + (parts[2].astype(F32) + parts[3])).astype(BF)
    parts = [part] + [swap(part, "tile", step << 1) for step in range(1, 4)]
    part = ((parts[0].astype(F32) + parts[1]) + (parts[2].astype(F32) + parts[3])).astype(BF)
    parts = [part] + [swap(part, "tile", step << 3) for step in range(1, 4)]
    (merged,) = call(merge_kernel, [((2, half, SIDE), BF)], (which, *parts), 1)
    (probe_grad,) = call(
        finish_kernel, [((1, 2) + square, F32)], (which, merged, swap(merged, "tile", 1)), 1
    )

    bands = lax.all_to_all(grads, "mode", 0, 0, tiled=True)
    shape = (DEPTH, 2, SIDE // 8, 2 * SIDE)
    own, spill = call(gather_kernel, [(shape, F32), (shape, BF)], (which, positions, bands), 2)
    object_grad = own + shift(spill, "tile", 1).astype(F32)
    return (object_grad, probe_grad)


def solution(mesh):
    placed = (
        P(None, None, "tile", None),
        P("mode", None, None, None),
        P("tile", None),
        P("tile", None, None),
    )
    return jax.shard_map(
        on_device,
        mesh=mesh,
        in_specs=placed,
        out_specs=(P(None, None, ("tile", "mode"), None), P("mode", None, None, None)),
        check_vma=False,
    )
```

time: 713 us -> 125 us (0.18); the launches traced: 704 us -> 125 us
  waiting for transfers between devices: 426 us -> 38.6 us
  matrix products: 112 us -> 0 us
  local copies, waits for them, and re-layouts: 94.1 us -> 3.84 us
  starting transfers between devices: 11.1 us -> 45.8 us
  Pallas kernels: 0 us -> 32 us
  other arithmetic: 29.6 us -> 4.06 us
  loops' own time: 15.9 us -> 0 us
  between operations: 14.7 us -> 0.8 us
    psum x2 -> x0, waiting for transfers between devices: 331 us -> none  [the longest x1 253 us: on_device(): lax.psum(jnp.stack(probe_list).astype(jnp.bfloat16), 'tile')]
    dot_general x80 -> x0, matrix products: 112 us -> none  [product(): return jnp.einsum(form, first, second, preferred_element_type=jnp.float32)]
    dynamic_update_slice x4 -> x0, local copies, waits for them, and re-layouts: 69.1 us -> none  [place(): return lax.dynamic_update_slice(total, current + pieces[index], begin)]
    reduce_scatter x1 -> x0, waiting for transfers between devices: 38.2 us -> none  [on_device(): lax.psum_scatter(owned.astype(jnp.bfloat16), 'mode', scatter_dimension=2,...]
    pallas_call x0 -> x7, Pallas kernels: none -> 32 us  [call(): pl.pallas_call(kernel, out_shape=[jax.ShapeDtypeStruct(shape, dtype) for...]
    ppermute x2 -> x21, starting transfers between devices: 11 us -> 42.2 us  [the longest x18 28.2 us: swap(): return lax.ppermute(block, axis, route)]
    ppermute x2 -> x21, waiting for transfers between devices: 56.7 us -> 38.6 us  [the longest x18 37.9 us: swap(): return lax.ppermute(block, axis, route)]
    another operation x2 -> x0, loops' own time: 15.9 us -> none  [the longest x1 15.6 us: on_device(): lax.fori_loop(0, count, place, jnp.zeros((depth, 2, 2 * strip, breadth),...]
  transfers between devices with their start and end apart: 5 -> 22, of which waited for: 5 -> 12; matrix products, arithmetic and copies ran while one was open for 2% -> 0% of each run, Pallas kernels for 0% -> 5%
where the time goes in v1:
time: 125 us
  starting transfers between devices  45.8 us (37%)
  waiting for transfers between devices  38.6 us (31%)
  Pallas kernels  32 us (26%)
  other arithmetic  4.06 us (3%)
  local copies, waits for them, and re-layouts  3.84 us (3%)
    ppermute x18, waiting for transfers between devices, swap(): return lax.ppermute(block, axis, route)  37.9 us
    pallas_call x7, Pallas kernels, call(): pl.pallas_call(kernel, out_shape=[jax.ShapeDtypeStruct(shape, dtype) for...  32 us
    ppermute x18, starting transfers between devices, swap(): return lax.ppermute(block, axis, route)  28.2 us
    ppermute x3, starting transfers between devices, shift(): lax.ppermute(block, axis, [(i, (i + distance) % size) for i in range(size)])  14 us
    all_to_all x1, starting transfers between devices, on_device(): bands = lax.all_to_all(grads, 'mode', 0, 0, tiled=True)  3.55 us
  transfers between devices with their start and end apart: 22, of which 12 were waited for; matrix products, arithmetic and copies ran while one was open for 0% of the time, Pallas kernels for 5%

profile of v1, /device:TPU:1, one launch (start us, length us, event | category | flops | bytes accessed | tf_op | source)
XLA Modules:
  0.0 125.2 jit_solution(4925783213247673590)
XLA Ops:
  0.6 0.0 copy-start
  0.6 0.0 copy-start.4
  0.7 0.0 copy-start.5
  0.7 1.0 dynamic-slice_reduce_fusion.pos_ref
  1.7 4.5 %collective-permute-start = (s32[2]{0:T(128)S(1)}, s32[2]{0:T(128)S(1)}, u32[]{:S(2)}, u32[]{:S(2)}) collective-permute-start(s32[2]{0:T(128)S(1)} %dynamic-slice_reduce_fusion.pos_ref), channel_id=1, source_target_pairs={{0,8},{8,16},{16,24},{24,32},{32,40},{40,48},{48,56},{56,64},{64,7... | collective-permute-start | bytes 32 | tf_op jit(solution)/shard_map/ppermute | solution.py:44
  6.1 0.7 collective-permute-done
  6.9 0.6 slice.21
  7.5 0.6 iota_compare_fusion
  8.2 2.4 %slice_select_fusion = bf16[3,2,256,256]{3,2,1,0:T(8,128)(2,1)} fusion(bf16[3,2,256,512]{3,2,1,0:T(8,128)(2,1)} %own.1, pred[256]{0:T(512)(128)(4,1)S(1)} %iota_compare_fusion), kind=kLoop, calls=%fused_computation.1 | loop fusion | flops 393216 | bytes 2359552 | tf_op jit(solution)/shard_map/jit(_where)/select_n | solution.py:267
  10.5 5.6 %collective-permute-start.1 = (bf16[3,2,256,256]{3,2,1,0:T(8,128)(2,1)}, bf16[3,2,256,256]{3,2,1,0:T(8,128)(2,1)S(1)}, u32[]{:S(2)}, u32[]{:S(2)}) collective-permute-start(bf16[3,2,256,256]{3,2,1,0:T(8,128)(2,1)} %slice_select_fusion), channel_id=1, source_target_pairs={{0,248},{8,0},{16,8},{24,16},{32,24},{40,32},{48,40},{56,48},{64,5... | collective-permute-start | bytes 2359304 | tf_op jit(solution)/shard_map/ppermute | solution.py:44
  16.1 1.3 %collective-permute-start.2 = (bf16[2,256,256]{2,1,0:T(8,128)(2,1)}, bf16[2,256,256]{2,1,0:T(8,128)(2,1)}, u32[]{:S(2)}, u32[]{:S(2)}) collective-permute-start(bf16[2,256,256]{2,1,0:T(8,128)(2,1)} %bitcast.5.probe0), channel_id=1, source_target_pairs={{0,1},{1,0},{2,3},{3,2},{4,5},{5,4},{6,7},{7,6},{8,9},{9,8},{10,11... | collective-permute-start | bytes 786440 | tf_op jit(solution)/shard_map/ppermute | solution.py:39
  17.4 2.6 %collective-permute-start.3 = (bf16[2,256,256]{2,1,0:T(8,128)(2,1)}, bf16[2,256,256]{2,1,0:T(8,128)(2,1)}, u32[]{:S(2)}, u32[]{:S(2)}) collective-permute-start(bf16[2,256,256]{2,1,0:T(8,128)(2,1)} %bitcast.5.probe0), channel_id=1, source_target_pairs={{0,2},{1,3},{2,0},{3,1},{4,6},{5,7},{6,4},{7,5},{8,10},{9,11},{10,... | collective-permute-start | bytes 786440 | tf_op jit(solution)/shard_map/ppermute | solution.py:39
  20.0 0.0 collective-permute-start.4
  20.0 4.3 %collective-permute-done.2.probe1 = bf16[2,256,256]{2,1,0:T(8,128)(2,1)} collective-permute-done((bf16[2,256,256]{2,1,0:T(8,128)(2,1)}, bf16[2,256,256]{2,1,0:T(8,128)(2,1)}, u32[]{:S(2)}, u32[]{:S(2)}) %collective-permute-start.2) | collective-permute-done | bytes 262176 | tf_op jit(solution)/shard_map/ppermute | solution.py:39
  24.3 8.1 %collective-permute-done.3.probe2 = bf16[2,256,256]{2,1,0:T(8,128)(2,1)} collective-permute-done((bf16[2,256,256]{2,1,0:T(8,128)(2,1)}, bf16[2,256,256]{2,1,0:T(8,128)(2,1)}, u32[]{:S(2)}, u32[]{:S(2)}) %collective-permute-start.3) | collective-permute-done | bytes 262176 | tf_op jit(solution)/shard_map/ppermute | solution.py:39
  32.4 2.0 %collective-permute-done.4.probe3 = bf16[2,256,256]{2,1,0:T(8,128)(2,1)} collective-permute-done((bf16[2,256,256]{2,1,0:T(8,128)(2,1)}, bf16[2,256,256]{2,1,0:T(8,128)(2,1)}, u32[]{:S(2)}, u32[]{:S(2)}) %collective-permute-start.4) | collective-permute-done | bytes 262176 | tf_op jit(solution)/shard_map/ppermute | solution.py:39
  34.4 2.6 %shard_map.86 = (bf16[512,512]{1,0:T(8,128)(2,1)S(1)}, bf16[512,512]{1,0:T(8,128)(2,1)S(1)}, bf16[512,512]{1,0:T(8,128)(2,1)S(1)}, bf16[512,512]{1,0:T(8,128)(2,1)S(1)}, bf16[4,2,256,256]{3,2,1,0:T(8,128)(2,1)S(1)}) custom-call(s32[2]{0:T(128)S(1)} %dynamic-slice_reduce_fusion.pos_ref, bf16[512,512]{1,0:T(8,128)(2,1)S(1)} %copy-done.5, ...), custom_call_target="tpu_custom_call" | custom-call | tf_op jit(solution)/shard_map/pallas_call | solution.py:242
  37.0 1.0 copy-done.1
  37.9 0.0 collective-permute-done.1.halo
  37.9 12.4 %shard_map.87 = (bf16[3,2,256,256]{3,2,1,0:T(8,128)(2,1)S(1)}, bf16[4,2,256,256]{3,2,1,0:T(8,128)(2,1)S(1)}, bf16[4,2,256,256]{3,2,1,0:T(8,128)(2,1)}, f32[4,2,2...) custom-call(s32[2]{0:T(128)S(1)} %dynamic-slice_reduce_fusion.pos_ref, ...), custom_call_target="tpu_custom_call" | custom-call | tf_op jit(solution)/shard_map/pallas_call | solution.py:242
  50.4 1.0 copy-done.3
  51.4 0.7 collective-permute-start.5
  52.1 0.1 pad_add_fusion.which_ref
  52.2 3.0 %collective-permute-done.5.total_got = bf16[256,256]{1,0:T(8,128)(2,1)S(1)} collective-permute-done((bf16[256,256]{1,0:T(8,128)(2,1)S(1)}, bf16[256,256]{1,0:T(8,128)(2,1)S(1)}, u32[]{:S(2)}, u32[]{:S(2)}) %collective-permute-start.5) | collective-permute-done | bytes 131104 | tf_op jit(solution)/shard_map/ppermute | solution.py:39
  55.2 13.5 %shard_map.88 = (bf16[8,3,2,32,256]{4,3,2,1,0:T(8,128)(2,1)}, bf16[4,2,128,256]{3,2,1,0:T(8,128)(2,1)S(1)}, bf16[4,2,128,256]{3,2,1,0:T(8,128)(2,1)S(1)}) custom-call(s32[2]{0:T(128)S(1)} %dynamic-slice_reduce_fusion.pos_ref, s32[4]{0:T(128)S(1)} %pad_add_fusion.which_ref, bf16[3,2,256,256]{3,2,1,0:T(8,128)(2,1)S(1)} %get-tuple-element.27.window, ...), custom_call_target="tpu_custom_call" | custom-call | tf_op jit(solution)/shard_map/pallas_call | solution.py:242
  68.7 2.6 %collective-permute-start.7 = (bf16[4,2,128,256]{3,2,1,0:T(8,128)(2,1)S(1)}, bf16[4,2,128,256]{3,2,1,0:T(8,128)(2,1)S(1)}, u32[]{:S(2)}, u32[]{:S(2)}) collective-permute-start(bf16[4,2,128,256]{3,2,1,0:T(8,128)(2,1)S(1)} %get-tuple-element.37), channel_id=1, source_target_pairs={{0,8},{8,0},{16,24},{24,16},{32,40},{40,32},{48,56},{56,48},{64,72... | collective-permute-start | bytes 1572872 | tf_op jit(solution)/shard_map/ppermute | solution.py:39
  71.4 3.5 %all-to-all-start = ((bf16[8,3,2,32,256]{4,3,2,1,0:T(8,128)(2,1)}), bf16[8,3,2,32,256]{4,3,2,1,0:T(8,128)(2,1)S(1)}, u32[]{:S(2)}, u32[]{:S(2)}) async-start(bf16[8,3,2,32,256]{4,3,2,1,0:T(8,128)(2,1)} %get-tuple-element.33), calls=%async_computation | async-start | bytes 1572864 | tf_op jit(solution)/shard_map/all_to_all | solution.py:325
  74.9 0.0 collective-permute-done.7
  74.9 0.0 copy-start.6
  74.9 0.1 add_convert_fusion
  75.1 2.7 %collective-permute-start.10 = (bf16[2,128,256]{2,1,0:T(8,128)(2,1)S(1)}, bf16[2,128,256]{2,1,0:T(8,128)(2,1)S(1)}, u32[]{:S(2)}, u32[]{:S(2)}) collective-permute-start(bf16[2,128,256]{2,1,0:T(8,128)(2,1)S(1)} %get-tuple-element.42), channel_id=1, source_target_pairs={{0,3},{1,2},{2,1},{3,0},{4,7},{5,6},{6,5},{7,4},{8,11},{9,10},{10,... | collective-permute-start | bytes 393224 | tf_op jit(solution)/shard_map/ppermute | solution.py:39
  77.8 0.0 collective-permute-start.8
  77.8 1.3 %collective-permute-start.9 = (bf16[2,128,256]{2,1,0:T(8,128)(2,1)S(1)}, bf16[2,128,256]{2,1,0:T(8,128)(2,1)S(1)}, u32[]{:S(2)}, u32[]{:S(2)}) collective-permute-start(bf16[2,128,256]{2,1,0:T(8,128)(2,1)S(1)} %get-tuple-element.43), channel_id=1, source_target_pairs={{0,2},{1,3},{2,0},{3,1},{4,6},{5,7},{6,4},{7,5},{8,10},{9,11},{10,... | collective-permute-start | bytes 393224 | tf_op jit(solution)/shard_map/ppermute | solution.py:39
  79.1 10.8 %collective-permute-done.10.got3 = bf16[2,128,256]{2,1,0:T(8,128)(2,1)S(1)} collective-permute-done((bf16[2,128,256]{2,1,0:T(8,128)(2,1)S(1)}, bf16[2,128,256]{2,1,0:T(8,128)(2,1)S(1)}, u32[]{:S(2)}, u32[]{:S(2)}) %collective-permute-start.10) | collective-permute-done | bytes 131104 | tf_op jit(solution)/shard_map/ppermute | solution.py:39
  89.9 3.1 %collective-permute-done.9.got2 = bf16[2,128,256]{2,1,0:T(8,128)(2,1)S(1)} collective-permute-done((bf16[2,128,256]{2,1,0:T(8,128)(2,1)S(1)}, bf16[2,128,256]{2,1,0:T(8,128)(2,1)S(1)}, u32[]{:S(2)}, u32[]{:S(2)}) %collective-permute-start.9) | collective-permute-done | bytes 131104 | tf_op jit(solution)/shard_map/ppermute | solution.py:39
  92.9 0.6 shard_map.90
  93.6 0.1 collective-permute-start.11
  93.7 1.7 %collective-permute-start.12 = (bf16[2,32,256]{2,1,0:T(8,128)(2,1)S(1)}, bf16[2,32,256]{2,1,0:T(8,128)(2,1)S(1)}, u32[]{:S(2)}, u32[]{:S(2)}) collective-permute-start(bf16[2,32,256]{2,1,0:T(8,128)(2,1)S(1)} %get-tuple-element.40), channel_id=1, source_target_pairs={{0,128},{8,136},{16,144},{24,152},{32,160},{40,168},{48,176},{56,1... | collective-permute-start | bytes 98312 | tf_op jit(solution)/shard_map/ppermute | solution.py:39
  95.4 2.1 %collective-permute-start.13 = (bf16[2,32,256]{2,1,0:T(8,128)(2,1)S(1)}, bf16[2,32,256]{2,1,0:T(8,128)(2,1)S(1)}, u32[]{:S(2)}, u32[]{:S(2)}) collective-permute-start(bf16[2,32,256]{2,1,0:T(8,128)(2,1)S(1)} %get-tuple-element.41), channel_id=1, source_target_pairs={{0,192},{8,200},{16,208},{24,216},{32,224},{40,232},{48,240},{56,2... | collective-permute-start | bytes 98312 | tf_op jit(solution)/shard_map/ppermute | solution.py:39
  97.5 0.0 collective-permute-done.11
  97.5 0.8 collective-permute-done.12
  98.3 1.5 %collective-permute-done.13 = bf16[2,32,256]{2,1,0:T(8,128)(2,1)S(1)} collective-permute-done((bf16[2,32,256]{2,1,0:T(8,128)(2,1)S(1)}, bf16[2,32,256]{2,1,0:T(8,128)(2,1)S(1)}, u32[]{:S(2)}, u32[]{:S(2)}) %collective-permute-start.13) | collective-permute-done | bytes 32800 | tf_op jit(solution)/shard_map/ppermute | solution.py:39
  99.9 0.7 collective-permute-start.14
  100.5 3.8 %collective-permute-start.15 = (bf16[2,32,256]{2,1,0:T(8,128)(2,1)S(1)}, bf16[2,32,256]{2,1,0:T(8,128)(2,1)S(1)}, u32[]{:S(2)}, u32[]{:S(2)}) collective-permute-start(bf16[2,32,256]{2,1,0:T(8,128)(2,1)S(1)} %add_convert_fusion.2), channel_id=1, source_target_pairs={{0,32},{8,40},{16,48},{24,56},{32,0},{40,8},{48,16},{56,24},{64,96... | collective-permute-start | bytes 98312 | tf_op jit(solution)/shard_map/ppermute | solution.py:39
  104.4 1.3 %collective-permute-start.16 = (bf16[2,32,256]{2,1,0:T(8,128)(2,1)S(1)}, bf16[2,32,256]{2,1,0:T(8,128)(2,1)S(1)}, u32[]{:S(2)}, u32[]{:S(2)}) collective-permute-start(bf16[2,32,256]{2,1,0:T(8,128)(2,1)S(1)} %add_convert_fusion.2), channel_id=1, source_target_pairs={{0,48},{8,56},{16,32},{24,40},{32,16},{40,24},{48,0},{56,8},{64,11... | collective-permute-start | bytes 98312 | tf_op jit(solution)/shard_map/ppermute | solution.py:39
  105.6 0.1 copy.9.positions
  105.7 0.0 all-to-all-done.grads
  105.7 1.0 shard_map.89
  106.7 4.0 %collective-permute-start.6 = (bf16[3,2,32,512]{3,2,1,0:T(8,128)(2,1)S(1)}, bf16[3,2,32,512]{3,2,1,0:T(8,128)(2,1)S(1)}, u32[]{:S(2)}, u32[]{:S(2)}) collective-permute-start(bf16[3,2,32,512]{3,2,1,0:T(8,128)(2,1)S(1)} %get-tuple-element.35), channel_id=1, source_target_pairs={{0,8},{8,16},{16,24},{24,32},{32,40},{40,48},{48,56},{56,64},{64,7... | collective-permute-start | bytes 589832 | tf_op jit(solution)/shard_map/ppermute | solution.py:44
  110.7 0.0 collective-permute-done.14
  110.7 0.0 collective-permute-done.15
  110.7 0.0 collective-permute-done.16
  110.8 0.1 collective-permute-start.17
  110.9 1.9 %collective-permute-start.18 = (bf16[2,32,256]{2,1,0:T(8,128)(2,1)S(1)}, bf16[2,32,256]{2,1,0:T(8,128)(2,1)S(1)}, u32[]{:S(2)}, u32[]{:S(2)}) collective-permute-start(bf16[2,32,256]{2,1,0:T(8,128)(2,1)S(1)} %add_convert_fusion.1.part0), channel_id=1, source_target_pairs={{0,128},{8,136},{16,144},{24,152},{32,160},{40,168},{48,176},{56,1... | collective-permute-start | bytes 98312 | tf_op jit(solution)/shard_map/ppermute | solution.py:39
  112.8 1.9 %collective-permute-start.19 = (bf16[2,32,256]{2,1,0:T(8,128)(2,1)S(1)}, bf16[2,32,256]{2,1,0:T(8,128)(2,1)S(1)}, u32[]{:S(2)}, u32[]{:S(2)}) collective-permute-start(bf16[2,32,256]{2,1,0:T(8,128)(2,1)S(1)} %add_convert_fusion.1.part0), channel_id=1, source_target_pairs={{0,192},{8,200},{16,208},{24,216},{32,224},{40,232},{48,240},{56,2... | collective-permute-start | bytes 98312 | tf_op jit(solution)/shard_map/ppermute | solution.py:39
  114.7 0.0 collective-permute-done.17.part1
  114.7 0.7 collective-permute-done.18.part2
  115.4 2.7 %collective-permute-done.19.part3 = bf16[2,32,256]{2,1,0:T(8,128)(2,1)S(1)} collective-permute-done((bf16[2,32,256]{2,1,0:T(8,128)(2,1)S(1)}, bf16[2,32,256]{2,1,0:T(8,128)(2,1)S(1)}, u32[]{:S(2)}, u32[]{:S(2)}) %collective-permute-start.19) | collective-permute-done | bytes 32800 | tf_op jit(solution)/shard_map/ppermute | solution.py:39
  118.1 0.6 shard_map.91.own
  118.7 3.3 %collective-permute-start.20 = (bf16[2,128,256]{2,1,0:T(8,128)(2,1)S(1)}, bf16[2,128,256]{2,1,0:T(8,128)(2,1)S(1)}, u32[]{:S(2)}, u32[]{:S(2)}) collective-permute-start(bf16[2,128,256]{2,1,0:T(8,128)(2,1)S(1)} %shard_map.91.own), channel_id=1, source_target_pairs={{0,8},{8,0},{16,24},{24,16},{32,40},{40,32},{48,56},{56,48},{64,72... | collective-permute-start | bytes 393224 | tf_op jit(solution)/shard_map/ppermute | solution.py:39
  122.0 1.0 collective-permute-done.20.got
  123.0 1.4 %shard_map.92 = f32[1,2,256,256]{3,2,1,0:T(8,128)} custom-call(s32[4]{0:T(128)S(1)} %pad_add_fusion.which_ref, bf16[2,128,256]{2,1,0:T(8,128)(2,1)S(1)} %shard_map.91.own, bf16[2,128,256]{2,1,0:T(8,128)(2,1)S(1)} %collective-permute-done.20.got), custom_call_target="tpu_custom_call" | custom-call | tf_op jit(solution)/shard_map/pallas_call | solution.py:242
  124.4 0.0 collective-permute-done.6
  124.4 0.8 convert_add_fusion
  (13 shorter events, 0.1 us)
Async XLA Ops:
  0.6 51.6 %copy-start = (f32[4,256,256]{2,1,0:T(8,128)S(1)}, f32[4,256,256]{2,1,0:T(8,128)}, u32[]{:S(2)}) copy-start(f32[4,256,256]{2,1,0:T(8,128)} %param.10) | copy-start | bytes 3145732
  0.6 33.7 %copy-start.4 = (bf16[512,512]{1,0:T(8,128)(2,1)S(1)}, bf16[512,512]{1,0:T(8,128)(2,1)}, u32[]{:S(2)}) copy-start(bf16[512,512]{1,0:T(8,128)(2,1)} %constant.29.clone.table_t_ref) | copy-start | bytes 1572868
  0.7 33.7 %copy-start.5 = (bf16[512,512]{1,0:T(8,128)(2,1)S(1)}, bf16[512,512]{1,0:T(8,128)(2,1)}, u32[]{:S(2)}) copy-start(bf16[512,512]{1,0:T(8,128)(2,1)} %constant.30.clone.table_ref) | copy-start | bytes 1572868
  1.7 5.2 %collective-permute-start = (s32[2]{0:T(128)S(1)}, s32[2]{0:T(128)S(1)}, u32[]{:S(2)}, u32[]{:S(2)}) collective-permute-start(s32[2]{0:T(128)S(1)} %dynamic-slice_reduce_fusion.pos_ref), channel_id=1, source_target_pairs={{0,8},{8,16},{16,24},{24,32},{32,40},{40,48},{48,56},{56,64},{64,7... | collective-permute-start | bytes 32 | tf_op jit(solution)/shard_map/ppermute | solution.py:44
  10.5 27.4 %copy-start.2 = (f32[2,256,256]{2,1,0:T(8,128)S(1)}, f32[2,256,256]{2,1,0:T(8,128)}, u32[]{:S(2)}) copy-start(f32[2,256,256]{2,1,0:T(8,128)} %constant.31.clone.kernel) | copy-start | bytes 1572868
  10.5 27.4 %collective-permute-start.1 = (bf16[3,2,256,256]{3,2,1,0:T(8,128)(2,1)}, bf16[3,2,256,256]{3,2,1,0:T(8,128)(2,1)S(1)}, u32[]{:S(2)}, u32[]{:S(2)}) collective-permute-start(bf16[3,2,256,256]{3,2,1,0:T(8,128)(2,1)} %slice_select_fusion), channel_id=1, source_target_pairs={{0,248},{8,0},{16,8},{24,16},{32,24},{40,32},{48,40},{56,48},{64,5... | collective-permute-start | bytes 2359304 | tf_op jit(solution)/shard_map/ppermute | solution.py:44
  16.1 8.2 %collective-permute-start.2 = (bf16[2,256,256]{2,1,0:T(8,128)(2,1)}, bf16[2,256,256]{2,1,0:T(8,128)(2,1)}, u32[]{:S(2)}, u32[]{:S(2)}) collective-permute-start(bf16[2,256,256]{2,1,0:T(8,128)(2,1)} %bitcast.5.probe0), channel_id=1, source_target_pairs={{0,1},{1,0},{2,3},{3,2},{4,5},{5,4},{6,7},{7,6},{8,9},{9,8},{10,11... | collective-permute-start | bytes 786440 | tf_op jit(solution)/shard_map/ppermute | solution.py:39
  17.4 15.0 %collective-permute-start.3 = (bf16[2,256,256]{2,1,0:T(8,128)(2,1)}, bf16[2,256,256]{2,1,0:T(8,128)(2,1)}, u32[]{:S(2)}, u32[]{:S(2)}) collective-permute-start(bf16[2,256,256]{2,1,0:T(8,128)(2,1)} %bitcast.5.probe0), channel_id=1, source_target_pairs={{0,2},{1,3},{2,0},{3,1},{4,6},{5,7},{6,4},{7,5},{8,10},{9,11},{10,... | collective-permute-start | bytes 786440 | tf_op jit(solution)/shard_map/ppermute | solution.py:39
  20.0 14.4 %collective-permute-start.4 = (bf16[2,256,256]{2,1,0:T(8,128)(2,1)}, bf16[2,256,256]{2,1,0:T(8,128)(2,1)}, u32[]{:S(2)}, u32[]{:S(2)}) collective-permute-start(bf16[2,256,256]{2,1,0:T(8,128)(2,1)} %bitcast.5.probe0), channel_id=1, source_target_pairs={{0,3},{1,2},{2,1},{3,0},{4,7},{5,6},{6,5},{7,4},{8,11},{9,10},{10,... | collective-permute-start | bytes 786440 | tf_op jit(solution)/shard_map/ppermute | solution.py:39
  36.9 1.0 copy-start.1
  50.4 1.0 copy-start.3
  51.4 3.8 %collective-permute-start.5 = (bf16[256,256]{1,0:T(8,128)(2,1)S(1)}, bf16[256,256]{1,0:T(8,128)(2,1)S(1)}, u32[]{:S(2)}, u32[]{:S(2)}) collective-permute-start(bf16[256,256]{1,0:T(8,128)(2,1)S(1)} %get-tuple-element.32), channel_id=1, source_target_pairs={{0,4},{1,5},{2,6},{3,7},{4,0},{5,1},{6,2},{7,3},{8,12},{9,13},{10,... | collective-permute-start | bytes 393224 | tf_op jit(solution)/shard_map/ppermute | solution.py:39
  68.7 6.2 %collective-permute-start.7 = (bf16[4,2,128,256]{3,2,1,0:T(8,128)(2,1)S(1)}, bf16[4,2,128,256]{3,2,1,0:T(8,128)(2,1)S(1)}, u32[]{:S(2)}, u32[]{:S(2)}) collective-permute-start(bf16[4,2,128,256]{3,2,1,0:T(8,128)(2,1)S(1)} %get-tuple-element.37), channel_id=1, source_target_pairs={{0,8},{8,0},{16,24},{24,16},{32,40},{40,32},{48,56},{56,48},{64,72... | collective-permute-start | bytes 1572872 | tf_op jit(solution)/shard_map/ppermute | solution.py:39
  71.4 34.3 %all-to-all-start = ((bf16[8,3,2,32,256]{4,3,2,1,0:T(8,128)(2,1)}), bf16[8,3,2,32,256]{4,3,2,1,0:T(8,128)(2,1)S(1)}, u32[]{:S(2)}, u32[]{:S(2)}) async-start(bf16[8,3,2,32,256]{4,3,2,1,0:T(8,128)(2,1)} %get-tuple-element.33), calls=%async_computation | async-start | bytes 1572864 | tf_op jit(solution)/shard_map/all_to_all | solution.py:325
  74.9 30.7 %copy-start.6 = (s32[4,2]{0,1:T(2,128)S(1)}, s32[4,2]{0,1:T(2,128)}, u32[]{:S(2)}) copy-start(s32[4,2]{0,1:T(2,128)} %param.9) | copy-start | bytes 100
  75.1 14.7 %collective-permute-start.10 = (bf16[2,128,256]{2,1,0:T(8,128)(2,1)S(1)}, bf16[2,128,256]{2,1,0:T(8,128)(2,1)S(1)}, u32[]{:S(2)}, u32[]{:S(2)}) collective-permute-start(bf16[2,128,256]{2,1,0:T(8,128)(2,1)S(1)} %get-tuple-element.42), channel_id=1, source_target_pairs={{0,3},{1,2},{2,1},{3,0},{4,7},{5,6},{6,5},{7,4},{8,11},{9,10},{10,... | collective-permute-start | bytes 393224 | tf_op jit(solution)/shard_map/ppermute | solution.py:39
  77.8 12.1 %collective-permute-start.8 = (bf16[2,128,256]{2,1,0:T(8,128)(2,1)S(1)}, bf16[2,128,256]{2,1,0:T(8,128)(2,1)S(1)}, u32[]{:S(2)}, u32[]{:S(2)}) collective-permute-start(bf16[2,128,256]{2,1,0:T(8,128)(2,1)S(1)} %get-tuple-element.44), channel_id=1, source_target_pairs={{0,1},{1,0},{2,3},{3,2},{4,5},{5,4},{6,7},{7,6},{8,9},{9,8},{10,11... | collective-permute-start | bytes 393224 | tf_op jit(solution)/shard_map/ppermute | solution.py:39
  77.8 15.2 %collective-permute-start.9 = (bf16[2,128,256]{2,1,0:T(8,128)(2,1)S(1)}, bf16[2,128,256]{2,1,0:T(8,128)(2,1)S(1)}, u32[]{:S(2)}, u32[]{:S(2)}) collective-permute-start(bf16[2,128,256]{2,1,0:T(8,128)(2,1)S(1)} %get-tuple-element.43), channel_id=1, source_target_pairs={{0,2},{1,3},{2,0},{3,1},{4,6},{5,7},{6,4},{7,5},{8,10},{9,11},{10,... | collective-permute-start | bytes 393224 | tf_op jit(solution)/shard_map/ppermute | solution.py:39
  93.6 4.0 %collective-permute-start.11 = (bf16[2,32,256]{2,1,0:T(8,128)(2,1)S(1)}, bf16[2,32,256]{2,1,0:T(8,128)(2,1)S(1)}, u32[]{:S(2)}, u32[]{:S(2)}) collective-permute-start(bf16[2,32,256]{2,1,0:T(8,128)(2,1)S(1)} %get-tuple-element.39), channel_id=1, source_target_pairs={{0,64},{8,72},{16,80},{24,88},{32,96},{40,104},{48,112},{56,120},{... | collective-permute-start | bytes 98312 | tf_op jit(solution)/shard_map/ppermute | solution.py:39
  93.7 4.6 %collective-permute-start.12 = (bf16[2,32,256]{2,1,0:T(8,128)(2,1)S(1)}, bf16[2,32,256]{2,1,0:T(8,128)(2,1)S(1)}, u32[]{:S(2)}, u32[]{:S(2)}) collective-permute-start(bf16[2,32,256]{2,1,0:T(8,128)(2,1)S(1)} %get-tuple-element.40), channel_id=1, source_target_pairs={{0,128},{8,136},{16,144},{24,152},{32,160},{40,168},{48,176},{56,1... | collective-permute-start | bytes 98312 | tf_op jit(solution)/shard_map/ppermute | solution.py:39
  95.4 4.4 %collective-permute-start.13 = (bf16[2,32,256]{2,1,0:T(8,128)(2,1)S(1)}, bf16[2,32,256]{2,1,0:T(8,128)(2,1)S(1)}, u32[]{:S(2)}, u32[]{:S(2)}) collective-permute-start(bf16[2,32,256]{2,1,0:T(8,128)(2,1)S(1)} %get-tuple-element.41), channel_id=1, source_target_pairs={{0,192},{8,200},{16,208},{24,216},{32,224},{40,232},{48,240},{56,2... | collective-permute-start | bytes 98312 | tf_op jit(solution)/shard_map/ppermute | solution.py:39
  99.9 10.8 %collective-permute-start.14 = (bf16[2,32,256]{2,1,0:T(8,128)(2,1)S(1)}, bf16[2,32,256]{2,1,0:T(8,128)(2,1)S(1)}, u32[]{:S(2)}, u32[]{:S(2)}) collective-permute-start(bf16[2,32,256]{2,1,0:T(8,128)(2,1)S(1)} %add_convert_fusion.2), channel_id=1, source_target_pairs={{0,16},{8,24},{16,0},{24,8},{32,48},{40,56},{48,32},{56,40},{64,80... | collective-permute-start | bytes 98312 | tf_op jit(solution)/shard_map/ppermute | solution.py:39
  100.5 10.2 %collective-permute-start.15 = (bf16[2,32,256]{2,1,0:T(8,128)(2,1)S(1)}, bf16[2,32,256]{2,1,0:T(8,128)(2,1)S(1)}, u32[]{:S(2)}, u32[]{:S(2)}) collective-permute-start(bf16[2,32,256]{2,1,0:T(8,128)(2,1)S(1)} %add_convert_fusion.2), channel_id=1, source_target_pairs={{0,32},{8,40},{16,48},{24,56},{32,0},{40,8},{48,16},{56,24},{64,96... | collective-permute-start | bytes 98312 | tf_op jit(solution)/shard_map/ppermute | solution.py:39
  104.4 6.4 %collective-permute-start.16 = (bf16[2,32,256]{2,1,0:T(8,128)(2,1)S(1)}, bf16[2,32,256]{2,1,0:T(8,128)(2,1)S(1)}, u32[]{:S(2)}, u32[]{:S(2)}) collective-permute-start(bf16[2,32,256]{2,1,0:T(8,128)(2,1)S(1)} %add_convert_fusion.2), channel_id=1, source_target_pairs={{0,48},{8,56},{16,32},{24,40},{32,16},{40,24},{48,0},{56,8},{64,11... | collective-permute-start | bytes 98312 | tf_op jit(solution)/shard_map/ppermute | solution.py:39
  106.7 17.7 %collective-permute-start.6 = (bf16[3,2,32,512]{3,2,1,0:T(8,128)(2,1)S(1)}, bf16[3,2,32,512]{3,2,1,0:T(8,128)(2,1)S(1)}, u32[]{:S(2)}, u32[]{:S(2)}) collective-permute-start(bf16[3,2,32,512]{3,2,1,0:T(8,128)(2,1)S(1)} %get-tuple-element.35), channel_id=1, source_target_pairs={{0,8},{8,16},{16,24},{24,32},{32,40},{40,48},{48,56},{56,64},{64,7... | collective-permute-start | bytes 589832 | tf_op jit(solution)/shard_map/ppermute | solution.py:44
  110.8 3.9 %collective-permute-start.17 = (bf16[2,32,256]{2,1,0:T(8,128)(2,1)S(1)}, bf16[2,32,256]{2,1,0:T(8,128)(2,1)S(1)}, u32[]{:S(2)}, u32[]{:S(2)}) collective-permute-start(bf16[2,32,256]{2,1,0:T(8,128)(2,1)S(1)} %add_convert_fusion.1.part0), channel_id=1, source_target_pairs={{0,64},{8,72},{16,80},{24,88},{32,96},{40,104},{48,112},{56,120},{... | collective-permute-start | bytes 98312 | tf_op jit(solution)/shard_map/ppermute | solution.py:39
  110.9 4.5 %collective-permute-start.18 = (bf16[2,32,256]{2,1,0:T(8,128)(2,1)S(1)}, bf16[2,32,256]{2,1,0:T(8,128)(2,1)S(1)}, u32[]{:S(2)}, u32[]{:S(2)}) collective-permute-start(bf16[2,32,256]{2,1,0:T(8,128)(2,1)S(1)} %add_convert_fusion.1.part0), channel_id=1, source_target_pairs={{0,128},{8,136},{16,144},{24,152},{32,160},{40,168},{48,176},{56,1... | collective-permute-start | bytes 98312 | tf_op jit(solution)/shard_map/ppermute | solution.py:39
  112.8 5.3 %collective-permute-start.19 = (bf16[2,32,256]{2,1,0:T(8,128)(2,1)S(1)}, bf16[2,32,256]{2,1,0:T(8,128)(2,1)S(1)}, u32[]{:S(2)}, u32[]{:S(2)}) collective-permute-start(bf16[2,32,256]{2,1,0:T(8,128)(2,1)S(1)} %add_convert_fusion.1.part0), channel_id=1, source_target_pairs={{0,192},{8,200},{16,208},{24,216},{32,224},{40,232},{48,240},{56,2... | collective-permute-start | bytes 98312 | tf_op jit(solution)/shard_map/ppermute | solution.py:39
  118.7 4.3 %collective-permute-start.20 = (bf16[2,128,256]{2,1,0:T(8,128)(2,1)S(1)}, bf16[2,128,256]{2,1,0:T(8,128)(2,1)S(1)}, u32[]{:S(2)}, u32[]{:S(2)}) collective-permute-start(bf16[2,128,256]{2,1,0:T(8,128)(2,1)S(1)} %shard_map.91.own), channel_id=1, source_target_pairs={{0,8},{8,0},{16,24},{24,16},{32,40},{40,32},{48,56},{56,48},{64,72... | collective-permute-start | bytes 393224 | tf_op jit(solution)/shard_map/ppermute | solution.py:39

commit v2 on v1

v2 whole, which is shorter than its diff:
```python
import math

import jax
import jax.numpy as jnp
import numpy as np
from jax import lax
from jax.experimental import pallas as pl
from jax.experimental.pallas import tpu as pltpu
from jax.sharding import PartitionSpec as P

fresnel = 0.4
SIDE = 256
DEPTH = 3
SLOTS = 4
BF = jnp.bfloat16
F32 = jnp.float32
VMEM = pl.BlockSpec(memory_space=pltpu.VMEM)
HBM = pl.BlockSpec(memory_space=pltpu.HBM)
SMEM = pl.BlockSpec(memory_space=pltpu.SMEM)
PARAMS = pltpu.CompilerParams(vmem_limit_bytes=16 * 1024 * 1024)


def constants():
    index = np.arange(SIDE)
    folded = index[:, None] * index[None, :] % SIDE
    angle = np.float32(2.0 * math.pi / SIDE) * folded.astype(np.float32)
    scale = np.float32(1.0 / math.sqrt(SIDE))
    real = (np.cos(angle) * scale).astype(jnp.bfloat16)
    imag = (-np.sin(angle) * scale).astype(jnp.bfloat16)
    return np.concatenate([real, imag], 1)


def swap(block, axis, bits):
    route = [(i, i ^ bits) for i in range(lax.axis_size(axis))]
    return lax.ppermute(block, axis, route)


def shift(block, axis, distance):
    size = lax.axis_size(axis)
    return lax.ppermute(block, axis, [(i, (i + distance) % size) for i in range(size)])


def dot(first, second):
    return jnp.dot(first, second, preferred_element_type=F32)


def row_of(which, place):
    return which[4 + 2 * place]


def column_of(which, place):
    return which[5 + 2 * place]


def iotas():
    rows = lax.broadcasted_iota(jnp.int32, (SIDE, SIDE), 0)
    cols = lax.broadcasted_iota(jnp.int32, (SIDE, SIDE), 1)
    return rows, cols


def to_residues(offset):
    rows, cols = iotas()
    return jnp.where(((rows - offset) & (SIDE - 1)) == cols, 1.0, 0.0).astype(BF)


def from_residues(offset):
    rows, cols = iotas()
    return jnp.where(((cols - offset) & (SIDE - 1)) == rows, 1.0, 0.0).astype(BF)


def make_tables(which, table, row_t, row_tt, col_t, col_tt, kernel):
    place = which[1]
    offsets = (row_of(which, place), column_of(which, place))
    for offset, plain, turned in zip(offsets, (row_t, col_t), (row_tt, col_tt)):
        rolled = dot(to_residues(offset), table[...]).astype(BF)
        real, imag = rolled[:, :SIDE], rolled[:, SIDE:]
        plain[:SIDE, :SIDE] = real
        plain[:SIDE, SIDE:] = imag
        plain[SIDE:, :SIDE] = -imag
        plain[SIDE:, SIDE:] = real
        back = from_residues(offset)
        real = dot(table[:, :SIDE], back).astype(BF)
        imag = dot(table[:, SIDE:], back).astype(BF)
        turned[:SIDE, :SIDE] = real
        turned[:SIDE, SIDE:] = -imag
        turned[SIDE:, :SIDE] = imag
        turned[SIDE:, SIDE:] = real
    index = lax.broadcasted_iota(jnp.int32, (8, SIDE), 1)
    freq = (((index + SIDE // 2) & (SIDE - 1)) - SIDE // 2).astype(F32)
    phase = freq * freq * (-math.pi * fresnel / SIDE)
    cos_row = jnp.broadcast_to(jnp.cos(phase)[:1], (SIDE, SIDE))
    sin_row = jnp.broadcast_to(jnp.sin(phase)[:1], (SIDE, SIDE))
    cos_col, sin_col = cos_row.T, sin_row.T
    kernel[0] = cos_col * cos_row - sin_col * sin_row
    kernel[1] = cos_col * sin_row + sin_col * cos_row


def fill(field, slot, real, imag):
    field[slot, :SIDE, :] = real.astype(BF)
    field[slot, SIDE:, :] = imag.astype(BF)


def transform(field, mid, slot, left, right):
    turned = dot(left[...], field[slot])
    mid[slot, :, :SIDE] = turned[:SIDE].astype(BF)
    mid[slot, :, SIDE:] = turned[SIDE:].astype(BF)
    out = dot(mid[slot], right[...])
    return out[:, :SIDE], out[:, SIDE:]


def transform_all(field, mid, slots, left, right, store):
    for slot in range(slots):
        store(slot, *transform(field, mid, slot, left, right))


def propagate_all(field, mid, slots, forth, back, kernel, sign, store):
    def turn(slot, real, imag):
        turned = sign * kernel[1]
        fill(field, slot, real * kernel[0] - imag * turned, real * turned + imag * kernel[0])

    transform_all(field, mid, slots, *forth, turn)
    transform_all(field, mid, slots, *back, store)


def choose_kernel(which, above, strip, out):
    cols = lax.broadcasted_iota(jnp.int32, (SIDE, SIDE), 1)
    on_left = cols >= above[which[1], 1]
    part = which[0] >> 2
    for layer in range(DEPTH):
        value = strip[layer, part].astype(F32)
        out[layer] = jnp.where(on_left, value[:, :SIDE], value[:, SIDE:]).astype(BF)


def forward_kernel(which, strip_hbm, *refs):
    mine, other, *probes_hbm = refs[:7]
    table, window, wave0, wave1, wave2, far, total, total_sent, *refs = refs[7:]
    row_t, row_tt, col_t, col_tt, kernel, field, mid, own, probes, sem = refs
    copies = [pltpu.make_async_copy(strip_hbm, own, sem.at[0])]
    places = (probes.at[0], probes.at[1], probes.at[2, 0], probes.at[2, 1], probes.at[3])
    for index, (source, target) in enumerate(zip(probes_hbm, places)):
        copies.append(pltpu.make_async_copy(source, target, sem.at[index + 1]))
    for copy in copies:
        copy.start()
    mode, place = which[0], which[1]
    row, col = row_of(which, place), column_of(which, place)
    make_tables(which, table, row_t, row_tt, col_t, col_tt, kernel)
    there = to_residues(row)
    back = from_residues(col)
    for copy in copies:
        copy.wait()
    for slot in range(SLOTS):
        for part in range(2):
            moved = dot(there, probes[slot, part]).astype(BF)
            wave0[slot, part] = dot(moved, back).astype(BF)
    rows, cols = iotas()
    on_left = cols >= col
    on_strip = rows >= row
    for layer in range(DEPTH):
        for part in range(2):
            strip = own[layer, part].astype(F32)
            picked = jnp.where(on_left, strip[:, :SIDE], strip[:, SIDE:])
            have = (mode >> 2) == part
            below = jnp.where(have, mine[layer].astype(F32), other[layer].astype(F32))
            window[layer, part] = jnp.where(on_strip, picked, below).astype(BF)
    forth = (row_tt, col_t)
    back = (row_t, col_tt)
    waves = (wave0, wave1, wave2)

    def store_far(slot, real, imag):
        far[slot, 0] = real
        far[slot, 1] = imag
        power = real * real + imag * imag
        total[...] = power if slot == 0 else total[...] + power

    for layer in range(DEPTH):
        for slot in range(SLOTS):
            obj_real = window[layer, 0].astype(F32)
            obj_imag = window[layer, 1].astype(F32)
            real = waves[layer][slot, 0].astype(F32)
            imag = waves[layer][slot, 1].astype(F32)
            fill(field, slot, real * obj_real - imag * obj_imag, real * obj_imag + imag * obj_real)
        if layer + 1 < DEPTH:

            def store(slot, real, imag, wave=waves[layer + 1]):
                wave[slot, 0] = real.astype(BF)
                wave[slot, 1] = imag.astype(BF)

            propagate_all(field, mid, SLOTS, forth, back, kernel, 1.0, store)
        else:
            transform_all(field, mid, SLOTS, *forth, store_far)
    total_sent[...] = total[...].astype(BF)


def backward_kernel(
    which, window, wave0, wave1, wave2, far, total, total_got, measured_hbm,
    table,
    grad_keep, grad_send, keep_out, send_out,
    row_t, row_tt, col_t, col_tt, kernel, field, mid, residual, grads, sums, backs, measured, sem,
):
    place = which[1]
    copy = pltpu.make_async_copy(measured_hbm.at[place], measured, sem)
    copy.start()
    row, col = row_of(which, place), column_of(which, place)
    make_tables(which, table, row_t, row_tt, col_t, col_tt, kernel)
    copy.wait()
    residual[...] = total[...] + total_got[...].astype(F32) - measured[...]
    forth = (row_tt, col_t)
    back = (row_t, col_tt)
    waves = (wave0, wave1, wave2)

    def store(slot, real, imag):
        backs[slot, 0] = real.astype(BF)
        backs[slot, 1] = imag.astype(BF)

    for slot in range(SLOTS):
        fill(field, slot, residual[...] * far[slot, 0], residual[...] * far[slot, 1])
    transform_all(field, mid, SLOTS, *back, store)
    for layer in reversed(range(DEPTH)):
        for slot in range(SLOTS):
            gin_real = backs[slot, 0].astype(F32)
            gin_imag = backs[slot, 1].astype(F32)
            real = waves[layer][slot, 0].astype(F32)
            imag = waves[layer][slot, 1].astype(F32)
            grad_real = real * gin_real + imag * gin_imag
            grad_imag = real * gin_imag - imag * gin_real
            if slot > 0:
                grad_real += grads[0]
                grad_imag += grads[1]
            if slot + 1 < SLOTS:
                grads[0] = grad_real
                grads[1] = grad_imag
            else:
                sums[layer, 0] = grad_real.astype(BF)
                sums[layer, 1] = grad_imag.astype(BF)
            obj_real = window[layer, 0].astype(F32)
            obj_imag = window[layer, 1].astype(F32)
            next_real = obj_real * gin_real + obj_imag * gin_imag
            next_imag = obj_real * gin_imag - obj_imag * gin_real
            fill(field, slot, next_real, next_imag)
        if layer > 0:
            propagate_all(field, mid, SLOTS, forth, back, kernel, -1.0, store)
    rows = from_residues(row)
    cols = to_residues(col)
    for slot in range(SLOTS):
        for part in range(2):
            moved = dot(rows, field[slot, part * SIDE : (part + 1) * SIDE, :]).astype(BF)
            backs[slot, part] = dot(moved, cols).astype(BF)
    half = SIDE // 2
    kept = pl.multiple_of((which[0] >> 2) * half, half)
    sent = pl.multiple_of(half - kept, half)
    grad_keep[...] = sums[:, :, pl.ds(kept, half), :]
    grad_send[...] = sums[:, :, pl.ds(sent, half), :]
    kept = pl.multiple_of(which[2] * half, half)
    sent = pl.multiple_of(half - kept, half)
    keep_out[...] = backs[:, :, pl.ds(kept, half), :]
    send_out[...] = backs[:, :, pl.ds(sent, half), :]


def pair_kernel(which, keep, got, own_out, *outs):
    band = SIDE // 8
    for step in range(SLOTS):
        part = pl.ds(pl.multiple_of((which[1] ^ step) * band, band), band)
        for layer in range(DEPTH):
            for side in range(2):
                value = keep[layer, side, part, :].astype(F32) + got[layer, side, part, :].astype(F32)
                if step == 0:
                    own_out[layer, side] = value
                else:
                    outs[step - 1][layer, side] = value.astype(BF)


def gather_kernel(which, own, got1, got2, got3, own_out, spill_out):
    band = SIDE // 8
    top = which[0] * band
    shape = (band, SIDE)
    rows = lax.broadcasted_iota(jnp.int32, shape, 0) + top
    cols = lax.broadcasted_iota(jnp.int32, shape, 1)
    for layer in range(DEPTH):
        for part in range(2):
            sums = [jnp.zeros(shape, F32) for _ in range(4)]
            for step, grads in enumerate((own, got1, got2, got3)):
                value = grads[layer, part].astype(F32)
                place = which[1] ^ step
                on_strip = rows >= row_of(which, place)
                on_left = cols >= column_of(which, place)
                for index, (here, left) in enumerate(
                    ((True, True), (True, False), (False, True), (False, False))
                ):
                    picked = on_strip if here else ~on_strip
                    picked &= on_left if left else ~on_left
                    sums[index] += jnp.where(picked, value, 0.0)
            own_out[layer, part, :, :SIDE] = sums[0]
            own_out[layer, part, :, SIDE:] = sums[1]
            spill_out[layer, part, :, :SIDE] = sums[2].astype(BF)
            spill_out[layer, part, :, SIDE:] = sums[3].astype(BF)


def first_kernel(keep, got, own, sent_one, sent_three):
    for slot in range(SLOTS):
        for part in range(2):
            total = (keep[slot, part].astype(F32) + got[slot, part].astype(F32)).astype(BF)
            if part == 0 and slot in (1, 2):
                sent_one[slot - 1] = total
            elif part == 1 and slot in (2, 3):
                sent_three[3 - slot] = total
            else:
                own[slot if slot == 0 else 1, part] = total


def second_kernel(own, got_one, got_three, held, sent_three, sent_one):
    for part, got, sent in ((0, got_one, sent_three), (1, got_three, sent_one)):
        held[part] = own[0, part].astype(F32) + got[0].astype(F32)
        sent[...] = (own[1, part].astype(F32) + got[1].astype(F32)).astype(BF)


def quarter_kernel(which, held, got_three, got_one, *outs):
    scratch = outs[-1]
    scratch[0] = (held[0] + got_three[...].astype(F32)).astype(BF)
    scratch[1] = (held[1] + got_one[...].astype(F32)).astype(BF)
    depth = scratch.shape[1] // 4
    for step in range(4):
        top = pl.multiple_of((which[3] ^ step) * depth, depth)
        outs[step][...] = scratch[:, pl.ds(top, depth), :]


def merge_kernel(which, part0, part1, part2, part3, out):
    depth = part0.shape[1]
    for step, part in enumerate((part0, part1, part2, part3)):
        top = pl.multiple_of((which[3] ^ step) * depth, depth)
        out[:, pl.ds(top, depth), :] = part[...]


def finish_kernel(which, own, got, out):
    half = SIDE // 2
    kept = pl.multiple_of(which[2] * half, half)
    out[0, :, pl.ds(kept, half), :] = own[...].astype(F32)
    out[0, :, pl.ds(pl.multiple_of(half - kept, half), half), :] = got[...].astype(F32)


def call(kernel, outs, arguments, scalars, scratch=()):
    return pl.pallas_call(
        kernel,
        out_shape=[jax.ShapeDtypeStruct(shape, dtype) for shape, dtype in outs],
        in_specs=[SMEM] * scalars + [VMEM] * (len(arguments) - scalars),
        out_specs=[VMEM] * len(outs),
        scratch_shapes=[pltpu.VMEM(shape, dtype) for shape, dtype in scratch],
        compiler_params=PARAMS,
    )(*arguments)


def on_device(object_slices, probe_modes, positions, measured):
    tile = lax.axis_index("tile")
    mode = lax.axis_index("mode")
    place = mode & (SLOTS - 1)
    which = jnp.stack([mode, place, tile & 1, tile >> 3]).astype(jnp.int32)
    which = jnp.concatenate([which, positions.reshape(-1)])
    half = SIDE // 2
    band = SIDE // 8
    square = (SIDE, SIDE)
    wide = (2 * SIDE, 2 * SIDE)
    table = jnp.asarray(constants())

    above = shift(positions, "tile", 1)
    (chosen,) = call(choose_kernel, [((DEPTH,) + square, BF)], (which, above, object_slices), 2)
    mine = shift(chosen, "tile", -1)
    one, three = (swap(probe_modes[0], "mode", step) for step in (1, 3))
    two = [swap(three[0], "mode", 1), swap(one[1], "mode", 3)]
    other = swap(mine, "mode", 4)

    slots = (SLOTS, 2) + square
    layers = (DEPTH, 2) + square
    scratch = [(wide, BF)] * 4 + [((2,) + square, F32)]
    scratch += [((SLOTS, 2 * SIDE, SIDE), BF), ((SLOTS, SIDE, 2 * SIDE), BF)]
    outs = [(layers, BF)] + [(slots, BF)] * 3 + [(slots, F32), (square, F32), (square, BF)]
    window, wave0, wave1, wave2, far, total, total_sent = pl.pallas_call(
        forward_kernel,
        out_shape=[jax.ShapeDtypeStruct(*out) for out in outs],
        in_specs=[SMEM, HBM] + [VMEM] * 2 + [HBM] * 5 + [VMEM],
        out_specs=[VMEM] * 7,
        scratch_shapes=[
            pltpu.VMEM(*shape)
            for shape in scratch + [((DEPTH, 2, SIDE, 2 * SIDE), BF), (slots, BF)]
        ]
        + [pltpu.SemaphoreType.DMA((6,))],
        compiler_params=PARAMS,
    )(which, object_slices, mine, other, probe_modes[0], one, *two, three, table)
    total_got = swap(total_sent, "mode", 4)
    piece = ((SLOTS, 2, half, SIDE), BF)
    outs = [((DEPTH, 2, half, SIDE), BF)] * 2 + [piece, piece]
    scratch += [(square, F32), ((2,) + square, F32), (layers, BF), (slots, BF), (square, F32)]
    grad_keep, grad_send, keep, send = pl.pallas_call(
        backward_kernel,
        out_shape=[jax.ShapeDtypeStruct(*out) for out in outs],
        in_specs=[SMEM] + [VMEM] * 7 + [HBM, VMEM],
        out_specs=[VMEM] * 4,
        scratch_shapes=[pltpu.VMEM(*shape) for shape in scratch] + [pltpu.SemaphoreType.DMA],
        compiler_params=PARAMS,
    )(which, window, wave0, wave1, wave2, far, total, total_got, measured, table)

    grad_got = swap(grad_send, "mode", 4)

    pair = ((2, half, SIDE), BF)
    own, sent_one, sent_three = call(
        first_kernel, [((2,) + pair[0], BF), pair, pair], (keep, swap(send, "tile", 1)), 0
    )
    held, sent_three, sent_one = call(
        second_kernel,
        [(pair[0], F32), ((half, SIDE), BF), ((half, SIDE), BF)],
        (own, swap(sent_one, "mode", 1), swap(sent_three, "mode", 3)),
        0,
    )
    quarters = call(
        quarter_kernel,
        [((2, half // 4, SIDE), BF)] * 4,
        (which, held, swap(sent_three, "mode", 3), swap(sent_one, "mode", 1)),
        1,
        [pair],
    )
    parts = [quarters[0]] + [swap(quarters[step], "tile", step << 3) for step in range(1, 4)]
    grad_got, quarters = lax.optimization_barrier((grad_got, quarters))
    shape = (DEPTH, 2, band, SIDE)
    bands = call(
        pair_kernel, [(shape, F32)] + [(shape, BF)] * 3, (which, grad_keep, grad_got), 1
    )
    bands, parts = lax.optimization_barrier((bands, parts))
    bands = [bands[0]] + [swap(bands[step], "mode", step) for step in range(1, 4)]
    part = ((parts[0].astype(F32) + parts[1]) + (parts[2].astype(F32) + parts[3])).astype(BF)
    parts = [part] + [swap(part, "tile", step << 1) for step in range(1, 4)]
    part = ((parts[0].astype(F32) + parts[1]) + (parts[2].astype(F32) + parts[3])).astype(BF)
    shape = (DEPTH, 2, band, 2 * SIDE)
    own_grad, spill = call(gather_kernel, [(shape, F32), (shape, BF)], (which, *bands), 1)
    part, spill = lax.optimization_barrier((part, spill))
    parts = [part] + [swap(part, "tile", step << 3) for step in range(1, 4)]
    (merged,) = call(merge_kernel, [((2, half, SIDE), BF)], (which, *parts), 1)
    (probe_grad,) = call(
        finish_kernel, [((1, 2) + square, F32)], (which, merged, swap(merged, "tile", 1)), 1
    )

    object_grad = own_grad + shift(spill, "tile", 1).astype(F32)
    return (object_grad, probe_grad)


def solution(mesh):
    placed = (
        P(None, None, "tile", None),
        P("mode", None, None, None),
        P("tile", None),
        P("tile", None, None),
    )
    return jax.shard_map(
        on_device,
        mesh=mesh,
        in_specs=placed,
        out_specs=(P(None, None, ("tile", "mode"), None), P("mode", None, None, None)),
        check_vma=False,
    )
```

time: 125 us -> 112 us (0.90)
  Pallas kernels: 32 us -> 22.4 us
  starting transfers between devices: 45.8 us -> 50.7 us
  waiting for transfers between devices: 38.6 us -> 34.9 us
  other arithmetic: 4.06 us -> 0.84 us
  local copies, waits for them, and re-layouts: 3.84 us -> 2.37 us
    pallas_call x7 -> x8, Pallas kernels: 32 us -> 4.87 us  [call(): pl.pallas_call(kernel, out_shape=[jax.ShapeDtypeStruct(shape, dtype) for...]
    pallas_call x0 -> x2, Pallas kernels: none -> 17.6 us  [the longest x1 8.98 us: on_device(): pl.pallas_call(backward_kernel, out_shape=[jax.ShapeDtypeStruct(*out) for...]
    ppermute x18 -> x25, waiting for transfers between devices: 37.9 us -> 29.5 us  [swap(): return lax.ppermute(block, axis, route)]
    ppermute x3, starting transfers between devices: 14 us -> 18.8 us  [shift(): lax.ppermute(block, axis, [(i, (i + distance) % size) for i in range(size)])]
    ppermute x3, waiting for transfers between devices: 0.73 us -> 5.35 us  [shift(): lax.ppermute(block, axis, [(i, (i + distance) % size) for i in range(size)])]
    ppermute x18 -> x25, starting transfers between devices: 28.2 us -> 31.9 us  [swap(): return lax.ppermute(block, axis, route)]
    all_to_all x1 -> x0, starting transfers between devices: 3.55 us -> none  [on_device(): bands = lax.all_to_all(grads, 'mode', 0, 0, tiled=True)]
    select_n x1 -> x0, other arithmetic: 2.36 us -> none  [on_device(): jnp.where(columns >= above[1], object_slices[..., :SIDE], object_slices[....]
  transfers between devices with their start and end apart: 22 -> 28, of which waited for: 12 -> 21; matrix products, arithmetic and copies ran while one was open for 0% -> 0% of each run, Pallas kernels for 5% -> 3%
where the time goes in v2:
time: 112 us
  starting transfers between devices  50.7 us (45%)
  waiting for transfers between devices  34.9 us (31%)
  Pallas kernels  22.4 us (20%)
  local copies, waits for them, and re-layouts  2.37 us (2%)
    ppermute x25, starting transfers between devices, swap(): return lax.ppermute(block, axis, route)  31.9 us
    ppermute x25, waiting for transfers between devices, swap(): return lax.ppermute(block, axis, route)  29.5 us
    ppermute x3, starting transfers between devices, shift(): lax.ppermute(block, axis, [(i, (i + distance) % size) for i in range(size)])  18.8 us
    pallas_call x1, Pallas kernels, on_device(): pl.pallas_call(backward_kernel, out_shape=[jax.ShapeDtypeStruct(*out) for...  8.98 us
    pallas_call x1, Pallas kernels, on_device(): pl.pallas_call(forward_kernel, out_shape=[jax.ShapeDtypeStruct(*out) for...  8.58 us
    ppermute x3, waiting for transfers between devices, shift(): lax.ppermute(block, axis, [(i, (i + distance) % size) for i in range(size)])  5.35 us
    pallas_call x8, Pallas kernels, call(): pl.pallas_call(kernel, out_shape=[jax.ShapeDtypeStruct(shape, dtype) for...  4.87 us
  transfers between devices with their start and end apart: 28, of which 21 were waited for; matrix products, arithmetic and copies ran while one was open for 0% of the time, Pallas kernels for 3%

profile of v2, /device:TPU:1, one launch (start us, length us, event | category | flops | bytes accessed | tf_op | source)
XLA Modules:
  0.0 112.0 jit_solution(681041816548665375)
XLA Ops:
  0.6 0.8 copy.9
  1.4 4.4 %collective-permute-start = (s32[4,2]{1,0:T(4,128)S(1)}, s32[4,2]{1,0:T(4,128)S(1)}, u32[]{:S(2)}, u32[]{:S(2)}) collective-permute-start(s32[4,2]{1,0:T(4,128)S(1)} %copy.9), channel_id=1, source_target_pairs={{0,8},{8,16},{16,24},{24,32},{32,40},{40,48},{48,56},{56,64},{64,7... | collective-permute-start | bytes 104 | tf_op jit(solution)/shard_map/ppermute | solution.py:40
  5.8 0.1 reshape.7
  5.9 0.1 concatenate.3.which
  5.9 0.6 collective-permute-done.above
  6.5 1.4 %copy-done = bf16[3,2,256,512]{3,2,1,0:T(8,128)(2,1)S(1)} copy-done((bf16[3,2,256,512]{3,2,1,0:T(8,128)(2,1)S(1)}, bf16[3,2,256,512]{3,2,1,0:T(8,128)(2,1)}, u32[]{:S(2)}) %copy-start) | copy-done | bytes 1572888
  7.9 0.7 shard_map.68
  8.6 5.7 %collective-permute-start.1 = (bf16[3,256,256]{2,1,0:T(8,128)(2,1)S(1)}, bf16[3,256,256]{2,1,0:T(8,128)(2,1)S(1)}, u32[]{:S(2)}, u32[]{:S(2)}) collective-permute-start(bf16[3,256,256]{2,1,0:T(8,128)(2,1)S(1)} %shard_map.68), channel_id=1, source_target_pairs={{0,248},{8,0},{16,8},{24,16},{32,24},{40,32},{48,40},{56,48},{64,5... | collective-permute-start | bytes 1179656 | tf_op jit(solution)/shard_map/ppermute | solution.py:40
  14.3 2.8 %collective-permute-start.4 = (bf16[2,256,256]{2,1,0:T(8,128)(2,1)}, bf16[2,256,256]{2,1,0:T(8,128)(2,1)S(1)}, u32[]{:S(2)}, u32[]{:S(2)}) collective-permute-start(bf16[2,256,256]{2,1,0:T(8,128)(2,1)} %bitcast.9), channel_id=1, source_target_pairs={{0,3},{1,2},{2,1},{3,0},{4,7},{5,6},{6,5},{7,4},{8,11},{9,10},{10,... | collective-permute-start | bytes 786440 | tf_op jit(solution)/shard_map/ppermute | solution.py:35
  17.0 0.0 collective-permute-start.3
  17.0 4.8 %collective-permute-done.1.refs_0_ = bf16[3,256,256]{2,1,0:T(8,128)(2,1)S(1)} collective-permute-done((bf16[3,256,256]{2,1,0:T(8,128)(2,1)S(1)}, bf16[3,256,256]{2,1,0:T(8,128)(2,1)S(1)}, u32[]{:S(2)}, u32[]{:S(2)}) %collective-permute-start.1) | collective-permute-done | bytes 393248 | tf_op jit(solution)/shard_map/ppermute | solution.py:40
  21.8 1.8 %collective-permute-done.4.refs_6_ = bf16[2,256,256]{2,1,0:T(8,128)(2,1)S(1)} collective-permute-done((bf16[2,256,256]{2,1,0:T(8,128)(2,1)}, bf16[2,256,256]{2,1,0:T(8,128)(2,1)S(1)}, u32[]{:S(2)}, u32[]{:S(2)}) %collective-permute-start.4) | collective-permute-done | bytes 262176 | tf_op jit(solution)/shard_map/ppermute | solution.py:35
  23.7 0.1 collective-permute-start.5
  23.8 1.0 collective-permute-done.3.refs_3_
  24.8 1.7 %collective-permute-start.6 = (bf16[256,256]{1,0:T(8,128)(2,1)S(1)}, bf16[256,256]{1,0:T(8,128)(2,1)S(1)}, u32[]{:S(2)}, u32[]{:S(2)}) collective-permute-start(bf16[256,256]{1,0:T(8,128)(2,1)S(1)} %slice_bitcast_fusion), channel_id=1, source_target_pairs={{0,3},{1,2},{2,1},{3,0},{4,7},{5,6},{6,5},{7,4},{8,11},{9,10},{10,... | collective-permute-start | bytes 393224 | tf_op jit(solution)/shard_map/ppermute | solution.py:35
  26.5 1.4 %collective-permute-done.5.refs_4_ = bf16[256,256]{1,0:T(8,128)(2,1)S(1)} collective-permute-done((bf16[256,256]{1,0:T(8,128)(2,1)S(1)}, bf16[256,256]{1,0:T(8,128)(2,1)S(1)}, u32[]{:S(2)}, u32[]{:S(2)}) %collective-permute-start.5) | collective-permute-done | bytes 131104 | tf_op jit(solution)/shard_map/ppermute | solution.py:35
  27.9 2.0 %collective-permute-done.6.refs_5_ = bf16[256,256]{1,0:T(8,128)(2,1)S(1)} collective-permute-done((bf16[256,256]{1,0:T(8,128)(2,1)S(1)}, bf16[256,256]{1,0:T(8,128)(2,1)S(1)}, u32[]{:S(2)}, u32[]{:S(2)}) %collective-permute-start.6) | collective-permute-done | bytes 131104 | tf_op jit(solution)/shard_map/ppermute | solution.py:35
  29.9 0.5 collective-permute-done.2.refs_1_
  30.4 8.6 %shard_map.69 = (bf16[3,2,256,256]{3,2,1,0:T(8,128)(2,1)S(1)}, bf16[4,2,256,256]{3,2,1,0:T(8,128)(2,1)S(1)}, bf16[4,2,256,256]{3,2,1,0:T(8,128)(2,1)S(1)}, bf16[...) custom-call(s32[12]{0:T(128)S(1)} %concatenate.3.which, ...), custom_call_target="tpu_custom_call" | custom-call | tf_op jit(solution)/shard_map/pallas_call | solution.py:375
  39.0 0.6 collective-permute-start.7
  39.5 3.5 %collective-permute-done.7.total_got = bf16[256,256]{1,0:T(8,128)(2,1)S(1)} collective-permute-done((bf16[256,256]{1,0:T(8,128)(2,1)S(1)}, bf16[256,256]{1,0:T(8,128)(2,1)S(1)}, u32[]{:S(2)}, u32[]{:S(2)}) %collective-permute-start.7) | collective-permute-done | bytes 131104 | tf_op jit(solution)/shard_map/ppermute | solution.py:35
  43.1 9.0 %shard_map.70 = (bf16[3,2,128,256]{3,2,1,0:T(8,128)(2,1)S(1)}, bf16[3,2,128,256]{3,2,1,0:T(8,128)(2,1)S(1)}, bf16[4,2,128,256]{3,2,1,0:T(8,128)(2,1)S(1)}, bf16[4,2,128,256]{3,2,1,0:T(8,128)(2,1)S(1)}) custom-call(s32[12]{0:T(128)S(1)} %concatenate.3.which, bf16[3,2,256,256]{3,2,1,0:T(8,128)(2,1)S(1)} %get-tuple-element.40.window, ...), custom_call_target="tpu_custom_call" | custom-call | tf_op jit(solution)/shard_map/pallas_call | solution.py:391
  52.1 4.2 %collective-permute-start.9 = (bf16[4,2,128,256]{3,2,1,0:T(8,128)(2,1)S(1)}, bf16[4,2,128,256]{3,2,1,0:T(8,128)(2,1)S(1)}, u32[]{:S(2)}, u32[]{:S(2)}) collective-permute-start(bf16[4,2,128,256]{3,2,1,0:T(8,128)(2,1)S(1)} %get-tuple-element.50), channel_id=1, source_target_pairs={{0,8},{8,0},{16,24},{24,16},{32,40},{40,32},{48,56},{56,48},{64,72... | collective-permute-start | bytes 1572872 | tf_op jit(solution)/shard_map/ppermute | solution.py:35
  56.2 0.3 collective-permute-start.8
  56.5 1.3 %collective-permute-done.9.got = bf16[4,2,128,256]{3,2,1,0:T(8,128)(2,1)S(1)} collective-permute-done((bf16[4,2,128,256]{3,2,1,0:T(8,128)(2,1)S(1)}, bf16[4,2,128,256]{3,2,1,0:T(8,128)(2,1)S(1)}, u32[]{:S(2)}, u32[]{:S(2)}) %collective-permute-start.9) | collective-permute-done | bytes 524320 | tf_op jit(solution)/shard_map/ppermute | solution.py:35
  57.8 0.1 shard_map.71
  57.9 1.1 collective-permute-start.10
  59.0 1.9 %collective-permute-start.11 = (bf16[2,128,256]{2,1,0:T(8,128)(2,1)S(1)}, bf16[2,128,256]{2,1,0:T(8,128)(2,1)S(1)}, u32[]{:S(2)}, u32[]{:S(2)}) collective-permute-start(bf16[2,128,256]{2,1,0:T(8,128)(2,1)S(1)} %get-tuple-element.53), channel_id=1, source_target_pairs={{0,3},{1,2},{2,1},{3,0},{4,7},{5,6},{6,5},{7,4},{8,11},{9,10},{10,... | collective-permute-start | bytes 393224 | tf_op jit(solution)/shard_map/ppermute | solution.py:35
  60.9 1.8 %collective-permute-done.10.got_one = bf16[2,128,256]{2,1,0:T(8,128)(2,1)S(1)} collective-permute-done((bf16[2,128,256]{2,1,0:T(8,128)(2,1)S(1)}, bf16[2,128,256]{2,1,0:T(8,128)(2,1)S(1)}, u32[]{:S(2)}, u32[]{:S(2)}) %collective-permute-start.10) | collective-permute-done | bytes 131104 | tf_op jit(solution)/shard_map/ppermute | solution.py:35
  62.7 1.9 %collective-permute-done.11.got_three = bf16[2,128,256]{2,1,0:T(8,128)(2,1)S(1)} collective-permute-done((bf16[2,128,256]{2,1,0:T(8,128)(2,1)S(1)}, bf16[2,128,256]{2,1,0:T(8,128)(2,1)S(1)}, u32[]{:S(2)}, u32[]{:S(2)}) %collective-permute-start.11) | collective-permute-done | bytes 131104 | tf_op jit(solution)/shard_map/ppermute | solution.py:35
  64.6 0.1 shard_map.72
  64.7 2.0 %collective-permute-start.12 = (bf16[128,256]{1,0:T(8,128)(2,1)S(1)}, bf16[128,256]{1,0:T(8,128)(2,1)S(1)}, u32[]{:S(2)}, u32[]{:S(2)}) collective-permute-start(bf16[128,256]{1,0:T(8,128)(2,1)S(1)} %get-tuple-element.55), channel_id=1, source_target_pairs={{0,3},{1,2},{2,1},{3,0},{4,7},{5,6},{6,5},{7,4},{8,11},{9,10},{10,... | collective-permute-start | bytes 196616 | tf_op jit(solution)/shard_map/ppermute | solution.py:35
  66.7 2.4 %collective-permute-done.12.got_three = bf16[128,256]{1,0:T(8,128)(2,1)S(1)} collective-permute-done((bf16[128,256]{1,0:T(8,128)(2,1)S(1)}, bf16[128,256]{1,0:T(8,128)(2,1)S(1)}, u32[]{:S(2)}, u32[]{:S(2)}) %collective-permute-start.12) | collective-permute-done | bytes 65568 | tf_op jit(solution)/shard_map/ppermute | solution.py:35
  69.1 0.7 collective-permute-done.13.got_one
  69.8 0.6 shard_map.73
  70.4 1.8 %collective-permute-start.14 = (bf16[2,32,256]{2,1,0:T(8,128)(2,1)S(1)}, bf16[2,32,256]{2,1,0:T(8,128)(2,1)S(1)}, u32[]{:S(2)}, u32[]{:S(2)}) collective-permute-start(bf16[2,32,256]{2,1,0:T(8,128)(2,1)S(1)} %get-tuple-element.58), channel_id=1, source_target_pairs={{0,64},{8,72},{16,80},{24,88},{32,96},{40,104},{48,112},{56,120},{... | collective-permute-start | bytes 98312 | tf_op jit(solution)/shard_map/ppermute | solution.py:35
  72.2 2.1 %collective-permute-start.15 = (bf16[2,32,256]{2,1,0:T(8,128)(2,1)S(1)}, bf16[2,32,256]{2,1,0:T(8,128)(2,1)S(1)}, u32[]{:S(2)}, u32[]{:S(2)}) collective-permute-start(bf16[2,32,256]{2,1,0:T(8,128)(2,1)S(1)} %get-tuple-element.59), channel_id=1, source_target_pairs={{0,128},{8,136},{16,144},{24,152},{32,160},{40,168},{48,176},{56,1... | collective-permute-start | bytes 98312 | tf_op jit(solution)/shard_map/ppermute | solution.py:35
  74.3 0.3 collective-permute-start.16
  74.7 0.6 shard_map.74
  75.3 0.0 collective-permute-done.14
  75.3 1.1 %collective-permute-done.15 = bf16[2,32,256]{2,1,0:T(8,128)(2,1)S(1)} collective-permute-done((bf16[2,32,256]{2,1,0:T(8,128)(2,1)S(1)}, bf16[2,32,256]{2,1,0:T(8,128)(2,1)S(1)}, u32[]{:S(2)}, u32[]{:S(2)}) %collective-permute-start.15) | collective-permute-done | bytes 32800 | tf_op jit(solution)/shard_map/ppermute | solution.py:35
  76.5 1.8 %collective-permute-done.16 = bf16[2,32,256]{2,1,0:T(8,128)(2,1)S(1)} collective-permute-done((bf16[2,32,256]{2,1,0:T(8,128)(2,1)S(1)}, bf16[2,32,256]{2,1,0:T(8,128)(2,1)S(1)}, u32[]{:S(2)}, u32[]{:S(2)}) %collective-permute-start.16) | collective-permute-done | bytes 32800 | tf_op jit(solution)/shard_map/ppermute | solution.py:35
  78.3 2.8 %collective-permute-start.22 = (bf16[2,32,256]{2,1,0:T(8,128)(2,1)S(1)}, bf16[2,32,256]{2,1,0:T(8,128)(2,1)S(1)}, u32[]{:S(2)}, u32[]{:S(2)}) collective-permute-start(bf16[2,32,256]{2,1,0:T(8,128)(2,1)S(1)} %add_convert_fusion.1), channel_id=1, source_target_pairs={{0,48},{8,56},{16,32},{24,40},{32,16},{40,24},{48,0},{56,8},{64,11... | collective-permute-start | bytes 98312 | tf_op jit(solution)/shard_map/ppermute | solution.py:35
  81.2 2.7 %collective-permute-start.21 = (bf16[2,32,256]{2,1,0:T(8,128)(2,1)S(1)}, bf16[2,32,256]{2,1,0:T(8,128)(2,1)S(1)}, u32[]{:S(2)}, u32[]{:S(2)}) collective-permute-start(bf16[2,32,256]{2,1,0:T(8,128)(2,1)S(1)} %add_convert_fusion.1), channel_id=1, source_target_pairs={{0,32},{8,40},{16,48},{24,56},{32,0},{40,8},{48,16},{56,24},{64,96... | collective-permute-start | bytes 98312 | tf_op jit(solution)/shard_map/ppermute | solution.py:35
  83.9 0.2 collective-permute-start.20
  84.1 0.3 collective-permute-start.17
  84.4 2.1 %collective-permute-start.18 = (bf16[3,2,32,256]{3,2,1,0:T(8,128)(2,1)S(1)}, bf16[3,2,32,256]{3,2,1,0:T(8,128)(2,1)S(1)}, u32[]{:S(2)}, u32[]{:S(2)}) collective-permute-start(bf16[3,2,32,256]{3,2,1,0:T(8,128)(2,1)S(1)} %get-tuple-element.68), channel_id=1, source_target_pairs={{0,2},{1,3},{2,0},{3,1},{4,6},{5,7},{6,4},{7,5},{8,10},{9,11},{10,... | collective-permute-start | bytes 294920 | tf_op jit(solution)/shard_map/ppermute | solution.py:35
  86.5 0.0 collective-permute-done.22
  86.5 1.5 %collective-permute-start.19 = (bf16[3,2,32,256]{3,2,1,0:T(8,128)(2,1)S(1)}, bf16[3,2,32,256]{3,2,1,0:T(8,128)(2,1)S(1)}, u32[]{:S(2)}, u32[]{:S(2)}) collective-permute-start(bf16[3,2,32,256]{3,2,1,0:T(8,128)(2,1)S(1)} %get-tuple-element.69), channel_id=1, source_target_pairs={{0,3},{1,2},{2,1},{3,0},{4,7},{5,6},{6,5},{7,4},{8,11},{9,10},{10,... | collective-permute-start | bytes 294920 | tf_op jit(solution)/shard_map/ppermute | solution.py:35
  88.0 0.6 collective-permute-done.20
  88.6 1.0 collective-permute-done.18.got2
  89.5 1.6 %collective-permute-done.19.got3 = bf16[3,2,32,256]{3,2,1,0:T(8,128)(2,1)S(1)} collective-permute-done((bf16[3,2,32,256]{3,2,1,0:T(8,128)(2,1)S(1)}, bf16[3,2,32,256]{3,2,1,0:T(8,128)(2,1)S(1)}, u32[]{:S(2)}, u32[]{:S(2)}) %collective-permute-start.19) | collective-permute-done | bytes 98336 | tf_op jit(solution)/shard_map/ppermute | solution.py:35
  91.2 0.9 shard_map.75
  92.1 8.8 %collective-permute-start.23 = (bf16[3,2,32,512]{3,2,1,0:T(8,128)(2,1)S(1)}, bf16[3,2,32,512]{3,2,1,0:T(8,128)(2,1)S(1)}, u32[]{:S(2)}, u32[]{:S(2)}) collective-permute-start(bf16[3,2,32,512]{3,2,1,0:T(8,128)(2,1)S(1)} %get-tuple-element.76), channel_id=1, source_target_pairs={{0,8},{8,16},{16,24},{24,32},{32,40},{40,48},{48,56},{56,64},{64,7... | collective-permute-start | bytes 589832 | tf_op jit(solution)/shard_map/ppermute | solution.py:40
  100.9 0.4 collective-permute-start.26
  101.3 0.1 collective-permute-start.25
  101.4 2.8 %collective-permute-start.24 = (bf16[2,32,256]{2,1,0:T(8,128)(2,1)S(1)}, bf16[2,32,256]{2,1,0:T(8,128)(2,1)S(1)}, u32[]{:S(2)}, u32[]{:S(2)}) collective-permute-start(bf16[2,32,256]{2,1,0:T(8,128)(2,1)S(1)} %add_convert_fusion.part0), channel_id=1, source_target_pairs={{0,64},{8,72},{16,80},{24,88},{32,96},{40,104},{48,112},{56,120},{... | collective-permute-start | bytes 98312 | tf_op jit(solution)/shard_map/ppermute | solution.py:35
  104.1 0.7 collective-permute-done.26.part3
  104.8 3.0 %collective-permute-done.25.part2 = bf16[2,32,256]{2,1,0:T(8,128)(2,1)S(1)} collective-permute-done((bf16[2,32,256]{2,1,0:T(8,128)(2,1)S(1)}, bf16[2,32,256]{2,1,0:T(8,128)(2,1)S(1)}, u32[]{:S(2)}, u32[]{:S(2)}) %collective-permute-start.25) | collective-permute-done | bytes 32800 | tf_op jit(solution)/shard_map/ppermute | solution.py:35
  107.9 0.6 shard_map.76.own
  108.4 0.1 collective-permute-start.27
  108.5 1.3 %collective-permute-done.27.got = bf16[2,128,256]{2,1,0:T(8,128)(2,1)S(1)} collective-permute-done((bf16[2,128,256]{2,1,0:T(8,128)(2,1)S(1)}, bf16[2,128,256]{2,1,0:T(8,128)(2,1)S(1)}, u32[]{:S(2)}, u32[]{:S(2)}) %collective-permute-start.27) | collective-permute-done | bytes 131104 | tf_op jit(solution)/shard_map/ppermute | solution.py:35
  109.9 1.4 %shard_map.77 = f32[1,2,256,256]{3,2,1,0:T(8,128)} custom-call(s32[12]{0:T(128)S(1)} %concatenate.3.which, bf16[2,128,256]{2,1,0:T(8,128)(2,1)S(1)} %shard_map.76.own, bf16[2,128,256]{2,1,0:T(8,128)(2,1)S(1)} %collective-permute-done.27.got), custom_call_target="tpu_custom_call" | custom-call | tf_op jit(solution)/shard_map/pallas_call | solution.py:341
  111.2 0.8 convert_add_fusion
  (20 shorter events, 0.1 us)
Async XLA Ops:
  1.4 5.1 %collective-permute-start = (s32[4,2]{1,0:T(4,128)S(1)}, s32[4,2]{1,0:T(4,128)S(1)}, u32[]{:S(2)}, u32[]{:S(2)}) collective-permute-start(s32[4,2]{1,0:T(4,128)S(1)} %copy.9), channel_id=1, source_target_pairs={{0,8},{8,16},{16,24},{24,32},{32,40},{40,48},{48,56},{56,64},{64,7... | collective-permute-start | bytes 104 | tf_op jit(solution)/shard_map/ppermute | solution.py:40
  6.5 1.4 %copy-start = (bf16[3,2,256,512]{3,2,1,0:T(8,128)(2,1)S(1)}, bf16[3,2,256,512]{3,2,1,0:T(8,128)(2,1)}, u32[]{:S(2)}) copy-start(bf16[3,2,256,512]{3,2,1,0:T(8,128)(2,1)} %strip_hbm.1) | copy-start | bytes 4718596
  7.9 22.5 %copy-start.1 = (bf16[3,2,256,512]{3,2,1,0:T(8,128)(2,1)S(1)}, bf16[3,2,256,512]{3,2,1,0:T(8,128)(2,1)}, u32[]{:S(2)}) copy-start(bf16[3,2,256,512]{3,2,1,0:T(8,128)(2,1)} %strip_hbm.1) | copy-start | bytes 4718596
  7.9 22.5 %copy-start.3 = (bf16[256,512]{1,0:T(8,128)(2,1)S(1)}, bf16[256,512]{1,0:T(8,128)(2,1)}, u32[]{:S(2)}) copy-start(bf16[256,512]{1,0:T(8,128)(2,1)} %constant.15.clone.refs_7_.table) | copy-start | bytes 786436
  7.9 22.5 %copy-start.4 = (bf16[1,2,256,256]{3,2,1,0:T(8,128)(2,1)S(1)}, bf16[1,2,256,256]{3,2,1,0:T(8,128)(2,1)}, u32[]{:S(2)}) copy-start(bf16[1,2,256,256]{3,2,1,0:T(8,128)(2,1)} %param.6) | copy-start | bytes 786436
  8.6 13.2 %collective-permute-start.1 = (bf16[3,256,256]{2,1,0:T(8,128)(2,1)S(1)}, bf16[3,256,256]{2,1,0:T(8,128)(2,1)S(1)}, u32[]{:S(2)}, u32[]{:S(2)}) collective-permute-start(bf16[3,256,256]{2,1,0:T(8,128)(2,1)S(1)} %shard_map.68), channel_id=1, source_target_pairs={{0,248},{8,0},{16,8},{24,16},{32,24},{40,32},{48,40},{56,48},{64,5... | collective-permute-start | bytes 1179656 | tf_op jit(solution)/shard_map/ppermute | solution.py:40
  14.3 28.8 %copy-start.2 = (f32[4,256,256]{2,1,0:T(8,128)S(1)}, f32[4,256,256]{2,1,0:T(8,128)}, u32[]{:S(2)}) copy-start(f32[4,256,256]{2,1,0:T(8,128)} %measured_hbm.1) | copy-start | bytes 3145732
  14.3 9.4 %collective-permute-start.4 = (bf16[2,256,256]{2,1,0:T(8,128)(2,1)}, bf16[2,256,256]{2,1,0:T(8,128)(2,1)S(1)}, u32[]{:S(2)}, u32[]{:S(2)}) collective-permute-start(bf16[2,256,256]{2,1,0:T(8,128)(2,1)} %bitcast.9), channel_id=1, source_target_pairs={{0,3},{1,2},{2,1},{3,0},{4,7},{5,6},{6,5},{7,4},{8,11},{9,10},{10,... | collective-permute-start | bytes 786440 | tf_op jit(solution)/shard_map/ppermute | solution.py:35
  17.0 7.7 %collective-permute-start.3 = (bf16[2,256,256]{2,1,0:T(8,128)(2,1)}, bf16[2,256,256]{2,1,0:T(8,128)(2,1)S(1)}, u32[]{:S(2)}, u32[]{:S(2)}) collective-permute-start(bf16[2,256,256]{2,1,0:T(8,128)(2,1)} %bitcast.10), channel_id=1, source_target_pairs={{0,1},{1,0},{2,3},{3,2},{4,5},{5,4},{6,7},{7,6},{8,9},{9,8},{10,11... | collective-permute-start | bytes 786440 | tf_op jit(solution)/shard_map/ppermute | solution.py:35
  21.8 8.6 %collective-permute-start.2 = (bf16[3,256,256]{2,1,0:T(8,128)(2,1)S(1)}, bf16[3,256,256]{2,1,0:T(8,128)(2,1)S(1)}, u32[]{:S(2)}, u32[]{:S(2)}) collective-permute-start(bf16[3,256,256]{2,1,0:T(8,128)(2,1)S(1)} %collective-permute-done.1.refs_0_), channel_id=1, source_target_pairs={{0,4},{1,5},{2,6},{3,7},{4,0},{5,1},{6,2},{7,3},{8,12},{9,13},{10,... | collective-permute-start | bytes 1179656 | tf_op jit(solution)/shard_map/ppermute | solution.py:35
  23.7 4.3 %collective-permute-start.5 = (bf16[256,256]{1,0:T(8,128)(2,1)S(1)}, bf16[256,256]{1,0:T(8,128)(2,1)S(1)}, u32[]{:S(2)}, u32[]{:S(2)}) collective-permute-start(bf16[256,256]{1,0:T(8,128)(2,1)S(1)} %slice_bitcast_fusion.1), channel_id=1, source_target_pairs={{0,1},{1,0},{2,3},{3,2},{4,5},{5,4},{6,7},{7,6},{8,9},{9,8},{10,11... | collective-permute-start | bytes 393224 | tf_op jit(solution)/shard_map/ppermute | solution.py:35
  24.8 5.1 %collective-permute-start.6 = (bf16[256,256]{1,0:T(8,128)(2,1)S(1)}, bf16[256,256]{1,0:T(8,128)(2,1)S(1)}, u32[]{:S(2)}, u32[]{:S(2)}) collective-permute-start(bf16[256,256]{1,0:T(8,128)(2,1)S(1)} %slice_bitcast_fusion), channel_id=1, source_target_pairs={{0,3},{1,2},{2,1},{3,0},{4,7},{5,6},{6,5},{7,4},{8,11},{9,10},{10,... | collective-permute-start | bytes 393224 | tf_op jit(solution)/shard_map/ppermute | solution.py:35
  39.0 4.1 %collective-permute-start.7 = (bf16[256,256]{1,0:T(8,128)(2,1)S(1)}, bf16[256,256]{1,0:T(8,128)(2,1)S(1)}, u32[]{:S(2)}, u32[]{:S(2)}) collective-permute-start(bf16[256,256]{1,0:T(8,128)(2,1)S(1)} %get-tuple-element.46), channel_id=1, source_target_pairs={{0,4},{1,5},{2,6},{3,7},{4,0},{5,1},{6,2},{7,3},{8,12},{9,13},{10,... | collective-permute-start | bytes 393224 | tf_op jit(solution)/shard_map/ppermute | solution.py:35
  52.1 5.7 %collective-permute-start.9 = (bf16[4,2,128,256]{3,2,1,0:T(8,128)(2,1)S(1)}, bf16[4,2,128,256]{3,2,1,0:T(8,128)(2,1)S(1)}, u32[]{:S(2)}, u32[]{:S(2)}) collective-permute-start(bf16[4,2,128,256]{3,2,1,0:T(8,128)(2,1)S(1)} %get-tuple-element.50), channel_id=1, source_target_pairs={{0,8},{8,0},{16,24},{24,16},{32,40},{40,32},{48,56},{56,48},{64,72... | collective-permute-start | bytes 1572872 | tf_op jit(solution)/shard_map/ppermute | solution.py:35
  56.2 18.4 %collective-permute-start.8 = (bf16[3,2,128,256]{3,2,1,0:T(8,128)(2,1)S(1)}, bf16[3,2,128,256]{3,2,1,0:T(8,128)(2,1)S(1)}, u32[]{:S(2)}, u32[]{:S(2)}) collective-permute-start(bf16[3,2,128,256]{3,2,1,0:T(8,128)(2,1)S(1)} %get-tuple-element.48), channel_id=1, source_target_pairs={{0,4},{1,5},{2,6},{3,7},{4,0},{5,1},{6,2},{7,3},{8,12},{9,13},{10,... | collective-permute-start | bytes 1179656 | tf_op jit(solution)/shard_map/ppermute | solution.py:35
  57.9 4.8 %collective-permute-start.10 = (bf16[2,128,256]{2,1,0:T(8,128)(2,1)S(1)}, bf16[2,128,256]{2,1,0:T(8,128)(2,1)S(1)}, u32[]{:S(2)}, u32[]{:S(2)}) collective-permute-start(bf16[2,128,256]{2,1,0:T(8,128)(2,1)S(1)} %get-tuple-element.52), channel_id=1, source_target_pairs={{0,1},{1,0},{2,3},{3,2},{4,5},{5,4},{6,7},{7,6},{8,9},{9,8},{10,11... | collective-permute-start | bytes 393224 | tf_op jit(solution)/shard_map/ppermute | solution.py:35
  59.0 5.6 %collective-permute-start.11 = (bf16[2,128,256]{2,1,0:T(8,128)(2,1)S(1)}, bf16[2,128,256]{2,1,0:T(8,128)(2,1)S(1)}, u32[]{:S(2)}, u32[]{:S(2)}) collective-permute-start(bf16[2,128,256]{2,1,0:T(8,128)(2,1)S(1)} %get-tuple-element.53), channel_id=1, source_target_pairs={{0,3},{1,2},{2,1},{3,0},{4,7},{5,6},{6,5},{7,4},{8,11},{9,10},{10,... | collective-permute-start | bytes 393224 | tf_op jit(solution)/shard_map/ppermute | solution.py:35
  64.7 4.4 %collective-permute-start.12 = (bf16[128,256]{1,0:T(8,128)(2,1)S(1)}, bf16[128,256]{1,0:T(8,128)(2,1)S(1)}, u32[]{:S(2)}, u32[]{:S(2)}) collective-permute-start(bf16[128,256]{1,0:T(8,128)(2,1)S(1)} %get-tuple-element.55), channel_id=1, source_target_pairs={{0,3},{1,2},{2,1},{3,0},{4,7},{5,6},{6,5},{7,4},{8,11},{9,10},{10,... | collective-permute-start | bytes 196616 | tf_op jit(solution)/shard_map/ppermute | solution.py:35
  66.7 3.1 %collective-permute-start.13 = (bf16[128,256]{1,0:T(8,128)(2,1)S(1)}, bf16[128,256]{1,0:T(8,128)(2,1)S(1)}, u32[]{:S(2)}, u32[]{:S(2)}) collective-permute-start(bf16[128,256]{1,0:T(8,128)(2,1)S(1)} %get-tuple-element.56), channel_id=1, source_target_pairs={{0,1},{1,0},{2,3},{3,2},{4,5},{5,4},{6,7},{7,6},{8,9},{9,8},{10,11... | collective-permute-start | bytes 196616 | tf_op jit(solution)/shard_map/ppermute | solution.py:35
  70.4 5.0 %collective-permute-start.14 = (bf16[2,32,256]{2,1,0:T(8,128)(2,1)S(1)}, bf16[2,32,256]{2,1,0:T(8,128)(2,1)S(1)}, u32[]{:S(2)}, u32[]{:S(2)}) collective-permute-start(bf16[2,32,256]{2,1,0:T(8,128)(2,1)S(1)} %get-tuple-element.58), channel_id=1, source_target_pairs={{0,64},{8,72},{16,80},{24,88},{32,96},{40,104},{48,112},{56,120},{... | collective-permute-start | bytes 98312 | tf_op jit(solution)/shard_map/ppermute | solution.py:35
  72.2 4.3 %collective-permute-start.15 = (bf16[2,32,256]{2,1,0:T(8,128)(2,1)S(1)}, bf16[2,32,256]{2,1,0:T(8,128)(2,1)S(1)}, u32[]{:S(2)}, u32[]{:S(2)}) collective-permute-start(bf16[2,32,256]{2,1,0:T(8,128)(2,1)S(1)} %get-tuple-element.59), channel_id=1, source_target_pairs={{0,128},{8,136},{16,144},{24,152},{32,160},{40,168},{48,176},{56,1... | collective-permute-start | bytes 98312 | tf_op jit(solution)/shard_map/ppermute | solution.py:35
  74.3 4.0 %collective-permute-start.16 = (bf16[2,32,256]{2,1,0:T(8,128)(2,1)S(1)}, bf16[2,32,256]{2,1,0:T(8,128)(2,1)S(1)}, u32[]{:S(2)}, u32[]{:S(2)}) collective-permute-start(bf16[2,32,256]{2,1,0:T(8,128)(2,1)S(1)} %get-tuple-element.60), channel_id=1, source_target_pairs={{0,192},{8,200},{16,208},{24,216},{32,224},{40,232},{48,240},{56,2... | collective-permute-start | bytes 98312 | tf_op jit(solution)/shard_map/ppermute | solution.py:35
  78.3 8.2 %collective-permute-start.22 = (bf16[2,32,256]{2,1,0:T(8,128)(2,1)S(1)}, bf16[2,32,256]{2,1,0:T(8,128)(2,1)S(1)}, u32[]{:S(2)}, u32[]{:S(2)}) collective-permute-start(bf16[2,32,256]{2,1,0:T(8,128)(2,1)S(1)} %add_convert_fusion.1), channel_id=1, source_target_pairs={{0,48},{8,56},{16,32},{24,40},{32,16},{40,24},{48,0},{56,8},{64,11... | collective-permute-start | bytes 98312 | tf_op jit(solution)/shard_map/ppermute | solution.py:35
  81.2 6.8 %collective-permute-start.21 = (bf16[2,32,256]{2,1,0:T(8,128)(2,1)S(1)}, bf16[2,32,256]{2,1,0:T(8,128)(2,1)S(1)}, u32[]{:S(2)}, u32[]{:S(2)}) collective-permute-start(bf16[2,32,256]{2,1,0:T(8,128)(2,1)S(1)} %add_convert_fusion.1), channel_id=1, source_target_pairs={{0,32},{8,40},{16,48},{24,56},{32,0},{40,8},{48,16},{56,24},{64,96... | collective-permute-start | bytes 98312 | tf_op jit(solution)/shard_map/ppermute | solution.py:35
  83.9 4.6 %collective-permute-start.20 = (bf16[2,32,256]{2,1,0:T(8,128)(2,1)S(1)}, bf16[2,32,256]{2,1,0:T(8,128)(2,1)S(1)}, u32[]{:S(2)}, u32[]{:S(2)}) collective-permute-start(bf16[2,32,256]{2,1,0:T(8,128)(2,1)S(1)} %add_convert_fusion.1), channel_id=1, source_target_pairs={{0,16},{8,24},{16,0},{24,8},{32,48},{40,56},{48,32},{56,40},{64,80... | collective-permute-start | bytes 98312 | tf_op jit(solution)/shard_map/ppermute | solution.py:35
  84.1 4.5 %collective-permute-start.17 = (bf16[3,2,32,256]{3,2,1,0:T(8,128)(2,1)S(1)}, bf16[3,2,32,256]{3,2,1,0:T(8,128)(2,1)S(1)}, u32[]{:S(2)}, u32[]{:S(2)}) collective-permute-start(bf16[3,2,32,256]{3,2,1,0:T(8,128)(2,1)S(1)} %get-tuple-element.67), channel_id=1, source_target_pairs={{0,1},{1,0},{2,3},{3,2},{4,5},{5,4},{6,7},{7,6},{8,9},{9,8},{10,11... | collective-permute-start | bytes 294920 | tf_op jit(solution)/shard_map/ppermute | solution.py:35
  84.4 5.2 %collective-permute-start.18 = (bf16[3,2,32,256]{3,2,1,0:T(8,128)(2,1)S(1)}, bf16[3,2,32,256]{3,2,1,0:T(8,128)(2,1)S(1)}, u32[]{:S(2)}, u32[]{:S(2)}) collective-permute-start(bf16[3,2,32,256]{3,2,1,0:T(8,128)(2,1)S(1)} %get-tuple-element.68), channel_id=1, source_target_pairs={{0,2},{1,3},{2,0},{3,1},{4,6},{5,7},{6,4},{7,5},{8,10},{9,11},{10,... | collective-permute-start | bytes 294920 | tf_op jit(solution)/shard_map/ppermute | solution.py:35
  86.5 4.7 %collective-permute-start.19 = (bf16[3,2,32,256]{3,2,1,0:T(8,128)(2,1)S(1)}, bf16[3,2,32,256]{3,2,1,0:T(8,128)(2,1)S(1)}, u32[]{:S(2)}, u32[]{:S(2)}) collective-permute-start(bf16[3,2,32,256]{3,2,1,0:T(8,128)(2,1)S(1)} %get-tuple-element.69), channel_id=1, source_target_pairs={{0,3},{1,2},{2,1},{3,0},{4,7},{5,6},{6,5},{7,4},{8,11},{9,10},{10,... | collective-permute-start | bytes 294920 | tf_op jit(solution)/shard_map/ppermute | solution.py:35
  92.1 19.2 %collective-permute-start.23 = (bf16[3,2,32,512]{3,2,1,0:T(8,128)(2,1)S(1)}, bf16[3,2,32,512]{3,2,1,0:T(8,128)(2,1)S(1)}, u32[]{:S(2)}, u32[]{:S(2)}) collective-permute-start(bf16[3,2,32,512]{3,2,1,0:T(8,128)(2,1)S(1)} %get-tuple-element.76), channel_id=1, source_target_pairs={{0,8},{8,16},{16,24},{24,32},{32,40},{40,48},{48,56},{56,64},{64,7... | collective-permute-start | bytes 589832 | tf_op jit(solution)/shard_map/ppermute | solution.py:40
  100.9 4.0 %collective-permute-start.26 = (bf16[2,32,256]{2,1,0:T(8,128)(2,1)S(1)}, bf16[2,32,256]{2,1,0:T(8,128)(2,1)S(1)}, u32[]{:S(2)}, u32[]{:S(2)}) collective-permute-start(bf16[2,32,256]{2,1,0:T(8,128)(2,1)S(1)} %add_convert_fusion.part0), channel_id=1, source_target_pairs={{0,192},{8,200},{16,208},{24,216},{32,224},{40,232},{48,240},{56,2... | collective-permute-start | bytes 98312 | tf_op jit(solution)/shard_map/ppermute | solution.py:35
  101.3 6.6 %collective-permute-start.25 = (bf16[2,32,256]{2,1,0:T(8,128)(2,1)S(1)}, bf16[2,32,256]{2,1,0:T(8,128)(2,1)S(1)}, u32[]{:S(2)}, u32[]{:S(2)}) collective-permute-start(bf16[2,32,256]{2,1,0:T(8,128)(2,1)S(1)} %add_convert_fusion.part0), channel_id=1, source_target_pairs={{0,128},{8,136},{16,144},{24,152},{32,160},{40,168},{48,176},{56,1... | collective-permute-start | bytes 98312 | tf_op jit(solution)/shard_map/ppermute | solution.py:35
  101.4 6.5 %collective-permute-start.24 = (bf16[2,32,256]{2,1,0:T(8,128)(2,1)S(1)}, bf16[2,32,256]{2,1,0:T(8,128)(2,1)S(1)}, u32[]{:S(2)}, u32[]{:S(2)}) collective-permute-start(bf16[2,32,256]{2,1,0:T(8,128)(2,1)S(1)} %add_convert_fusion.part0), channel_id=1, source_target_pairs={{0,64},{8,72},{16,80},{24,88},{32,96},{40,104},{48,112},{56,120},{... | collective-permute-start | bytes 98312 | tf_op jit(solution)/shard_map/ppermute | solution.py:35
  108.4 1.4 %collective-permute-start.27 = (bf16[2,128,256]{2,1,0:T(8,128)(2,1)S(1)}, bf16[2,128,256]{2,1,0:T(8,128)(2,1)S(1)}, u32[]{:S(2)}, u32[]{:S(2)}) collective-permute-start(bf16[2,128,256]{2,1,0:T(8,128)(2,1)S(1)} %shard_map.76.own), channel_id=1, source_target_pairs={{0,8},{8,0},{16,24},{24,16},{32,40},{40,32},{48,56},{56,48},{64,72... | collective-permute-start | bytes 393224 | tf_op jit(solution)/shard_map/ppermute | solution.py:35

commit v3 on v2

--- a/solution.py
+++ b/solution.py
@@ -1,3 +1,4 @@
+import functools
 import math
 
 import jax
@@ -122,91 +123,88 @@
     transform_all(field, mid, slots, *back, store)
 
 
-def choose_kernel(which, above, strip, out):
+def choose_kernel(which, above, strip, *outs):
     cols = lax.broadcasted_iota(jnp.int32, (SIDE, SIDE), 1)
     on_left = cols >= above[which[1], 1]
     part = which[0] >> 2
-    for layer in range(DEPTH):
+    for layer, out in enumerate(outs):
         value = strip[layer, part].astype(F32)
-        out[layer] = jnp.where(on_left, value[:, :SIDE], value[:, SIDE:]).astype(BF)
-
-
-def forward_kernel(which, strip_hbm, *refs):
-    mine, other, *probes_hbm = refs[:7]
-    table, window, wave0, wave1, wave2, far, total, total_sent, *refs = refs[7:]
-    row_t, row_tt, col_t, col_tt, kernel, field, mid, own, probes, sem = refs
-    copies = [pltpu.make_async_copy(strip_hbm, own, sem.at[0])]
-    places = (probes.at[0], probes.at[1], probes.at[2, 0], probes.at[2, 1], probes.at[3])
-    for index, (source, target) in enumerate(zip(probes_hbm, places)):
-        copies.append(pltpu.make_async_copy(source, target, sem.at[index + 1]))
-    for copy in copies:
-        copy.start()
-    mode, place = which[0], which[1]
-    row, col = row_of(which, place), column_of(which, place)
+        out[...] = jnp.where(on_left, value[:, :SIDE], value[:, SIDE:]).astype(BF)
+
+
+def prepare_kernel(which, table, strip, row_t, row_tt, col_t, col_tt, kernel, picked):
     make_tables(which, table, row_t, row_tt, col_t, col_tt, kernel)
-    there = to_residues(row)
-    back = from_residues(col)
-    for copy in copies:
-        copy.wait()
-    for slot in range(SLOTS):
-        for part in range(2):
-            moved = dot(there, probes[slot, part]).astype(BF)
-            wave0[slot, part] = dot(moved, back).astype(BF)
-    rows, cols = iotas()
-    on_left = cols >= col
-    on_strip = rows >= row
+    cols = lax.broadcasted_iota(jnp.int32, (SIDE, SIDE), 1)
+    on_left = cols >= column_of(which, which[1])
     for layer in range(DEPTH):
         for part in range(2):
-            strip = own[layer, part].astype(F32)
-            picked = jnp.where(on_left, strip[:, :SIDE], strip[:, SIDE:])
-            have = (mode >> 2) == part
-            below = jnp.where(have, mine[layer].astype(F32), other[layer].astype(F32))
-            window[layer, part] = jnp.where(on_strip, picked, below).astype(BF)
+            value = strip[layer, part].astype(F32)
+            picked[layer, part] = jnp.where(on_left, value[:, :SIDE], value[:, SIDE:]).astype(BF)
+
+
+def forward_kernel(layer, which, picked, mine, other, *refs):
+    row_t, row_tt, col_t, col_tt, kernel, *refs = refs
+    rows, cols = iotas()
+    on_strip = rows >= row_of(which, which[1])
+    if layer == 0:
+        probe, one, two_real, two_imag, three, window, wave, *outs, field, mid = refs
+        there = to_residues(row_of(which, which[1]))
+        back = from_residues(column_of(which, which[1]))
+        sources = (probe[0], probe[1], one[0], one[1], two_real[...], two_imag[...])
+        for index, source in enumerate(sources + (three[0], three[1])):
+            moved = dot(there, source).astype(BF)
+            wave[index // 2, index % 2] = dot(moved, back).astype(BF)
+    else:
+        wave, window, *outs, field, mid = refs
+    for part in range(2):
+        have = (which[0] >> 2) == part
+        below = jnp.where(have, mine[...].astype(F32), other[...].astype(F32))
+        above = picked[layer, part].astype(F32)
+        window[part] = jnp.where(on_strip, above, below).astype(BF)
     forth = (row_tt, col_t)
     back = (row_t, col_tt)
-    waves = (wave0, wave1, wave2)
-
-    def store_far(slot, real, imag):
-        far[slot, 0] = real
-        far[slot, 1] = imag
-        power = real * real + imag * imag
-        total[...] = power if slot == 0 else total[...] + power
-
-    for layer in range(DEPTH):
-        for slot in range(SLOTS):
-            obj_real = window[layer, 0].astype(F32)
-            obj_imag = window[layer, 1].astype(F32)
-            real = waves[layer][slot, 0].astype(F32)
-            imag = waves[layer][slot, 1].astype(F32)
-            fill(field, slot, real * obj_real - imag * obj_imag, real * obj_imag + imag * obj_real)
-        if layer + 1 < DEPTH:
-
-            def store(slot, real, imag, wave=waves[layer + 1]):
-                wave[slot, 0] = real.astype(BF)
-                wave[slot, 1] = imag.astype(BF)
-
-            propagate_all(field, mid, SLOTS, forth, back, kernel, 1.0, store)
-        else:
-            transform_all(field, mid, SLOTS, *forth, store_far)
-    total_sent[...] = total[...].astype(BF)
+    for slot in range(SLOTS):
+        obj_real = window[0].astype(F32)
+        obj_imag = window[1].astype(F32)
+        real = wave[slot, 0].astype(F32)
+        imag = wave[slot, 1].astype(F32)
+        fill(field, slot, real * obj_real - imag * obj_imag, real * obj_imag + imag * obj_real)
+    if layer + 1 < DEPTH:
+        (wave_out,) = outs
+
+        def store(slot, real, imag):
+            wave_out[slot, 0] = real.astype(BF)
+            wave_out[slot, 1] = imag.astype(BF)
+
+        propagate_all(field, mid, SLOTS, forth, back, kernel, 1.0, store)
+    else:
+        far, total, total_sent = outs
+
+        def store_far(slot, real, imag):
+            far[slot, 0] = real
+            far[slot, 1] = imag
+            power = real * real + imag * imag
+            total[...] = power if slot == 0 else total[...] + power
+
+        transform_all(field, mid, SLOTS, *forth, store_far)
+        total_sent[...] = total[...].astype(BF)
 
 
 def backward_kernel(
-    which, window, wave0, wave1, wave2, far, total, total_got, measured_hbm,
-    table,
-    grad_keep, grad_send, keep_out, send_out,
-    row_t, row_tt, col_t, col_tt, kernel, field, mid, residual, grads, sums, backs, measured, sem,
+    which, window0, window1, window2, wave0, wave1, wave2, far, total, total_got,
+    row_t, row_tt, col_t, col_tt, kernel, measured_hbm,
+    grad_keep, grad_send, keep_out, send_out, field, mid, residual, grads, sums, backs, measured, sem,
 ):
     place = which[1]
     copy = pltpu.make_async_copy(measured_hbm.at[place], measured, sem)
     copy.start()
     row, col = row_of(which, place), column_of(which, place)
-    make_tables(which, table, row_t, row_tt, col_t, col_tt, kernel)
     copy.wait()
     residual[...] = total[...] + total_got[...].astype(F32) - measured[...]
     forth = (row_tt, col_t)
     back = (row_t, col_tt)
     waves = (wave0, wave1, wave2)
+    windows = (window0, window1, window2)
 
     def store(slot, real, imag):
         backs[slot, 0] = real.astype(BF)
@@ -232,8 +230,8 @@
             else:
                 sums[layer, 0] = grad_real.astype(BF)
                 sums[layer, 1] = grad_imag.astype(BF)
-            obj_real = window[layer, 0].astype(F32)
-            obj_imag = window[layer, 1].astype(F32)
+            obj_real = windows[layer][0].astype(F32)
+            obj_imag = windows[layer][1].astype(F32)
             next_real = obj_real * gin_real + obj_imag * gin_imag
             next_imag = obj_real * gin_imag - obj_imag * gin_real
             fill(field, slot, next_real, next_imag)
@@ -360,30 +358,44 @@
     wide = (2 * SIDE, 2 * SIDE)
     table = jnp.asarray(constants())
 
-    above = shift(positions, "tile", 1)
-    (chosen,) = call(choose_kernel, [((DEPTH,) + square, BF)], (which, above, object_slices), 2)
-    mine = shift(chosen, "tile", -1)
-    one, three = (swap(probe_modes[0], "mode", step) for step in (1, 3))
-    two = [swap(three[0], "mode", 1), swap(one[1], "mode", 3)]
-    other = swap(mine, "mode", 4)
-
     slots = (SLOTS, 2) + square
     layers = (DEPTH, 2) + square
-    scratch = [(wide, BF)] * 4 + [((2,) + square, F32)]
-    scratch += [((SLOTS, 2 * SIDE, SIDE), BF), ((SLOTS, SIDE, 2 * SIDE), BF)]
-    outs = [(layers, BF)] + [(slots, BF)] * 3 + [(slots, F32), (square, F32), (square, BF)]
-    window, wave0, wave1, wave2, far, total, total_sent = pl.pallas_call(
-        forward_kernel,
-        out_shape=[jax.ShapeDtypeStruct(*out) for out in outs],
-        in_specs=[SMEM, HBM] + [VMEM] * 2 + [HBM] * 5 + [VMEM],
-        out_specs=[VMEM] * 7,
-        scratch_shapes=[
-            pltpu.VMEM(*shape)
-            for shape in scratch + [((DEPTH, 2, SIDE, 2 * SIDE), BF), (slots, BF)]
-        ]
-        + [pltpu.SemaphoreType.DMA((6,))],
-        compiler_params=PARAMS,
-    )(which, object_slices, mine, other, probe_modes[0], one, *two, three, table)
+    pair_of = ((2,) + square, BF)
+    above = shift(positions, "tile", 1)
+    *tables, picked = call(
+        prepare_kernel,
+        [(wide, BF)] * 4 + [((2,) + square, F32), (layers, BF)],
+        (which, table, object_slices),
+        1,
+    )
+    above, probe = lax.optimization_barrier((above, probe_modes[0]))
+    chosen = call(choose_kernel, [(square, BF)] * DEPTH, (which, above, object_slices), 2)
+    mine = [shift(part, "tile", -1) for part in chosen]
+    one, three = (swap(probe, "mode", step) for step in (1, 3))
+    mine[0], one, three, picked = lax.optimization_barrier((mine[0], one, three, picked))
+    two = [swap(three[0], "mode", 1), swap(one[1], "mode", 3)]
+    other = [swap(part, "mode", 4) for part in mine]
+
+    scratch = [((SLOTS, 2 * SIDE, SIDE), BF), ((SLOTS, SIDE, 2 * SIDE), BF)]
+    windows = []
+    waves = []
+    for layer in range(DEPTH):
+        common = (which, picked, mine[layer], other[layer], *tables)
+        if layer == 0:
+            given = (probe_modes[0], one, *two, three)
+            outs = [pair_of, (slots, BF), (slots, BF)]
+        elif layer + 1 < DEPTH:
+            given = (waves[layer],)
+            outs = [pair_of, (slots, BF)]
+        else:
+            given = (waves[layer],)
+            outs = [pair_of, (slots, F32), (square, F32), (square, BF)]
+        kernel = functools.partial(forward_kernel, layer)
+        window, *results = call(kernel, outs, common + given, 1, scratch)
+        windows.append(window)
+        if layer + 1 < DEPTH:
+            waves += results
+    far, total, total_sent = results
     total_got = swap(total_sent, "mode", 4)
     piece = ((SLOTS, 2, half, SIDE), BF)
     outs = [((DEPTH, 2, half, SIDE), BF)] * 2 + [piece, piece]
@@ -391,11 +403,11 @@
     grad_keep, grad_send, keep, send = pl.pallas_call(
         backward_kernel,
         out_shape=[jax.ShapeDtypeStruct(*out) for out in outs],
-        in_specs=[SMEM] + [VMEM] * 7 + [HBM, VMEM],
+        in_specs=[SMEM] + [VMEM] * 14 + [HBM],
         out_specs=[VMEM] * 4,
         scratch_shapes=[pltpu.VMEM(*shape) for shape in scratch] + [pltpu.SemaphoreType.DMA],
         compiler_params=PARAMS,
-    )(which, window, wave0, wave1, wave2, far, total, total_got, measured, table)
+    )(which, *windows, *waves, far, total, total_got, *tables, measured)
 
     grad_got = swap(grad_send, "mode", 4)
 
@@ -409,6 +421,12 @@
         (own, swap(sent_one, "mode", 1), swap(sent_three, "mode", 3)),
         0,
     )
+    grad_got, held = lax.optimization_barrier((grad_got, held))
+    shape = (DEPTH, 2, band, SIDE)
+    bands = call(
+        pair_kernel, [(shape, F32)] + [(shape, BF)] * 3, (which, grad_keep, grad_got), 1
+    )
+    bands, held = lax.optimization_barrier((bands, held))
     quarters = call(
         quarter_kernel,
         [((2, half // 4, SIDE), BF)] * 4,
@@ -417,13 +435,8 @@
         [pair],
     )
     parts = [quarters[0]] + [swap(quarters[step], "tile", step << 3) for step in range(1, 4)]
-    grad_got, quarters = lax.optimization_barrier((grad_got, quarters))
-    shape = (DEPTH, 2, band, SIDE)
-    bands = call(
-        pair_kernel, [(shape, F32)] + [(shape, BF)] * 3, (which, grad_keep, grad_got), 1
-    )
+    bands = [bands[0]] + [swap(bands[step], "mode", step) for step in range(1, 4)]
     bands, parts = lax.optimization_barrier((bands, parts))
-    bands = [bands[0]] + [swap(bands[step], "mode", step) for step in range(1, 4)]
     part = ((parts[0].astype(F32) + parts[1]) + (parts[2].astype(F32) + parts[3])).astype(BF)
     parts = [part] + [swap(part, "tile", step << 1) for step in range(1, 4)]
     part = ((parts[0].astype(F32) + parts[1]) + (parts[2].astype(F32) + parts[3])).astype(BF)

time: 112 us -> 108 us (0.964)
  waiting for transfers between devices: 34.9 us -> 27.8 us
  Pallas kernels: 22.4 us -> 25 us
    pallas_call x8 -> x12, Pallas kernels: 4.87 us -> 15.9 us  [call(): pl.pallas_call(kernel, out_shape=[jax.ShapeDtypeStruct(shape, dtype) for...]
    pallas_call x1 -> x0, Pallas kernels: 8.58 us -> none  [on_device(): pl.pallas_call(forward_kernel, out_shape=[jax.ShapeDtypeStruct(*out) for...]
    ppermute x25 -> x27, waiting for transfers between devices: 29.5 us -> 23.4 us  [swap(): return lax.ppermute(block, axis, route)]
    ppermute x25 -> x27, starting transfers between devices: 31.9 us -> 30.7 us  [swap(): return lax.ppermute(block, axis, route)]
    ppermute x3 -> x5, waiting for transfers between devices: 5.35 us -> 4.36 us  [shift(): lax.ppermute(block, axis, [(i, (i + distance) % size) for i in range(size)])]
    ppermute x3 -> x5, starting transfers between devices: 18.8 us -> 19.7 us  [shift(): lax.ppermute(block, axis, [(i, (i + distance) % size) for i in range(size)])]
  transfers between devices with their start and end apart: 28 -> 32, of which waited for: 21 -> 17; matrix products, arithmetic and copies ran while one was open for 0% -> 0% of each run, Pallas kernels for 3% -> 13%
where the time goes in v3:
time: 108 us
  starting transfers between devices  50.4 us (47%)
  waiting for transfers between devices  27.8 us (26%)
  Pallas kernels  25 us (23%)
  local copies, waits for them, and re-layouts  3.33 us (3%)
    ppermute x27, starting transfers between devices, swap(): return lax.ppermute(block, axis, route)  30.7 us
    ppermute x27, waiting for transfers between devices, swap(): return lax.ppermute(block, axis, route)  23.4 us
    ppermute x5, starting transfers between devices, shift(): lax.ppermute(block, axis, [(i, (i + distance) % size) for i in range(size)])  19.7 us
    pallas_call x12, Pallas kernels, call(): pl.pallas_call(kernel, out_shape=[jax.ShapeDtypeStruct(shape, dtype) for...  15.9 us
    pallas_call x1, Pallas kernels, on_device(): pl.pallas_call(backward_kernel, out_shape=[jax.ShapeDtypeStruct(*out) for...  9.12 us
    ppermute x5, waiting for transfers between devices, shift(): lax.ppermute(block, axis, [(i, (i + distance) % size) for i in range(size)])  4.36 us
    unnamed x11, local copies, waits for them, and re-layouts  3.14 us
  transfers between devices with their start and end apart: 32, of which 17 were waited for; matrix products, arithmetic and copies ran while one was open for 0% of the time, Pallas kernels for 13%

profile of v3, /device:TPU:1, one launch (start us, length us, event | category | flops | bytes accessed | tf_op | source)
XLA Modules:
  0.0 108.1 jit_solution(13259736412519848785)
XLA Ops:
  0.6 0.8 copy.9
  1.4 4.4 %collective-permute-start = (s32[4,2]{1,0:T(4,128)S(1)}, s32[4,2]{1,0:T(4,128)S(1)}, u32[]{:S(2)}, u32[]{:S(2)}) collective-permute-start(s32[4,2]{1,0:T(4,128)S(1)} %copy.9), channel_id=1, source_target_pairs={{0,8},{8,16},{16,24},{24,32},{32,40},{40,48},{48,56},{56,64},{64,7... | collective-permute-start | bytes 104 | tf_op jit(solution)/shard_map/ppermute | solution.py:41
  5.8 0.7 collective-permute-done.above
  6.5 2.7 %collective-permute-start.3 = (bf16[2,256,256]{2,1,0:T(8,128)(2,1)}, bf16[2,256,256]{2,1,0:T(8,128)(2,1)S(1)}, u32[]{:S(2)}, u32[]{:S(2)}) collective-permute-start(bf16[2,256,256]{2,1,0:T(8,128)(2,1)} %bitcast.9), channel_id=1, source_target_pairs={{0,3},{1,2},{2,1},{3,0},{4,7},{5,6},{6,5},{7,4},{8,11},{9,10},{10,... | collective-permute-start | bytes 786440 | tf_op jit(solution)/shard_map/ppermute | solution.py:36
  9.2 0.0 collective-permute-start.2
  9.3 0.1 reshape.7
  9.3 0.1 concatenate.3.which
  9.4 1.4 %copy-done = bf16[3,2,256,512]{3,2,1,0:T(8,128)(2,1)S(1)} copy-done((bf16[3,2,256,512]{3,2,1,0:T(8,128)(2,1)S(1)}, bf16[3,2,256,512]{3,2,1,0:T(8,128)(2,1)}, u32[]{:S(2)}) %copy-start) | copy-done | bytes 1572888
  10.8 0.7 shard_map.68
  11.5 6.1 %collective-permute-start.1 = (bf16[256,256]{1,0:T(8,128)(2,1)S(1)}, bf16[256,256]{1,0:T(8,128)(2,1)S(1)}, u32[]{:S(2)}, u32[]{:S(2)}) collective-permute-start(bf16[256,256]{1,0:T(8,128)(2,1)S(1)} %get-tuple-element.64), channel_id=1, source_target_pairs={{0,248},{8,0},{16,8},{24,16},{32,24},{40,32},{48,40},{56,48},{64,5... | collective-permute-start | bytes 393224 | tf_op jit(solution)/shard_map/ppermute | solution.py:41
  17.6 0.9 copy-done.4
  18.5 1.3 %shard_map.69 = (bf16[512,512]{1,0:T(8,128)(2,1)S(1)}, bf16[512,512]{1,0:T(8,128)(2,1)S(1)}, bf16[512,512]{1,0:T(8,128)(2,1)S(1)}, bf16[512,512]{1,0:T(8,128)(2,...) custom-call(s32[12]{0:T(128)S(1)} %concatenate.3.which, bf16[256,512]{1,0:T(8,128)(2,1)S(1)} %copy-done.4, ...), custom_call_target="tpu_custom_call" | custom-call | tf_op jit(solution)/shard_map/pallas_call | solution.py:339
  19.8 0.7 collective-permute-start.7
  20.5 2.7 %collective-permute-start.9 = (bf16[256,256]{1,0:T(8,128)(2,1)S(1)}, bf16[256,256]{1,0:T(8,128)(2,1)S(1)}, u32[]{:S(2)}, u32[]{:S(2)}) collective-permute-start(bf16[256,256]{1,0:T(8,128)(2,1)S(1)} %get-tuple-element.80), channel_id=1, source_target_pairs={{0,248},{8,0},{16,8},{24,16},{32,24},{40,32},{48,40},{56,48},{64,5... | collective-permute-start | bytes 393224 | tf_op jit(solution)/shard_map/ppermute | solution.py:41
  23.2 1.7 %collective-permute-start.5 = (bf16[256,256]{1,0:T(8,128)(2,1)S(1)}, bf16[256,256]{1,0:T(8,128)(2,1)S(1)}, u32[]{:S(2)}, u32[]{:S(2)}) collective-permute-start(bf16[256,256]{1,0:T(8,128)(2,1)S(1)} %slice_bitcast_fusion.1), channel_id=1, source_target_pairs={{0,1},{1,0},{2,3},{3,2},{4,5},{5,4},{6,7},{7,6},{8,9},{9,8},{10,11... | collective-permute-start | bytes 393224 | tf_op jit(solution)/shard_map/ppermute | solution.py:36
  25.0 0.1 collective-permute-start.6
  25.1 0.8 collective-permute-start.4
  25.9 1.0 collective-permute-done.7.mine
  26.9 2.6 %collective-permute-done.9.mine = bf16[256,256]{1,0:T(8,128)(2,1)S(1)} collective-permute-done((bf16[256,256]{1,0:T(8,128)(2,1)S(1)}, bf16[256,256]{1,0:T(8,128)(2,1)S(1)}, u32[]{:S(2)}, u32[]{:S(2)}) %collective-permute-start.9) | collective-permute-done | bytes 131104 | tf_op jit(solution)/shard_map/ppermute | solution.py:41
  29.5 0.0 collective-permute-start.10
  29.5 0.6 collective-permute-done.6.refs_8_
  30.1 1.8 %collective-permute-done.4.other = bf16[256,256]{1,0:T(8,128)(2,1)S(1)} collective-permute-done((bf16[256,256]{1,0:T(8,128)(2,1)S(1)}, bf16[256,256]{1,0:T(8,128)(2,1)S(1)}, u32[]{:S(2)}, u32[]{:S(2)}) %collective-permute-start.4) | collective-permute-done | bytes 131104 | tf_op jit(solution)/shard_map/ppermute | solution.py:36
  31.9 4.0 %shard_map.70 = (bf16[2,256,256]{2,1,0:T(8,128)(2,1)S(1)}, bf16[4,2,256,256]{3,2,1,0:T(8,128)(2,1)S(1)}, bf16[4,2,256,256]{3,2,1,0:T(8,128)(2,1)S(1)}) custom-call(s32[12]{0:T(128)S(1)} %concatenate.3.which, bf16[3,2,256,256]{3,2,1,0:T(8,128)(2,1)S(1)} %get-tuple-element.67.picked, bf16[256,256]{1,0:T(8,128)(2,1)S(1)} %collective-permute-done.1.mine, ...), custom_call_target="tpu_custom_call" | custom-call | tf_op jit(solution)/shard_map/pallas_call | solution.py:339
  36.0 3.5 %shard_map.71 = (bf16[2,256,256]{2,1,0:T(8,128)(2,1)S(1)}, bf16[4,2,256,256]{3,2,1,0:T(8,128)(2,1)S(1)}) custom-call(s32[12]{0:T(128)S(1)} %concatenate.3.which, bf16[3,2,256,256]{3,2,1,0:T(8,128)(2,1)S(1)} %get-tuple-element.67.picked, bf16[256,256]{1,0:T(8,128)(2,1)S(1)} %collective-permute-done.7.mine, bf16[256,256]{1,0:T(8,128)(2,1)S(1)} %collective-permute-done.8.other, ...), custom_call_target="tpu_custom_call" | custom-call | tf_op jit(solution)/shard_map/pallas_call | solution.py:339
  39.5 0.0 copy-start.2
  39.5 2.2 %shard_map.72 = (bf16[2,256,256]{2,1,0:T(8,128)(2,1)S(1)}, f32[4,2,256,256]{3,2,1,0:T(8,128)S(1)}, f32[256,256]{1,0:T(8,128)S(1)}, bf16[256,256]{1,0:T(8,128)(2,1)S(1)}) custom-call(s32[12]{0:T(128)S(1)} %concatenate.3.which, bf16[3,2,256,256]{3,2,1,0:T(8,128)(2,1)S(1)} %get-tuple-element.67.picked, bf16[256,256]{1,0:T(8,128)(2,1)S(1)} %collective-permute-done.9.mine, ...), custom_call_target="tpu_custom_call" | custom-call | tf_op jit(solution)/shard_map/pallas_call | solution.py:339
  41.7 0.3 collective-permute-start.11
  42.0 3.8 %collective-permute-done.11.total_got = bf16[256,256]{1,0:T(8,128)(2,1)S(1)} collective-permute-done((bf16[256,256]{1,0:T(8,128)(2,1)S(1)}, bf16[256,256]{1,0:T(8,128)(2,1)S(1)}, u32[]{:S(2)}, u32[]{:S(2)}) %collective-permute-start.11) | collective-permute-done | bytes 131104 | tf_op jit(solution)/shard_map/ppermute | solution.py:36
  45.8 9.1 %shard_map.73 = (bf16[3,2,128,256]{3,2,1,0:T(8,128)(2,1)S(1)}, bf16[3,2,128,256]{3,2,1,0:T(8,128)(2,1)S(1)}, bf16[4,2,128,256]{3,2,1,0:T(8,128)(2,1)S(1)}, bf16[4,2,128,256]{3,2,1,0:T(8,128)(2,1)S(1)}) custom-call(s32[12]{0:T(128)S(1)} %concatenate.3.which, bf16[2,256,256]{2,1,0:T(8,128)(2,1)S(1)} %get-tuple-element.76.window0, ...), custom_call_target="tpu_custom_call" | custom-call | tf_op jit(solution)/shard_map/pallas_call | solution.py:403
  55.0 3.6 %collective-permute-start.13 = (bf16[4,2,128,256]{3,2,1,0:T(8,128)(2,1)S(1)}, bf16[4,2,128,256]{3,2,1,0:T(8,128)(2,1)S(1)}, u32[]{:S(2)}, u32[]{:S(2)}) collective-permute-start(bf16[4,2,128,256]{3,2,1,0:T(8,128)(2,1)S(1)} %get-tuple-element.90), channel_id=1, source_target_pairs={{0,8},{8,0},{16,24},{24,16},{32,40},{40,32},{48,56},{56,48},{64,72... | collective-permute-start | bytes 1572872 | tf_op jit(solution)/shard_map/ppermute | solution.py:36
  58.5 1.5 %collective-permute-done.13.got = bf16[4,2,128,256]{3,2,1,0:T(8,128)(2,1)S(1)} collective-permute-done((bf16[4,2,128,256]{3,2,1,0:T(8,128)(2,1)S(1)}, bf16[4,2,128,256]{3,2,1,0:T(8,128)(2,1)S(1)}, u32[]{:S(2)}, u32[]{:S(2)}) %collective-permute-start.13) | collective-permute-done | bytes 524320 | tf_op jit(solution)/shard_map/ppermute | solution.py:36
  60.0 0.1 shard_map.74
  60.2 2.6 %collective-permute-start.14 = (bf16[2,128,256]{2,1,0:T(8,128)(2,1)S(1)}, bf16[2,128,256]{2,1,0:T(8,128)(2,1)S(1)}, u32[]{:S(2)}, u32[]{:S(2)}) collective-permute-start(bf16[2,128,256]{2,1,0:T(8,128)(2,1)S(1)} %get-tuple-element.92), channel_id=1, source_target_pairs={{0,1},{1,0},{2,3},{3,2},{4,5},{5,4},{6,7},{7,6},{8,9},{9,8},{10,11... | collective-permute-start | bytes 393224 | tf_op jit(solution)/shard_map/ppermute | solution.py:36
  62.8 3.6 %collective-permute-done.14.got_one = bf16[2,128,256]{2,1,0:T(8,128)(2,1)S(1)} collective-permute-done((bf16[2,128,256]{2,1,0:T(8,128)(2,1)S(1)}, bf16[2,128,256]{2,1,0:T(8,128)(2,1)S(1)}, u32[]{:S(2)}, u32[]{:S(2)}) %collective-permute-start.14) | collective-permute-done | bytes 131104 | tf_op jit(solution)/shard_map/ppermute | solution.py:36
  66.4 2.0 %collective-permute-done.15.got_three = bf16[2,128,256]{2,1,0:T(8,128)(2,1)S(1)} collective-permute-done((bf16[2,128,256]{2,1,0:T(8,128)(2,1)S(1)}, bf16[2,128,256]{2,1,0:T(8,128)(2,1)S(1)}, u32[]{:S(2)}, u32[]{:S(2)}) %collective-permute-start.15) | collective-permute-done | bytes 131104 | tf_op jit(solution)/shard_map/ppermute | solution.py:36
  68.4 0.1 shard_map.75
  68.5 0.4 collective-permute-start.19
  68.9 0.3 collective-permute-done.12.got
  69.2 0.6 shard_map.76
  69.8 2.6 %collective-permute-start.16 = (bf16[3,2,32,256]{3,2,1,0:T(8,128)(2,1)S(1)}, bf16[3,2,32,256]{3,2,1,0:T(8,128)(2,1)S(1)}, u32[]{:S(2)}, u32[]{:S(2)}) collective-permute-start(bf16[3,2,32,256]{3,2,1,0:T(8,128)(2,1)S(1)} %get-tuple-element.102), channel_id=1, source_target_pairs={{0,1},{1,0},{2,3},{3,2},{4,5},{5,4},{6,7},{7,6},{8,9},{9,8},{10,11... | collective-permute-start | bytes 294920 | tf_op jit(solution)/shard_map/ppermute | solution.py:36
  72.5 1.0 collective-permute-start.17
  73.5 1.7 %collective-permute-start.18 = (bf16[3,2,32,256]{3,2,1,0:T(8,128)(2,1)S(1)}, bf16[3,2,32,256]{3,2,1,0:T(8,128)(2,1)S(1)}, u32[]{:S(2)}, u32[]{:S(2)}) collective-permute-start(bf16[3,2,32,256]{3,2,1,0:T(8,128)(2,1)S(1)} %get-tuple-element.104), channel_id=1, source_target_pairs={{0,3},{1,2},{2,1},{3,0},{4,7},{5,6},{6,5},{7,4},{8,11},{9,10},{10,... | collective-permute-start | bytes 294920 | tf_op jit(solution)/shard_map/ppermute | solution.py:36
  75.2 0.6 shard_map.77
  75.8 0.1 collective-permute-start.21
  75.9 1.5 %collective-permute-start.22 = (bf16[2,32,256]{2,1,0:T(8,128)(2,1)S(1)}, bf16[2,32,256]{2,1,0:T(8,128)(2,1)S(1)}, u32[]{:S(2)}, u32[]{:S(2)}) collective-permute-start(bf16[2,32,256]{2,1,0:T(8,128)(2,1)S(1)} %get-tuple-element.110), channel_id=1, source_target_pairs={{0,128},{8,136},{16,144},{24,152},{32,160},{40,168},{48,176},{56,1... | collective-permute-start | bytes 98312 | tf_op jit(solution)/shard_map/ppermute | solution.py:36
  77.5 1.5 %collective-permute-done.21 = bf16[2,32,256]{2,1,0:T(8,128)(2,1)S(1)} collective-permute-done((bf16[2,32,256]{2,1,0:T(8,128)(2,1)S(1)}, bf16[2,32,256]{2,1,0:T(8,128)(2,1)S(1)}, u32[]{:S(2)}, u32[]{:S(2)}) %collective-permute-start.21) | collective-permute-done | bytes 32800 | tf_op jit(solution)/shard_map/ppermute | solution.py:36
  79.0 0.8 collective-permute-start.23
  79.8 0.5 collective-permute-done.22
  80.3 2.7 %collective-permute-done.23 = bf16[2,32,256]{2,1,0:T(8,128)(2,1)S(1)} collective-permute-done((bf16[2,32,256]{2,1,0:T(8,128)(2,1)S(1)}, bf16[2,32,256]{2,1,0:T(8,128)(2,1)S(1)}, u32[]{:S(2)}, u32[]{:S(2)}) %collective-permute-start.23) | collective-permute-done | bytes 32800 | tf_op jit(solution)/shard_map/ppermute | solution.py:36
  83.0 2.0 %collective-permute-start.26 = (bf16[2,32,256]{2,1,0:T(8,128)(2,1)S(1)}, bf16[2,32,256]{2,1,0:T(8,128)(2,1)S(1)}, u32[]{:S(2)}, u32[]{:S(2)}) collective-permute-start(bf16[2,32,256]{2,1,0:T(8,128)(2,1)S(1)} %add_convert_fusion.1), channel_id=1, source_target_pairs={{0,48},{8,56},{16,32},{24,40},{32,16},{40,24},{48,0},{56,8},{64,11... | collective-permute-start | bytes 98312 | tf_op jit(solution)/shard_map/ppermute | solution.py:36
  85.0 0.8 collective-permute-start.25
  85.8 2.9 %collective-permute-start.24 = (bf16[2,32,256]{2,1,0:T(8,128)(2,1)S(1)}, bf16[2,32,256]{2,1,0:T(8,128)(2,1)S(1)}, u32[]{:S(2)}, u32[]{:S(2)}) collective-permute-start(bf16[2,32,256]{2,1,0:T(8,128)(2,1)S(1)} %add_convert_fusion.1), channel_id=1, source_target_pairs={{0,16},{8,24},{16,0},{24,8},{32,48},{40,56},{48,32},{56,40},{64,80... | collective-permute-start | bytes 98312 | tf_op jit(solution)/shard_map/ppermute | solution.py:36
  88.7 0.9 shard_map.78
  89.6 2.0 %collective-permute-done.25 = bf16[2,32,256]{2,1,0:T(8,128)(2,1)S(1)} collective-permute-done((bf16[2,32,256]{2,1,0:T(8,128)(2,1)S(1)}, bf16[2,32,256]{2,1,0:T(8,128)(2,1)S(1)}, u32[]{:S(2)}, u32[]{:S(2)}) %collective-permute-start.25) | collective-permute-done | bytes 32800 | tf_op jit(solution)/shard_map/ppermute | solution.py:36
  91.7 5.8 %collective-permute-start.27 = (bf16[3,2,32,512]{3,2,1,0:T(8,128)(2,1)S(1)}, bf16[3,2,32,512]{3,2,1,0:T(8,128)(2,1)S(1)}, u32[]{:S(2)}, u32[]{:S(2)}) collective-permute-start(bf16[3,2,32,512]{3,2,1,0:T(8,128)(2,1)S(1)} %get-tuple-element.122), channel_id=1, source_target_pairs={{0,8},{8,16},{16,24},{24,32},{32,40},{40,48},{48,56},{56,64},{64,7... | collective-permute-start | bytes 589832 | tf_op jit(solution)/shard_map/ppermute | solution.py:41
  97.5 0.7 collective-permute-start.30
  98.3 2.5 %collective-permute-start.28 = (bf16[2,32,256]{2,1,0:T(8,128)(2,1)S(1)}, bf16[2,32,256]{2,1,0:T(8,128)(2,1)S(1)}, u32[]{:S(2)}, u32[]{:S(2)}) collective-permute-start(bf16[2,32,256]{2,1,0:T(8,128)(2,1)S(1)} %add_convert_fusion.part0), channel_id=1, source_target_pairs={{0,64},{8,72},{16,80},{24,88},{32,96},{40,104},{48,112},{56,120},{... | collective-permute-start | bytes 98312 | tf_op jit(solution)/shard_map/ppermute | solution.py:36
  100.8 0.7 collective-permute-done.30.part3
  101.5 1.3 %collective-permute-done.29.part2 = bf16[2,32,256]{2,1,0:T(8,128)(2,1)S(1)} collective-permute-done((bf16[2,32,256]{2,1,0:T(8,128)(2,1)S(1)}, bf16[2,32,256]{2,1,0:T(8,128)(2,1)S(1)}, u32[]{:S(2)}, u32[]{:S(2)}) %collective-permute-start.29) | collective-permute-done | bytes 32800 | tf_op jit(solution)/shard_map/ppermute | solution.py:36
  102.8 0.6 shard_map.79.own
  103.4 1.6 %collective-permute-start.31 = (bf16[2,128,256]{2,1,0:T(8,128)(2,1)S(1)}, bf16[2,128,256]{2,1,0:T(8,128)(2,1)S(1)}, u32[]{:S(2)}, u32[]{:S(2)}) collective-permute-start(bf16[2,128,256]{2,1,0:T(8,128)(2,1)S(1)} %shard_map.79.own), channel_id=1, source_target_pairs={{0,8},{8,0},{16,24},{24,16},{32,40},{40,32},{48,56},{56,48},{64,72... | collective-permute-start | bytes 393224 | tf_op jit(solution)/shard_map/ppermute | solution.py:36
  105.0 1.0 collective-permute-done.31.got
  106.0 1.4 %shard_map.80 = f32[1,2,256,256]{3,2,1,0:T(8,128)} custom-call(s32[12]{0:T(128)S(1)} %concatenate.3.which, bf16[2,128,256]{2,1,0:T(8,128)(2,1)S(1)} %shard_map.79.own, bf16[2,128,256]{2,1,0:T(8,128)(2,1)S(1)} %collective-permute-done.31.got), custom_call_target="tpu_custom_call" | custom-call | tf_op jit(solution)/shard_map/pallas_call | solution.py:339
  107.3 0.8 convert_add_fusion
  (31 shorter events, 0.1 us)
Async XLA Ops:
  1.4 5.1 %collective-permute-start = (s32[4,2]{1,0:T(4,128)S(1)}, s32[4,2]{1,0:T(4,128)S(1)}, u32[]{:S(2)}, u32[]{:S(2)}) collective-permute-start(s32[4,2]{1,0:T(4,128)S(1)} %copy.9), channel_id=1, source_target_pairs={{0,8},{8,16},{16,24},{24,32},{32,40},{40,48},{48,56},{56,64},{64,7... | collective-permute-start | bytes 104 | tf_op jit(solution)/shard_map/ppermute | solution.py:41
  6.5 16.7 %collective-permute-start.3 = (bf16[2,256,256]{2,1,0:T(8,128)(2,1)}, bf16[2,256,256]{2,1,0:T(8,128)(2,1)S(1)}, u32[]{:S(2)}, u32[]{:S(2)}) collective-permute-start(bf16[2,256,256]{2,1,0:T(8,128)(2,1)} %bitcast.9), channel_id=1, source_target_pairs={{0,3},{1,2},{2,1},{3,0},{4,7},{5,6},{6,5},{7,4},{8,11},{9,10},{10,... | collective-permute-start | bytes 786440 | tf_op jit(solution)/shard_map/ppermute | solution.py:36
  9.2 14.0 %collective-permute-start.2 = (bf16[2,256,256]{2,1,0:T(8,128)(2,1)}, bf16[2,256,256]{2,1,0:T(8,128)(2,1)S(1)}, u32[]{:S(2)}, u32[]{:S(2)}) collective-permute-start(bf16[2,256,256]{2,1,0:T(8,128)(2,1)} %bitcast.10), channel_id=1, source_target_pairs={{0,1},{1,0},{2,3},{3,2},{4,5},{5,4},{6,7},{7,6},{8,9},{9,8},{10,11... | collective-permute-start | bytes 786440 | tf_op jit(solution)/shard_map/ppermute | solution.py:36
  9.4 1.4 %copy-start = (bf16[3,2,256,512]{3,2,1,0:T(8,128)(2,1)S(1)}, bf16[3,2,256,512]{3,2,1,0:T(8,128)(2,1)}, u32[]{:S(2)}) copy-start(bf16[3,2,256,512]{3,2,1,0:T(8,128)(2,1)} %strip.3) | copy-start | bytes 4718596
  10.8 6.8 %copy-start.1 = (bf16[3,2,256,512]{3,2,1,0:T(8,128)(2,1)S(1)}, bf16[3,2,256,512]{3,2,1,0:T(8,128)(2,1)}, u32[]{:S(2)}) copy-start(bf16[3,2,256,512]{3,2,1,0:T(8,128)(2,1)} %strip.3) | copy-start | bytes 4718596
  10.8 21.1 %copy-start.3 = (bf16[1,2,256,256]{3,2,1,0:T(8,128)(2,1)S(1)}, bf16[1,2,256,256]{3,2,1,0:T(8,128)(2,1)}, u32[]{:S(2)}) copy-start(bf16[1,2,256,256]{3,2,1,0:T(8,128)(2,1)} %param.6) | copy-start | bytes 786436
  11.5 11.7 %collective-permute-start.1 = (bf16[256,256]{1,0:T(8,128)(2,1)S(1)}, bf16[256,256]{1,0:T(8,128)(2,1)S(1)}, u32[]{:S(2)}, u32[]{:S(2)}) collective-permute-start(bf16[256,256]{1,0:T(8,128)(2,1)S(1)} %get-tuple-element.64), channel_id=1, source_target_pairs={{0,248},{8,0},{16,8},{24,16},{32,24},{40,32},{48,40},{56,48},{64,5... | collective-permute-start | bytes 393224 | tf_op jit(solution)/shard_map/ppermute | solution.py:41
  17.6 1.0 copy-start.4
  19.8 7.1 %collective-permute-start.7 = (bf16[256,256]{1,0:T(8,128)(2,1)S(1)}, bf16[256,256]{1,0:T(8,128)(2,1)S(1)}, u32[]{:S(2)}, u32[]{:S(2)}) collective-permute-start(bf16[256,256]{1,0:T(8,128)(2,1)S(1)} %get-tuple-element.77), channel_id=1, source_target_pairs={{0,248},{8,0},{16,8},{24,16},{32,24},{40,32},{48,40},{56,48},{64,5... | collective-permute-start | bytes 393224 | tf_op jit(solution)/shard_map/ppermute | solution.py:41
  20.5 9.0 %collective-permute-start.9 = (bf16[256,256]{1,0:T(8,128)(2,1)S(1)}, bf16[256,256]{1,0:T(8,128)(2,1)S(1)}, u32[]{:S(2)}, u32[]{:S(2)}) collective-permute-start(bf16[256,256]{1,0:T(8,128)(2,1)S(1)} %get-tuple-element.80), channel_id=1, source_target_pairs={{0,248},{8,0},{16,8},{24,16},{32,24},{40,32},{48,40},{56,48},{64,5... | collective-permute-start | bytes 393224 | tf_op jit(solution)/shard_map/ppermute | solution.py:41
  23.2 6.3 %collective-permute-start.5 = (bf16[256,256]{1,0:T(8,128)(2,1)S(1)}, bf16[256,256]{1,0:T(8,128)(2,1)S(1)}, u32[]{:S(2)}, u32[]{:S(2)}) collective-permute-start(bf16[256,256]{1,0:T(8,128)(2,1)S(1)} %slice_bitcast_fusion.1), channel_id=1, source_target_pairs={{0,1},{1,0},{2,3},{3,2},{4,5},{5,4},{6,7},{7,6},{8,9},{9,8},{10,11... | collective-permute-start | bytes 393224 | tf_op jit(solution)/shard_map/ppermute | solution.py:36
  25.0 5.1 %collective-permute-start.6 = (bf16[256,256]{1,0:T(8,128)(2,1)S(1)}, bf16[256,256]{1,0:T(8,128)(2,1)S(1)}, u32[]{:S(2)}, u32[]{:S(2)}) collective-permute-start(bf16[256,256]{1,0:T(8,128)(2,1)S(1)} %slice_bitcast_fusion), channel_id=1, source_target_pairs={{0,3},{1,2},{2,1},{3,0},{4,7},{5,6},{6,5},{7,4},{8,11},{9,10},{10,... | collective-permute-start | bytes 393224 | tf_op jit(solution)/shard_map/ppermute | solution.py:36
  25.1 6.9 %collective-permute-start.4 = (bf16[256,256]{1,0:T(8,128)(2,1)S(1)}, bf16[256,256]{1,0:T(8,128)(2,1)S(1)}, u32[]{:S(2)}, u32[]{:S(2)}) collective-permute-start(bf16[256,256]{1,0:T(8,128)(2,1)S(1)} %collective-permute-done.1.mine), channel_id=1, source_target_pairs={{0,4},{1,5},{2,6},{3,7},{4,0},{5,1},{6,2},{7,3},{8,12},{9,13},{10,... | collective-permute-start | bytes 393224 | tf_op jit(solution)/shard_map/ppermute | solution.py:36
  26.9 9.1 %collective-permute-start.8 = (bf16[256,256]{1,0:T(8,128)(2,1)S(1)}, bf16[256,256]{1,0:T(8,128)(2,1)S(1)}, u32[]{:S(2)}, u32[]{:S(2)}) collective-permute-start(bf16[256,256]{1,0:T(8,128)(2,1)S(1)} %collective-permute-done.7.mine), channel_id=1, source_target_pairs={{0,4},{1,5},{2,6},{3,7},{4,0},{5,1},{6,2},{7,3},{8,12},{9,13},{10,... | collective-permute-start | bytes 393224 | tf_op jit(solution)/shard_map/ppermute | solution.py:36
  29.5 9.9 %collective-permute-start.10 = (bf16[256,256]{1,0:T(8,128)(2,1)S(1)}, bf16[256,256]{1,0:T(8,128)(2,1)S(1)}, u32[]{:S(2)}, u32[]{:S(2)}) collective-permute-start(bf16[256,256]{1,0:T(8,128)(2,1)S(1)} %collective-permute-done.9.mine), channel_id=1, source_target_pairs={{0,4},{1,5},{2,6},{3,7},{4,0},{5,1},{6,2},{7,3},{8,12},{9,13},{10,... | collective-permute-start | bytes 393224 | tf_op jit(solution)/shard_map/ppermute | solution.py:36
  39.5 6.4 %copy-start.2 = (f32[4,256,256]{2,1,0:T(8,128)S(1)}, f32[4,256,256]{2,1,0:T(8,128)}, u32[]{:S(2)}) copy-start(f32[4,256,256]{2,1,0:T(8,128)} %measured_hbm.1) | copy-start | bytes 3145732
  41.7 4.1 %collective-permute-start.11 = (bf16[256,256]{1,0:T(8,128)(2,1)S(1)}, bf16[256,256]{1,0:T(8,128)(2,1)S(1)}, u32[]{:S(2)}, u32[]{:S(2)}) collective-permute-start(bf16[256,256]{1,0:T(8,128)(2,1)S(1)} %get-tuple-element.86), channel_id=1, source_target_pairs={{0,4},{1,5},{2,6},{3,7},{4,0},{5,1},{6,2},{7,3},{8,12},{9,13},{10,... | collective-permute-start | bytes 393224 | tf_op jit(solution)/shard_map/ppermute | solution.py:36
  55.0 5.1 %collective-permute-start.13 = (bf16[4,2,128,256]{3,2,1,0:T(8,128)(2,1)S(1)}, bf16[4,2,128,256]{3,2,1,0:T(8,128)(2,1)S(1)}, u32[]{:S(2)}, u32[]{:S(2)}) collective-permute-start(bf16[4,2,128,256]{3,2,1,0:T(8,128)(2,1)S(1)} %get-tuple-element.90), channel_id=1, source_target_pairs={{0,8},{8,0},{16,24},{24,16},{32,40},{40,32},{48,56},{56,48},{64,72... | collective-permute-start | bytes 1572872 | tf_op jit(solution)/shard_map/ppermute | solution.py:36
  58.5 10.7 %collective-permute-start.12 = (bf16[3,2,128,256]{3,2,1,0:T(8,128)(2,1)S(1)}, bf16[3,2,128,256]{3,2,1,0:T(8,128)(2,1)S(1)}, u32[]{:S(2)}, u32[]{:S(2)}) collective-permute-start(bf16[3,2,128,256]{3,2,1,0:T(8,128)(2,1)S(1)} %get-tuple-element.88), channel_id=1, source_target_pairs={{0,4},{1,5},{2,6},{3,7},{4,0},{5,1},{6,2},{7,3},{8,12},{9,13},{10,... | collective-permute-start | bytes 1179656 | tf_op jit(solution)/shard_map/ppermute | solution.py:36
  60.2 6.2 %collective-permute-start.14 = (bf16[2,128,256]{2,1,0:T(8,128)(2,1)S(1)}, bf16[2,128,256]{2,1,0:T(8,128)(2,1)S(1)}, u32[]{:S(2)}, u32[]{:S(2)}) collective-permute-start(bf16[2,128,256]{2,1,0:T(8,128)(2,1)S(1)} %get-tuple-element.92), channel_id=1, source_target_pairs={{0,1},{1,0},{2,3},{3,2},{4,5},{5,4},{6,7},{7,6},{8,9},{9,8},{10,11... | collective-permute-start | bytes 393224 | tf_op jit(solution)/shard_map/ppermute | solution.py:36
  62.8 5.6 %collective-permute-start.15 = (bf16[2,128,256]{2,1,0:T(8,128)(2,1)S(1)}, bf16[2,128,256]{2,1,0:T(8,128)(2,1)S(1)}, u32[]{:S(2)}, u32[]{:S(2)}) collective-permute-start(bf16[2,128,256]{2,1,0:T(8,128)(2,1)S(1)} %get-tuple-element.93), channel_id=1, source_target_pairs={{0,3},{1,2},{2,1},{3,0},{4,7},{5,6},{6,5},{7,4},{8,11},{9,10},{10,... | collective-permute-start | bytes 393224 | tf_op jit(solution)/shard_map/ppermute | solution.py:36
  68.5 6.8 %collective-permute-start.19 = (bf16[128,256]{1,0:T(8,128)(2,1)S(1)}, bf16[128,256]{1,0:T(8,128)(2,1)S(1)}, u32[]{:S(2)}, u32[]{:S(2)}) collective-permute-start(bf16[128,256]{1,0:T(8,128)(2,1)S(1)} %get-tuple-element.106), channel_id=1, source_target_pairs={{0,3},{1,2},{2,1},{3,0},{4,7},{5,6},{6,5},{7,4},{8,11},{9,10},{10,... | collective-permute-start | bytes 196616 | tf_op jit(solution)/shard_map/ppermute | solution.py:36
  68.9 6.3 %collective-permute-start.20 = (bf16[128,256]{1,0:T(8,128)(2,1)S(1)}, bf16[128,256]{1,0:T(8,128)(2,1)S(1)}, u32[]{:S(2)}, u32[]{:S(2)}) collective-permute-start(bf16[128,256]{1,0:T(8,128)(2,1)S(1)} %get-tuple-element.107), channel_id=1, source_target_pairs={{0,1},{1,0},{2,3},{3,2},{4,5},{5,4},{6,7},{7,6},{8,9},{9,8},{10,11... | collective-permute-start | bytes 196616 | tf_op jit(solution)/shard_map/ppermute | solution.py:36
  69.8 13.1 %collective-permute-start.16 = (bf16[3,2,32,256]{3,2,1,0:T(8,128)(2,1)S(1)}, bf16[3,2,32,256]{3,2,1,0:T(8,128)(2,1)S(1)}, u32[]{:S(2)}, u32[]{:S(2)}) collective-permute-start(bf16[3,2,32,256]{3,2,1,0:T(8,128)(2,1)S(1)} %get-tuple-element.102), channel_id=1, source_target_pairs={{0,1},{1,0},{2,3},{3,2},{4,5},{5,4},{6,7},{7,6},{8,9},{9,8},{10,11... | collective-permute-start | bytes 294920 | tf_op jit(solution)/shard_map/ppermute | solution.py:36
  72.5 10.5 %collective-permute-start.17 = (bf16[3,2,32,256]{3,2,1,0:T(8,128)(2,1)S(1)}, bf16[3,2,32,256]{3,2,1,0:T(8,128)(2,1)S(1)}, u32[]{:S(2)}, u32[]{:S(2)}) collective-permute-start(bf16[3,2,32,256]{3,2,1,0:T(8,128)(2,1)S(1)} %get-tuple-element.103), channel_id=1, source_target_pairs={{0,2},{1,3},{2,0},{3,1},{4,6},{5,7},{6,4},{7,5},{8,10},{9,11},{10,... | collective-permute-start | bytes 294920 | tf_op jit(solution)/shard_map/ppermute | solution.py:36
  73.5 9.4 %collective-permute-start.18 = (bf16[3,2,32,256]{3,2,1,0:T(8,128)(2,1)S(1)}, bf16[3,2,32,256]{3,2,1,0:T(8,128)(2,1)S(1)}, u32[]{:S(2)}, u32[]{:S(2)}) collective-permute-start(bf16[3,2,32,256]{3,2,1,0:T(8,128)(2,1)S(1)} %get-tuple-element.104), channel_id=1, source_target_pairs={{0,3},{1,2},{2,1},{3,0},{4,7},{5,6},{6,5},{7,4},{8,11},{9,10},{10,... | collective-permute-start | bytes 294920 | tf_op jit(solution)/shard_map/ppermute | solution.py:36
  75.8 3.1 %collective-permute-start.21 = (bf16[2,32,256]{2,1,0:T(8,128)(2,1)S(1)}, bf16[2,32,256]{2,1,0:T(8,128)(2,1)S(1)}, u32[]{:S(2)}, u32[]{:S(2)}) collective-permute-start(bf16[2,32,256]{2,1,0:T(8,128)(2,1)S(1)} %get-tuple-element.109), channel_id=1, source_target_pairs={{0,64},{8,72},{16,80},{24,88},{32,96},{40,104},{48,112},{56,120},{... | collective-permute-start | bytes 98312 | tf_op jit(solution)/shard_map/ppermute | solution.py:36
  75.9 4.4 %collective-permute-start.22 = (bf16[2,32,256]{2,1,0:T(8,128)(2,1)S(1)}, bf16[2,32,256]{2,1,0:T(8,128)(2,1)S(1)}, u32[]{:S(2)}, u32[]{:S(2)}) collective-permute-start(bf16[2,32,256]{2,1,0:T(8,128)(2,1)S(1)} %get-tuple-element.110), channel_id=1, source_target_pairs={{0,128},{8,136},{16,144},{24,152},{32,160},{40,168},{48,176},{56,1... | collective-permute-start | bytes 98312 | tf_op jit(solution)/shard_map/ppermute | solution.py:36
  79.0 4.0 %collective-permute-start.23 = (bf16[2,32,256]{2,1,0:T(8,128)(2,1)S(1)}, bf16[2,32,256]{2,1,0:T(8,128)(2,1)S(1)}, u32[]{:S(2)}, u32[]{:S(2)}) collective-permute-start(bf16[2,32,256]{2,1,0:T(8,128)(2,1)S(1)} %get-tuple-element.111), channel_id=1, source_target_pairs={{0,192},{8,200},{16,208},{24,216},{32,224},{40,232},{48,240},{56,2... | collective-permute-start | bytes 98312 | tf_op jit(solution)/shard_map/ppermute | solution.py:36
  83.0 6.6 %collective-permute-start.26 = (bf16[2,32,256]{2,1,0:T(8,128)(2,1)S(1)}, bf16[2,32,256]{2,1,0:T(8,128)(2,1)S(1)}, u32[]{:S(2)}, u32[]{:S(2)}) collective-permute-start(bf16[2,32,256]{2,1,0:T(8,128)(2,1)S(1)} %add_convert_fusion.1), channel_id=1, source_target_pairs={{0,48},{8,56},{16,32},{24,40},{32,16},{40,24},{48,0},{56,8},{64,11... | collective-permute-start | bytes 98312 | tf_op jit(solution)/shard_map/ppermute | solution.py:36
  85.0 6.7 %collective-permute-start.25 = (bf16[2,32,256]{2,1,0:T(8,128)(2,1)S(1)}, bf16[2,32,256]{2,1,0:T(8,128)(2,1)S(1)}, u32[]{:S(2)}, u32[]{:S(2)}) collective-permute-start(bf16[2,32,256]{2,1,0:T(8,128)(2,1)S(1)} %add_convert_fusion.1), channel_id=1, source_target_pairs={{0,32},{8,40},{16,48},{24,56},{32,0},{40,8},{48,16},{56,24},{64,96... | collective-permute-start | bytes 98312 | tf_op jit(solution)/shard_map/ppermute | solution.py:36
  85.8 5.8 %collective-permute-start.24 = (bf16[2,32,256]{2,1,0:T(8,128)(2,1)S(1)}, bf16[2,32,256]{2,1,0:T(8,128)(2,1)S(1)}, u32[]{:S(2)}, u32[]{:S(2)}) collective-permute-start(bf16[2,32,256]{2,1,0:T(8,128)(2,1)S(1)} %add_convert_fusion.1), channel_id=1, source_target_pairs={{0,16},{8,24},{16,0},{24,8},{32,48},{40,56},{48,32},{56,40},{64,80... | collective-permute-start | bytes 98312 | tf_op jit(solution)/shard_map/ppermute | solution.py:36
  91.7 15.7 %collective-permute-start.27 = (bf16[3,2,32,512]{3,2,1,0:T(8,128)(2,1)S(1)}, bf16[3,2,32,512]{3,2,1,0:T(8,128)(2,1)S(1)}, u32[]{:S(2)}, u32[]{:S(2)}) collective-permute-start(bf16[3,2,32,512]{3,2,1,0:T(8,128)(2,1)S(1)} %get-tuple-element.122), channel_id=1, source_target_pairs={{0,8},{8,16},{16,24},{24,32},{32,40},{40,48},{48,56},{56,64},{64,7... | collective-permute-start | bytes 589832 | tf_op jit(solution)/shard_map/ppermute | solution.py:41
  97.5 4.0 %collective-permute-start.30 = (bf16[2,32,256]{2,1,0:T(8,128)(2,1)S(1)}, bf16[2,32,256]{2,1,0:T(8,128)(2,1)S(1)}, u32[]{:S(2)}, u32[]{:S(2)}) collective-permute-start(bf16[2,32,256]{2,1,0:T(8,128)(2,1)S(1)} %add_convert_fusion.part0), channel_id=1, source_target_pairs={{0,192},{8,200},{16,208},{24,216},{32,224},{40,232},{48,240},{56,2... | collective-permute-start | bytes 98312 | tf_op jit(solution)/shard_map/ppermute | solution.py:36
  98.3 4.6 %collective-permute-start.29 = (bf16[2,32,256]{2,1,0:T(8,128)(2,1)S(1)}, bf16[2,32,256]{2,1,0:T(8,128)(2,1)S(1)}, u32[]{:S(2)}, u32[]{:S(2)}) collective-permute-start(bf16[2,32,256]{2,1,0:T(8,128)(2,1)S(1)} %add_convert_fusion.part0), channel_id=1, source_target_pairs={{0,128},{8,136},{16,144},{24,152},{32,160},{40,168},{48,176},{56,1... | collective-permute-start | bytes 98312 | tf_op jit(solution)/shard_map/ppermute | solution.py:36
  98.3 4.6 %collective-permute-start.28 = (bf16[2,32,256]{2,1,0:T(8,128)(2,1)S(1)}, bf16[2,32,256]{2,1,0:T(8,128)(2,1)S(1)}, u32[]{:S(2)}, u32[]{:S(2)}) collective-permute-start(bf16[2,32,256]{2,1,0:T(8,128)(2,1)S(1)} %add_convert_fusion.part0), channel_id=1, source_target_pairs={{0,64},{8,72},{16,80},{24,88},{32,96},{40,104},{48,112},{56,120},{... | collective-permute-start | bytes 98312 | tf_op jit(solution)/shard_map/ppermute | solution.py:36
  103.4 2.6 %collective-permute-start.31 = (bf16[2,128,256]{2,1,0:T(8,128)(2,1)S(1)}, bf16[2,128,256]{2,1,0:T(8,128)(2,1)S(1)}, u32[]{:S(2)}, u32[]{:S(2)}) collective-permute-start(bf16[2,128,256]{2,1,0:T(8,128)(2,1)S(1)} %shard_map.79.own), channel_id=1, source_target_pairs={{0,8},{8,0},{16,24},{24,16},{32,40},{40,32},{48,56},{56,48},{64,72... | collective-permute-start | bytes 393224 | tf_op jit(solution)/shard_map/ppermute | solution.py:36

commit v4 on v3

--- a/solution.py
+++ b/solution.py
@@ -368,11 +368,11 @@
         (which, table, object_slices),
         1,
     )
-    above, probe = lax.optimization_barrier((above, probe_modes[0]))
+    above, probe, picked = lax.optimization_barrier((above, probe_modes[0], picked))
     chosen = call(choose_kernel, [(square, BF)] * DEPTH, (which, above, object_slices), 2)
     mine = [shift(part, "tile", -1) for part in chosen]
     one, three = (swap(probe, "mode", step) for step in (1, 3))
-    mine[0], one, three, picked = lax.optimization_barrier((mine[0], one, three, picked))
+    mine[0], one, three = lax.optimization_barrier((mine[0], one, three))
     two = [swap(three[0], "mode", 1), swap(one[1], "mode", 3)]
     other = [swap(part, "mode", 4) for part in mine]
 

time: 108 us -> 107 us (level)
  starting transfers between devices: 50.4 us -> 47.9 us
    ppermute x5, starting transfers between devices: 19.7 us -> 17 us  [shift(): lax.ppermute(block, axis, [(i, (i + distance) % size) for i in range(size)])]
    ppermute x27, waiting for transfers between devices: 23.4 us -> 25.1 us  [swap(): return lax.ppermute(block, axis, route)]
    unnamed x11 -> x9, local copies, waits for them, and re-layouts: 3.14 us -> 3.14 us
  transfers between devices with their start and end apart: 32 -> 32, of which waited for: 17 -> 16; matrix products, arithmetic and copies ran while one was open for 0% -> 0% of each run, Pallas kernels for 13% -> 13%
where the time goes in v4:
time: 107 us
  starting transfers between devices  47.9 us (45%)
  waiting for transfers between devices  28.8 us (27%)
  Pallas kernels  25 us (23%)
  local copies, waits for them, and re-layouts  3.32 us (3%)
    ppermute x27, starting transfers between devices, swap(): return lax.ppermute(block, axis, route)  31 us
    ppermute x27, waiting for transfers between devices, swap(): return lax.ppermute(block, axis, route)  25.1 us
    ppermute x5, starting transfers between devices, shift(): lax.ppermute(block, axis, [(i, (i + distance) % size) for i in range(size)])  17 us
    pallas_call x12, Pallas kernels, call(): pl.pallas_call(kernel, out_shape=[jax.ShapeDtypeStruct(shape, dtype) for...  15.9 us
    pallas_call x1, Pallas kernels, on_device(): pl.pallas_call(backward_kernel, out_shape=[jax.ShapeDtypeStruct(*out) for...  9.12 us
    ppermute x5, waiting for transfers between devices, shift(): lax.ppermute(block, axis, [(i, (i + distance) % size) for i in range(size)])  3.63 us
    unnamed x9, local copies, waits for them, and re-layouts  3.14 us
  transfers between devices with their start and end apart: 32, of which 16 were waited for; matrix products, arithmetic and copies ran while one was open for 0% of the time, Pallas kernels for 13%

profile of v4, /device:TPU:1, one launch (start us, length us, event | category | flops | bytes accessed | tf_op | source)
XLA Modules:
  0.0 106.7 jit_solution(16684571602161970478)
XLA Ops:
  0.6 0.8 copy.9
  1.4 4.4 %collective-permute-start = (s32[4,2]{1,0:T(4,128)S(1)}, s32[4,2]{1,0:T(4,128)S(1)}, u32[]{:S(2)}, u32[]{:S(2)}) collective-permute-start(s32[4,2]{1,0:T(4,128)S(1)} %copy.9), channel_id=1, source_target_pairs={{0,8},{8,16},{16,24},{24,32},{32,40},{40,48},{48,56},{56,64},{64,7... | collective-permute-start | bytes 104 | tf_op jit(solution)/shard_map/ppermute | solution.py:41
  5.8 0.1 reshape.7
  5.9 0.1 concatenate.3.which
  5.9 1.4 %copy-done = bf16[3,2,256,512]{3,2,1,0:T(8,128)(2,1)S(1)} copy-done((bf16[3,2,256,512]{3,2,1,0:T(8,128)(2,1)S(1)}, bf16[3,2,256,512]{3,2,1,0:T(8,128)(2,1)}, u32[]{:S(2)}) %copy-start) | copy-done | bytes 1572888
  7.4 0.9 copy-done.3
  8.3 1.3 %shard_map.68 = (bf16[512,512]{1,0:T(8,128)(2,1)S(1)}, bf16[512,512]{1,0:T(8,128)(2,1)S(1)}, bf16[512,512]{1,0:T(8,128)(2,1)S(1)}, bf16[512,512]{1,0:T(8,128)(2,...) custom-call(s32[12]{0:T(128)S(1)} %concatenate.3.which, bf16[256,512]{1,0:T(8,128)(2,1)S(1)} %copy-done.3, ...), custom_call_target="tpu_custom_call" | custom-call | tf_op jit(solution)/shard_map/pallas_call | solution.py:339
  9.6 0.0 collective-permute-done.above
  9.6 2.8 %collective-permute-start.3 = (bf16[2,256,256]{2,1,0:T(8,128)(2,1)}, bf16[2,256,256]{2,1,0:T(8,128)(2,1)S(1)}, u32[]{:S(2)}, u32[]{:S(2)}) collective-permute-start(bf16[2,256,256]{2,1,0:T(8,128)(2,1)} %bitcast.9), channel_id=1, source_target_pairs={{0,3},{1,2},{2,1},{3,0},{4,7},{5,6},{6,5},{7,4},{8,11},{9,10},{10,... | collective-permute-start | bytes 786440 | tf_op jit(solution)/shard_map/ppermute | solution.py:36
  12.4 0.0 collective-permute-start.2
  12.4 0.7 shard_map.69
  13.1 2.9 %collective-permute-start.1 = (bf16[256,256]{1,0:T(8,128)(2,1)S(1)}, bf16[256,256]{1,0:T(8,128)(2,1)S(1)}, u32[]{:S(2)}, u32[]{:S(2)}) collective-permute-start(bf16[256,256]{1,0:T(8,128)(2,1)S(1)} %get-tuple-element.66), channel_id=1, source_target_pairs={{0,248},{8,0},{16,8},{24,16},{32,24},{40,32},{48,40},{56,48},{64,5... | collective-permute-start | bytes 393224 | tf_op jit(solution)/shard_map/ppermute | solution.py:41
  16.0 2.2 %collective-permute-start.7 = (bf16[256,256]{1,0:T(8,128)(2,1)S(1)}, bf16[256,256]{1,0:T(8,128)(2,1)S(1)}, u32[]{:S(2)}, u32[]{:S(2)}) collective-permute-start(bf16[256,256]{1,0:T(8,128)(2,1)S(1)} %get-tuple-element.77), channel_id=1, source_target_pairs={{0,248},{8,0},{16,8},{24,16},{32,24},{40,32},{48,40},{56,48},{64,5... | collective-permute-start | bytes 393224 | tf_op jit(solution)/shard_map/ppermute | solution.py:41
  18.2 1.1 %collective-permute-start.9 = (bf16[256,256]{1,0:T(8,128)(2,1)S(1)}, bf16[256,256]{1,0:T(8,128)(2,1)S(1)}, u32[]{:S(2)}, u32[]{:S(2)}) collective-permute-start(bf16[256,256]{1,0:T(8,128)(2,1)S(1)} %get-tuple-element.80), channel_id=1, source_target_pairs={{0,248},{8,0},{16,8},{24,16},{32,24},{40,32},{48,40},{56,48},{64,5... | collective-permute-start | bytes 393224 | tf_op jit(solution)/shard_map/ppermute | solution.py:41
  19.4 1.7 %collective-permute-start.5 = (bf16[256,256]{1,0:T(8,128)(2,1)S(1)}, bf16[256,256]{1,0:T(8,128)(2,1)S(1)}, u32[]{:S(2)}, u32[]{:S(2)}) collective-permute-start(bf16[256,256]{1,0:T(8,128)(2,1)S(1)} %slice_bitcast_fusion.1), channel_id=1, source_target_pairs={{0,1},{1,0},{2,3},{3,2},{4,5},{5,4},{6,7},{7,6},{8,9},{9,8},{10,11... | collective-permute-start | bytes 393224 | tf_op jit(solution)/shard_map/ppermute | solution.py:36
  21.1 0.1 collective-permute-start.6
  21.2 0.8 collective-permute-start.4
  22.0 0.8 collective-permute-done.7.mine
  22.8 2.8 %collective-permute-done.9.mine = bf16[256,256]{1,0:T(8,128)(2,1)S(1)} collective-permute-done((bf16[256,256]{1,0:T(8,128)(2,1)S(1)}, bf16[256,256]{1,0:T(8,128)(2,1)S(1)}, u32[]{:S(2)}, u32[]{:S(2)}) %collective-permute-start.9) | collective-permute-done | bytes 131104 | tf_op jit(solution)/shard_map/ppermute | solution.py:41
  25.6 0.0 collective-permute-start.10
  25.6 0.6 collective-permute-done.6.refs_8_
  26.2 1.6 %collective-permute-done.4.other = bf16[256,256]{1,0:T(8,128)(2,1)S(1)} collective-permute-done((bf16[256,256]{1,0:T(8,128)(2,1)S(1)}, bf16[256,256]{1,0:T(8,128)(2,1)S(1)}, u32[]{:S(2)}, u32[]{:S(2)}) %collective-permute-start.4) | collective-permute-done | bytes 131104 | tf_op jit(solution)/shard_map/ppermute | solution.py:36
  27.8 4.0 %shard_map.70 = (bf16[2,256,256]{2,1,0:T(8,128)(2,1)S(1)}, bf16[4,2,256,256]{3,2,1,0:T(8,128)(2,1)S(1)}, bf16[4,2,256,256]{3,2,1,0:T(8,128)(2,1)S(1)}) custom-call(s32[12]{0:T(128)S(1)} %concatenate.3.which, bf16[3,2,256,256]{3,2,1,0:T(8,128)(2,1)S(1)} %get-tuple-element.64.picked, bf16[256,256]{1,0:T(8,128)(2,1)S(1)} %collective-permute-done.1.mine, ...), custom_call_target="tpu_custom_call" | custom-call | tf_op jit(solution)/shard_map/pallas_call | solution.py:339
  31.9 3.5 %shard_map.71 = (bf16[2,256,256]{2,1,0:T(8,128)(2,1)S(1)}, bf16[4,2,256,256]{3,2,1,0:T(8,128)(2,1)S(1)}) custom-call(s32[12]{0:T(128)S(1)} %concatenate.3.which, bf16[3,2,256,256]{3,2,1,0:T(8,128)(2,1)S(1)} %get-tuple-element.64.picked, bf16[256,256]{1,0:T(8,128)(2,1)S(1)} %collective-permute-done.7.mine, bf16[256,256]{1,0:T(8,128)(2,1)S(1)} %collective-permute-done.8.other, ...), custom_call_target="tpu_custom_call" | custom-call | tf_op jit(solution)/shard_map/pallas_call | solution.py:339
  35.3 0.0 copy-start.1
  35.4 2.2 %shard_map.72 = (bf16[2,256,256]{2,1,0:T(8,128)(2,1)S(1)}, f32[4,2,256,256]{3,2,1,0:T(8,128)S(1)}, f32[256,256]{1,0:T(8,128)S(1)}, bf16[256,256]{1,0:T(8,128)(2,1)S(1)}) custom-call(s32[12]{0:T(128)S(1)} %concatenate.3.which, bf16[3,2,256,256]{3,2,1,0:T(8,128)(2,1)S(1)} %get-tuple-element.64.picked, bf16[256,256]{1,0:T(8,128)(2,1)S(1)} %collective-permute-done.9.mine, ...), custom_call_target="tpu_custom_call" | custom-call | tf_op jit(solution)/shard_map/pallas_call | solution.py:339
  37.6 0.3 collective-permute-start.11
  37.9 3.8 %collective-permute-done.11.total_got = bf16[256,256]{1,0:T(8,128)(2,1)S(1)} collective-permute-done((bf16[256,256]{1,0:T(8,128)(2,1)S(1)}, bf16[256,256]{1,0:T(8,128)(2,1)S(1)}, u32[]{:S(2)}, u32[]{:S(2)}) %collective-permute-start.11) | collective-permute-done | bytes 131104 | tf_op jit(solution)/shard_map/ppermute | solution.py:36
  41.7 9.1 %shard_map.73 = (bf16[3,2,128,256]{3,2,1,0:T(8,128)(2,1)S(1)}, bf16[3,2,128,256]{3,2,1,0:T(8,128)(2,1)S(1)}, bf16[4,2,128,256]{3,2,1,0:T(8,128)(2,1)S(1)}, bf16[4,2,128,256]{3,2,1,0:T(8,128)(2,1)S(1)}) custom-call(s32[12]{0:T(128)S(1)} %concatenate.3.which, bf16[2,256,256]{2,1,0:T(8,128)(2,1)S(1)} %get-tuple-element.76.window0, ...), custom_call_target="tpu_custom_call" | custom-call | tf_op jit(solution)/shard_map/pallas_call | solution.py:403
  50.8 5.9 %collective-permute-start.13 = (bf16[4,2,128,256]{3,2,1,0:T(8,128)(2,1)S(1)}, bf16[4,2,128,256]{3,2,1,0:T(8,128)(2,1)S(1)}, u32[]{:S(2)}, u32[]{:S(2)}) collective-permute-start(bf16[4,2,128,256]{3,2,1,0:T(8,128)(2,1)S(1)} %get-tuple-element.90), channel_id=1, source_target_pairs={{0,8},{8,0},{16,24},{24,16},{32,40},{40,32},{48,56},{56,48},{64,72... | collective-permute-start | bytes 1572872 | tf_op jit(solution)/shard_map/ppermute | solution.py:36
  56.7 1.5 %collective-permute-done.13.got = bf16[4,2,128,256]{3,2,1,0:T(8,128)(2,1)S(1)} collective-permute-done((bf16[4,2,128,256]{3,2,1,0:T(8,128)(2,1)S(1)}, bf16[4,2,128,256]{3,2,1,0:T(8,128)(2,1)S(1)}, u32[]{:S(2)}, u32[]{:S(2)}) %collective-permute-start.13) | collective-permute-done | bytes 524320 | tf_op jit(solution)/shard_map/ppermute | solution.py:36
  58.2 0.1 shard_map.74
  58.4 2.4 %collective-permute-start.14 = (bf16[2,128,256]{2,1,0:T(8,128)(2,1)S(1)}, bf16[2,128,256]{2,1,0:T(8,128)(2,1)S(1)}, u32[]{:S(2)}, u32[]{:S(2)}) collective-permute-start(bf16[2,128,256]{2,1,0:T(8,128)(2,1)S(1)} %get-tuple-element.92), channel_id=1, source_target_pairs={{0,1},{1,0},{2,3},{3,2},{4,5},{5,4},{6,7},{7,6},{8,9},{9,8},{10,11... | collective-permute-start | bytes 393224 | tf_op jit(solution)/shard_map/ppermute | solution.py:36
  60.8 3.6 %collective-permute-done.14.got_one = bf16[2,128,256]{2,1,0:T(8,128)(2,1)S(1)} collective-permute-done((bf16[2,128,256]{2,1,0:T(8,128)(2,1)S(1)}, bf16[2,128,256]{2,1,0:T(8,128)(2,1)S(1)}, u32[]{:S(2)}, u32[]{:S(2)}) %collective-permute-start.14) | collective-permute-done | bytes 131104 | tf_op jit(solution)/shard_map/ppermute | solution.py:36
  64.4 2.0 %collective-permute-done.15.got_three = bf16[2,128,256]{2,1,0:T(8,128)(2,1)S(1)} collective-permute-done((bf16[2,128,256]{2,1,0:T(8,128)(2,1)S(1)}, bf16[2,128,256]{2,1,0:T(8,128)(2,1)S(1)}, u32[]{:S(2)}, u32[]{:S(2)}) %collective-permute-start.15) | collective-permute-done | bytes 131104 | tf_op jit(solution)/shard_map/ppermute | solution.py:36
  66.4 0.1 shard_map.75
  66.4 0.4 collective-permute-start.19
  66.9 0.5 collective-permute-done.12.got
  67.4 0.6 shard_map.76
  68.0 2.4 %collective-permute-start.16 = (bf16[3,2,32,256]{3,2,1,0:T(8,128)(2,1)S(1)}, bf16[3,2,32,256]{3,2,1,0:T(8,128)(2,1)S(1)}, u32[]{:S(2)}, u32[]{:S(2)}) collective-permute-start(bf16[3,2,32,256]{3,2,1,0:T(8,128)(2,1)S(1)} %get-tuple-element.102), channel_id=1, source_target_pairs={{0,1},{1,0},{2,3},{3,2},{4,5},{5,4},{6,7},{7,6},{8,9},{9,8},{10,11... | collective-permute-start | bytes 294920 | tf_op jit(solution)/shard_map/ppermute | solution.py:36
  70.4 1.0 collective-permute-start.17
  71.5 1.7 %collective-permute-start.18 = (bf16[3,2,32,256]{3,2,1,0:T(8,128)(2,1)S(1)}, bf16[3,2,32,256]{3,2,1,0:T(8,128)(2,1)S(1)}, u32[]{:S(2)}, u32[]{:S(2)}) collective-permute-start(bf16[3,2,32,256]{3,2,1,0:T(8,128)(2,1)S(1)} %get-tuple-element.104), channel_id=1, source_target_pairs={{0,3},{1,2},{2,1},{3,0},{4,7},{5,6},{6,5},{7,4},{8,11},{9,10},{10,... | collective-permute-start | bytes 294920 | tf_op jit(solution)/shard_map/ppermute | solution.py:36
  73.2 0.6 shard_map.77
  73.8 0.1 collective-permute-start.21
  73.9 1.4 %collective-permute-start.22 = (bf16[2,32,256]{2,1,0:T(8,128)(2,1)S(1)}, bf16[2,32,256]{2,1,0:T(8,128)(2,1)S(1)}, u32[]{:S(2)}, u32[]{:S(2)}) collective-permute-start(bf16[2,32,256]{2,1,0:T(8,128)(2,1)S(1)} %get-tuple-element.110), channel_id=1, source_target_pairs={{0,128},{8,136},{16,144},{24,152},{32,160},{40,168},{48,176},{56,1... | collective-permute-start | bytes 98312 | tf_op jit(solution)/shard_map/ppermute | solution.py:36
  75.2 1.7 %collective-permute-done.21 = bf16[2,32,256]{2,1,0:T(8,128)(2,1)S(1)} collective-permute-done((bf16[2,32,256]{2,1,0:T(8,128)(2,1)S(1)}, bf16[2,32,256]{2,1,0:T(8,128)(2,1)S(1)}, u32[]{:S(2)}, u32[]{:S(2)}) %collective-permute-start.21) | collective-permute-done | bytes 32800 | tf_op jit(solution)/shard_map/ppermute | solution.py:36
  76.9 0.8 collective-permute-start.23
  77.7 0.5 collective-permute-done.22
  78.2 2.7 %collective-permute-done.23 = bf16[2,32,256]{2,1,0:T(8,128)(2,1)S(1)} collective-permute-done((bf16[2,32,256]{2,1,0:T(8,128)(2,1)S(1)}, bf16[2,32,256]{2,1,0:T(8,128)(2,1)S(1)}, u32[]{:S(2)}, u32[]{:S(2)}) %collective-permute-start.23) | collective-permute-done | bytes 32800 | tf_op jit(solution)/shard_map/ppermute | solution.py:36
  81.0 1.4 %collective-permute-start.26 = (bf16[2,32,256]{2,1,0:T(8,128)(2,1)S(1)}, bf16[2,32,256]{2,1,0:T(8,128)(2,1)S(1)}, u32[]{:S(2)}, u32[]{:S(2)}) collective-permute-start(bf16[2,32,256]{2,1,0:T(8,128)(2,1)S(1)} %add_convert_fusion.1), channel_id=1, source_target_pairs={{0,48},{8,56},{16,32},{24,40},{32,16},{40,24},{48,0},{56,8},{64,11... | collective-permute-start | bytes 98312 | tf_op jit(solution)/shard_map/ppermute | solution.py:36
  82.4 2.1 %collective-permute-start.25 = (bf16[2,32,256]{2,1,0:T(8,128)(2,1)S(1)}, bf16[2,32,256]{2,1,0:T(8,128)(2,1)S(1)}, u32[]{:S(2)}, u32[]{:S(2)}) collective-permute-start(bf16[2,32,256]{2,1,0:T(8,128)(2,1)S(1)} %add_convert_fusion.1), channel_id=1, source_target_pairs={{0,32},{8,40},{16,48},{24,56},{32,0},{40,8},{48,16},{56,24},{64,96... | collective-permute-start | bytes 98312 | tf_op jit(solution)/shard_map/ppermute | solution.py:36
  84.5 2.2 %collective-permute-start.24 = (bf16[2,32,256]{2,1,0:T(8,128)(2,1)S(1)}, bf16[2,32,256]{2,1,0:T(8,128)(2,1)S(1)}, u32[]{:S(2)}, u32[]{:S(2)}) collective-permute-start(bf16[2,32,256]{2,1,0:T(8,128)(2,1)S(1)} %add_convert_fusion.1), channel_id=1, source_target_pairs={{0,16},{8,24},{16,0},{24,8},{32,48},{40,56},{48,32},{56,40},{64,80... | collective-permute-start | bytes 98312 | tf_op jit(solution)/shard_map/ppermute | solution.py:36
  86.7 0.9 shard_map.78
  87.6 1.5 %collective-permute-done.25 = bf16[2,32,256]{2,1,0:T(8,128)(2,1)S(1)} collective-permute-done((bf16[2,32,256]{2,1,0:T(8,128)(2,1)S(1)}, bf16[2,32,256]{2,1,0:T(8,128)(2,1)S(1)}, u32[]{:S(2)}, u32[]{:S(2)}) %collective-permute-start.25) | collective-permute-done | bytes 32800 | tf_op jit(solution)/shard_map/ppermute | solution.py:36
  89.1 6.4 %collective-permute-start.27 = (bf16[3,2,32,512]{3,2,1,0:T(8,128)(2,1)S(1)}, bf16[3,2,32,512]{3,2,1,0:T(8,128)(2,1)S(1)}, u32[]{:S(2)}, u32[]{:S(2)}) collective-permute-start(bf16[3,2,32,512]{3,2,1,0:T(8,128)(2,1)S(1)} %get-tuple-element.122), channel_id=1, source_target_pairs={{0,8},{8,16},{16,24},{24,32},{32,40},{40,48},{48,56},{56,64},{64,7... | collective-permute-start | bytes 589832 | tf_op jit(solution)/shard_map/ppermute | solution.py:41
  95.5 1.8 %collective-permute-start.30 = (bf16[2,32,256]{2,1,0:T(8,128)(2,1)S(1)}, bf16[2,32,256]{2,1,0:T(8,128)(2,1)S(1)}, u32[]{:S(2)}, u32[]{:S(2)}) collective-permute-start(bf16[2,32,256]{2,1,0:T(8,128)(2,1)S(1)} %add_convert_fusion.part0), channel_id=1, source_target_pairs={{0,192},{8,200},{16,208},{24,216},{32,224},{40,232},{48,240},{56,2... | collective-permute-start | bytes 98312 | tf_op jit(solution)/shard_map/ppermute | solution.py:36
  97.3 1.5 %collective-permute-start.28 = (bf16[2,32,256]{2,1,0:T(8,128)(2,1)S(1)}, bf16[2,32,256]{2,1,0:T(8,128)(2,1)S(1)}, u32[]{:S(2)}, u32[]{:S(2)}) collective-permute-start(bf16[2,32,256]{2,1,0:T(8,128)(2,1)S(1)} %add_convert_fusion.part0), channel_id=1, source_target_pairs={{0,64},{8,72},{16,80},{24,88},{32,96},{40,104},{48,112},{56,120},{... | collective-permute-start | bytes 98312 | tf_op jit(solution)/shard_map/ppermute | solution.py:36
  98.7 0.7 collective-permute-done.30.part3
  99.5 3.1 %collective-permute-done.29.part2 = bf16[2,32,256]{2,1,0:T(8,128)(2,1)S(1)} collective-permute-done((bf16[2,32,256]{2,1,0:T(8,128)(2,1)S(1)}, bf16[2,32,256]{2,1,0:T(8,128)(2,1)S(1)}, u32[]{:S(2)}, u32[]{:S(2)}) %collective-permute-start.29) | collective-permute-done | bytes 32800 | tf_op jit(solution)/shard_map/ppermute | solution.py:36
  102.5 0.6 shard_map.79.own
  103.1 0.1 collective-permute-start.31
  103.2 1.3 %collective-permute-done.31.got = bf16[2,128,256]{2,1,0:T(8,128)(2,1)S(1)} collective-permute-done((bf16[2,128,256]{2,1,0:T(8,128)(2,1)S(1)}, bf16[2,128,256]{2,1,0:T(8,128)(2,1)S(1)}, u32[]{:S(2)}, u32[]{:S(2)}) %collective-permute-start.31) | collective-permute-done | bytes 131104 | tf_op jit(solution)/shard_map/ppermute | solution.py:36
  104.5 1.4 %shard_map.80 = f32[1,2,256,256]{3,2,1,0:T(8,128)} custom-call(s32[12]{0:T(128)S(1)} %concatenate.3.which, bf16[2,128,256]{2,1,0:T(8,128)(2,1)S(1)} %shard_map.79.own, bf16[2,128,256]{2,1,0:T(8,128)(2,1)S(1)} %collective-permute-done.31.got), custom_call_target="tpu_custom_call" | custom-call | tf_op jit(solution)/shard_map/pallas_call | solution.py:339
  105.9 0.8 convert_add_fusion
  (29 shorter events, 0.1 us)
Async XLA Ops:
  1.4 8.2 %collective-permute-start = (s32[4,2]{1,0:T(4,128)S(1)}, s32[4,2]{1,0:T(4,128)S(1)}, u32[]{:S(2)}, u32[]{:S(2)}) collective-permute-start(s32[4,2]{1,0:T(4,128)S(1)} %copy.9), channel_id=1, source_target_pairs={{0,8},{8,16},{16,24},{24,32},{32,40},{40,48},{48,56},{56,64},{64,7... | collective-permute-start | bytes 104 | tf_op jit(solution)/shard_map/ppermute | solution.py:41
  5.9 1.4 %copy-start = (bf16[3,2,256,512]{3,2,1,0:T(8,128)(2,1)S(1)}, bf16[3,2,256,512]{3,2,1,0:T(8,128)(2,1)}, u32[]{:S(2)}) copy-start(bf16[3,2,256,512]{3,2,1,0:T(8,128)(2,1)} %strip.3) | copy-start | bytes 4718596
  7.4 0.9 copy-start.3
  8.3 19.5 %copy-start.2 = (bf16[1,2,256,256]{3,2,1,0:T(8,128)(2,1)S(1)}, bf16[1,2,256,256]{3,2,1,0:T(8,128)(2,1)}, u32[]{:S(2)}) copy-start(bf16[1,2,256,256]{3,2,1,0:T(8,128)(2,1)} %param.6) | copy-start | bytes 786436
  9.6 9.7 %collective-permute-start.3 = (bf16[2,256,256]{2,1,0:T(8,128)(2,1)}, bf16[2,256,256]{2,1,0:T(8,128)(2,1)S(1)}, u32[]{:S(2)}, u32[]{:S(2)}) collective-permute-start(bf16[2,256,256]{2,1,0:T(8,128)(2,1)} %bitcast.9), channel_id=1, source_target_pairs={{0,3},{1,2},{2,1},{3,0},{4,7},{5,6},{6,5},{7,4},{8,11},{9,10},{10,... | collective-permute-start | bytes 786440 | tf_op jit(solution)/shard_map/ppermute | solution.py:36
  12.4 6.9 %collective-permute-start.2 = (bf16[2,256,256]{2,1,0:T(8,128)(2,1)}, bf16[2,256,256]{2,1,0:T(8,128)(2,1)S(1)}, u32[]{:S(2)}, u32[]{:S(2)}) collective-permute-start(bf16[2,256,256]{2,1,0:T(8,128)(2,1)} %bitcast.10), channel_id=1, source_target_pairs={{0,1},{1,0},{2,3},{3,2},{4,5},{5,4},{6,7},{7,6},{8,9},{9,8},{10,11... | collective-permute-start | bytes 786440 | tf_op jit(solution)/shard_map/ppermute | solution.py:36
  13.1 6.2 %collective-permute-start.1 = (bf16[256,256]{1,0:T(8,128)(2,1)S(1)}, bf16[256,256]{1,0:T(8,128)(2,1)S(1)}, u32[]{:S(2)}, u32[]{:S(2)}) collective-permute-start(bf16[256,256]{1,0:T(8,128)(2,1)S(1)} %get-tuple-element.66), channel_id=1, source_target_pairs={{0,248},{8,0},{16,8},{24,16},{32,24},{40,32},{48,40},{56,48},{64,5... | collective-permute-start | bytes 393224 | tf_op jit(solution)/shard_map/ppermute | solution.py:41
  16.0 6.8 %collective-permute-start.7 = (bf16[256,256]{1,0:T(8,128)(2,1)S(1)}, bf16[256,256]{1,0:T(8,128)(2,1)S(1)}, u32[]{:S(2)}, u32[]{:S(2)}) collective-permute-start(bf16[256,256]{1,0:T(8,128)(2,1)S(1)} %get-tuple-element.77), channel_id=1, source_target_pairs={{0,248},{8,0},{16,8},{24,16},{32,24},{40,32},{48,40},{56,48},{64,5... | collective-permute-start | bytes 393224 | tf_op jit(solution)/shard_map/ppermute | solution.py:41
  18.2 7.4 %collective-permute-start.9 = (bf16[256,256]{1,0:T(8,128)(2,1)S(1)}, bf16[256,256]{1,0:T(8,128)(2,1)S(1)}, u32[]{:S(2)}, u32[]{:S(2)}) collective-permute-start(bf16[256,256]{1,0:T(8,128)(2,1)S(1)} %get-tuple-element.80), channel_id=1, source_target_pairs={{0,248},{8,0},{16,8},{24,16},{32,24},{40,32},{48,40},{56,48},{64,5... | collective-permute-start | bytes 393224 | tf_op jit(solution)/shard_map/ppermute | solution.py:41
  19.4 6.3 %collective-permute-start.5 = (bf16[256,256]{1,0:T(8,128)(2,1)S(1)}, bf16[256,256]{1,0:T(8,128)(2,1)S(1)}, u32[]{:S(2)}, u32[]{:S(2)}) collective-permute-start(bf16[256,256]{1,0:T(8,128)(2,1)S(1)} %slice_bitcast_fusion.1), channel_id=1, source_target_pairs={{0,1},{1,0},{2,3},{3,2},{4,5},{5,4},{6,7},{7,6},{8,9},{9,8},{10,11... | collective-permute-start | bytes 393224 | tf_op jit(solution)/shard_map/ppermute | solution.py:36
  21.1 5.1 %collective-permute-start.6 = (bf16[256,256]{1,0:T(8,128)(2,1)S(1)}, bf16[256,256]{1,0:T(8,128)(2,1)S(1)}, u32[]{:S(2)}, u32[]{:S(2)}) collective-permute-start(bf16[256,256]{1,0:T(8,128)(2,1)S(1)} %slice_bitcast_fusion), channel_id=1, source_target_pairs={{0,3},{1,2},{2,1},{3,0},{4,7},{5,6},{6,5},{7,4},{8,11},{9,10},{10,... | collective-permute-start | bytes 393224 | tf_op jit(solution)/shard_map/ppermute | solution.py:36
  21.2 6.6 %collective-permute-start.4 = (bf16[256,256]{1,0:T(8,128)(2,1)S(1)}, bf16[256,256]{1,0:T(8,128)(2,1)S(1)}, u32[]{:S(2)}, u32[]{:S(2)}) collective-permute-start(bf16[256,256]{1,0:T(8,128)(2,1)S(1)} %collective-permute-done.1.mine), channel_id=1, source_target_pairs={{0,4},{1,5},{2,6},{3,7},{4,0},{5,1},{6,2},{7,3},{8,12},{9,13},{10,... | collective-permute-start | bytes 393224 | tf_op jit(solution)/shard_map/ppermute | solution.py:36
  22.8 9.1 %collective-permute-start.8 = (bf16[256,256]{1,0:T(8,128)(2,1)S(1)}, bf16[256,256]{1,0:T(8,128)(2,1)S(1)}, u32[]{:S(2)}, u32[]{:S(2)}) collective-permute-start(bf16[256,256]{1,0:T(8,128)(2,1)S(1)} %collective-permute-done.7.mine), channel_id=1, source_target_pairs={{0,4},{1,5},{2,6},{3,7},{4,0},{5,1},{6,2},{7,3},{8,12},{9,13},{10,... | collective-permute-start | bytes 393224 | tf_op jit(solution)/shard_map/ppermute | solution.py:36
  25.6 9.7 %collective-permute-start.10 = (bf16[256,256]{1,0:T(8,128)(2,1)S(1)}, bf16[256,256]{1,0:T(8,128)(2,1)S(1)}, u32[]{:S(2)}, u32[]{:S(2)}) collective-permute-start(bf16[256,256]{1,0:T(8,128)(2,1)S(1)} %collective-permute-done.9.mine), channel_id=1, source_target_pairs={{0,4},{1,5},{2,6},{3,7},{4,0},{5,1},{6,2},{7,3},{8,12},{9,13},{10,... | collective-permute-start | bytes 393224 | tf_op jit(solution)/shard_map/ppermute | solution.py:36
  35.3 6.4 %copy-start.1 = (f32[4,256,256]{2,1,0:T(8,128)S(1)}, f32[4,256,256]{2,1,0:T(8,128)}, u32[]{:S(2)}) copy-start(f32[4,256,256]{2,1,0:T(8,128)} %measured_hbm.1) | copy-start | bytes 3145732
  37.6 4.1 %collective-permute-start.11 = (bf16[256,256]{1,0:T(8,128)(2,1)S(1)}, bf16[256,256]{1,0:T(8,128)(2,1)S(1)}, u32[]{:S(2)}, u32[]{:S(2)}) collective-permute-start(bf16[256,256]{1,0:T(8,128)(2,1)S(1)} %get-tuple-element.86), channel_id=1, source_target_pairs={{0,4},{1,5},{2,6},{3,7},{4,0},{5,1},{6,2},{7,3},{8,12},{9,13},{10,... | collective-permute-start | bytes 393224 | tf_op jit(solution)/shard_map/ppermute | solution.py:36
  50.8 7.4 %collective-permute-start.13 = (bf16[4,2,128,256]{3,2,1,0:T(8,128)(2,1)S(1)}, bf16[4,2,128,256]{3,2,1,0:T(8,128)(2,1)S(1)}, u32[]{:S(2)}, u32[]{:S(2)}) collective-permute-start(bf16[4,2,128,256]{3,2,1,0:T(8,128)(2,1)S(1)} %get-tuple-element.90), channel_id=1, source_target_pairs={{0,8},{8,0},{16,24},{24,16},{32,40},{40,32},{48,56},{56,48},{64,72... | collective-permute-start | bytes 1572872 | tf_op jit(solution)/shard_map/ppermute | solution.py:36
  56.7 10.7 %collective-permute-start.12 = (bf16[3,2,128,256]{3,2,1,0:T(8,128)(2,1)S(1)}, bf16[3,2,128,256]{3,2,1,0:T(8,128)(2,1)S(1)}, u32[]{:S(2)}, u32[]{:S(2)}) collective-permute-start(bf16[3,2,128,256]{3,2,1,0:T(8,128)(2,1)S(1)} %get-tuple-element.88), channel_id=1, source_target_pairs={{0,4},{1,5},{2,6},{3,7},{4,0},{5,1},{6,2},{7,3},{8,12},{9,13},{10,... | collective-permute-start | bytes 1179656 | tf_op jit(solution)/shard_map/ppermute | solution.py:36
  58.4 6.0 %collective-permute-start.14 = (bf16[2,128,256]{2,1,0:T(8,128)(2,1)S(1)}, bf16[2,128,256]{2,1,0:T(8,128)(2,1)S(1)}, u32[]{:S(2)}, u32[]{:S(2)}) collective-permute-start(bf16[2,128,256]{2,1,0:T(8,128)(2,1)S(1)} %get-tuple-element.92), channel_id=1, source_target_pairs={{0,1},{1,0},{2,3},{3,2},{4,5},{5,4},{6,7},{7,6},{8,9},{9,8},{10,11... | collective-permute-start | bytes 393224 | tf_op jit(solution)/shard_map/ppermute | solution.py:36
  60.8 5.6 %collective-permute-start.15 = (bf16[2,128,256]{2,1,0:T(8,128)(2,1)S(1)}, bf16[2,128,256]{2,1,0:T(8,128)(2,1)S(1)}, u32[]{:S(2)}, u32[]{:S(2)}) collective-permute-start(bf16[2,128,256]{2,1,0:T(8,128)(2,1)S(1)} %get-tuple-element.93), channel_id=1, source_target_pairs={{0,3},{1,2},{2,1},{3,0},{4,7},{5,6},{6,5},{7,4},{8,11},{9,10},{10,... | collective-permute-start | bytes 393224 | tf_op jit(solution)/shard_map/ppermute | solution.py:36
  66.4 6.8 %collective-permute-start.19 = (bf16[128,256]{1,0:T(8,128)(2,1)S(1)}, bf16[128,256]{1,0:T(8,128)(2,1)S(1)}, u32[]{:S(2)}, u32[]{:S(2)}) collective-permute-start(bf16[128,256]{1,0:T(8,128)(2,1)S(1)} %get-tuple-element.106), channel_id=1, source_target_pairs={{0,3},{1,2},{2,1},{3,0},{4,7},{5,6},{6,5},{7,4},{8,11},{9,10},{10,... | collective-permute-start | bytes 196616 | tf_op jit(solution)/shard_map/ppermute | solution.py:36
  66.9 6.3 %collective-permute-start.20 = (bf16[128,256]{1,0:T(8,128)(2,1)S(1)}, bf16[128,256]{1,0:T(8,128)(2,1)S(1)}, u32[]{:S(2)}, u32[]{:S(2)}) collective-permute-start(bf16[128,256]{1,0:T(8,128)(2,1)S(1)} %get-tuple-element.107), channel_id=1, source_target_pairs={{0,1},{1,0},{2,3},{3,2},{4,5},{5,4},{6,7},{7,6},{8,9},{9,8},{10,11... | collective-permute-start | bytes 196616 | tf_op jit(solution)/shard_map/ppermute | solution.py:36
  68.0 12.9 %collective-permute-start.16 = (bf16[3,2,32,256]{3,2,1,0:T(8,128)(2,1)S(1)}, bf16[3,2,32,256]{3,2,1,0:T(8,128)(2,1)S(1)}, u32[]{:S(2)}, u32[]{:S(2)}) collective-permute-start(bf16[3,2,32,256]{3,2,1,0:T(8,128)(2,1)S(1)} %get-tuple-element.102), channel_id=1, source_target_pairs={{0,1},{1,0},{2,3},{3,2},{4,5},{5,4},{6,7},{7,6},{8,9},{9,8},{10,11... | collective-permute-start | bytes 294920 | tf_op jit(solution)/shard_map/ppermute | solution.py:36
  70.4 10.5 %collective-permute-start.17 = (bf16[3,2,32,256]{3,2,1,0:T(8,128)(2,1)S(1)}, bf16[3,2,32,256]{3,2,1,0:T(8,128)(2,1)S(1)}, u32[]{:S(2)}, u32[]{:S(2)}) collective-permute-start(bf16[3,2,32,256]{3,2,1,0:T(8,128)(2,1)S(1)} %get-tuple-element.103), channel_id=1, source_target_pairs={{0,2},{1,3},{2,0},{3,1},{4,6},{5,7},{6,4},{7,5},{8,10},{9,11},{10,... | collective-permute-start | bytes 294920 | tf_op jit(solution)/shard_map/ppermute | solution.py:36
  71.5 9.4 %collective-permute-start.18 = (bf16[3,2,32,256]{3,2,1,0:T(8,128)(2,1)S(1)}, bf16[3,2,32,256]{3,2,1,0:T(8,128)(2,1)S(1)}, u32[]{:S(2)}, u32[]{:S(2)}) collective-permute-start(bf16[3,2,32,256]{3,2,1,0:T(8,128)(2,1)S(1)} %get-tuple-element.104), channel_id=1, source_target_pairs={{0,3},{1,2},{2,1},{3,0},{4,7},{5,6},{6,5},{7,4},{8,11},{9,10},{10,... | collective-permute-start | bytes 294920 | tf_op jit(solution)/shard_map/ppermute | solution.py:36
  73.8 3.1 %collective-permute-start.21 = (bf16[2,32,256]{2,1,0:T(8,128)(2,1)S(1)}, bf16[2,32,256]{2,1,0:T(8,128)(2,1)S(1)}, u32[]{:S(2)}, u32[]{:S(2)}) collective-permute-start(bf16[2,32,256]{2,1,0:T(8,128)(2,1)S(1)} %get-tuple-element.109), channel_id=1, source_target_pairs={{0,64},{8,72},{16,80},{24,88},{32,96},{40,104},{48,112},{56,120},{... | collective-permute-start | bytes 98312 | tf_op jit(solution)/shard_map/ppermute | solution.py:36
  73.9 4.4 %collective-permute-start.22 = (bf16[2,32,256]{2,1,0:T(8,128)(2,1)S(1)}, bf16[2,32,256]{2,1,0:T(8,128)(2,1)S(1)}, u32[]{:S(2)}, u32[]{:S(2)}) collective-permute-start(bf16[2,32,256]{2,1,0:T(8,128)(2,1)S(1)} %get-tuple-element.110), channel_id=1, source_target_pairs={{0,128},{8,136},{16,144},{24,152},{32,160},{40,168},{48,176},{56,1... | collective-permute-start | bytes 98312 | tf_op jit(solution)/shard_map/ppermute | solution.py:36
  76.9 4.0 %collective-permute-start.23 = (bf16[2,32,256]{2,1,0:T(8,128)(2,1)S(1)}, bf16[2,32,256]{2,1,0:T(8,128)(2,1)S(1)}, u32[]{:S(2)}, u32[]{:S(2)}) collective-permute-start(bf16[2,32,256]{2,1,0:T(8,128)(2,1)S(1)} %get-tuple-element.111), channel_id=1, source_target_pairs={{0,192},{8,200},{16,208},{24,216},{32,224},{40,232},{48,240},{56,2... | collective-permute-start | bytes 98312 | tf_op jit(solution)/shard_map/ppermute | solution.py:36
  81.0 6.6 %collective-permute-start.26 = (bf16[2,32,256]{2,1,0:T(8,128)(2,1)S(1)}, bf16[2,32,256]{2,1,0:T(8,128)(2,1)S(1)}, u32[]{:S(2)}, u32[]{:S(2)}) collective-permute-start(bf16[2,32,256]{2,1,0:T(8,128)(2,1)S(1)} %add_convert_fusion.1), channel_id=1, source_target_pairs={{0,48},{8,56},{16,32},{24,40},{32,16},{40,24},{48,0},{56,8},{64,11... | collective-permute-start | bytes 98312 | tf_op jit(solution)/shard_map/ppermute | solution.py:36
  82.4 6.7 %collective-permute-start.25 = (bf16[2,32,256]{2,1,0:T(8,128)(2,1)S(1)}, bf16[2,32,256]{2,1,0:T(8,128)(2,1)S(1)}, u32[]{:S(2)}, u32[]{:S(2)}) collective-permute-start(bf16[2,32,256]{2,1,0:T(8,128)(2,1)S(1)} %add_convert_fusion.1), channel_id=1, source_target_pairs={{0,32},{8,40},{16,48},{24,56},{32,0},{40,8},{48,16},{56,24},{64,96... | collective-permute-start | bytes 98312 | tf_op jit(solution)/shard_map/ppermute | solution.py:36
  84.5 4.7 %collective-permute-start.24 = (bf16[2,32,256]{2,1,0:T(8,128)(2,1)S(1)}, bf16[2,32,256]{2,1,0:T(8,128)(2,1)S(1)}, u32[]{:S(2)}, u32[]{:S(2)}) collective-permute-start(bf16[2,32,256]{2,1,0:T(8,128)(2,1)S(1)} %add_convert_fusion.1), channel_id=1, source_target_pairs={{0,16},{8,24},{16,0},{24,8},{32,48},{40,56},{48,32},{56,40},{64,80... | collective-permute-start | bytes 98312 | tf_op jit(solution)/shard_map/ppermute | solution.py:36
  89.1 16.8 %collective-permute-start.27 = (bf16[3,2,32,512]{3,2,1,0:T(8,128)(2,1)S(1)}, bf16[3,2,32,512]{3,2,1,0:T(8,128)(2,1)S(1)}, u32[]{:S(2)}, u32[]{:S(2)}) collective-permute-start(bf16[3,2,32,512]{3,2,1,0:T(8,128)(2,1)S(1)} %get-tuple-element.122), channel_id=1, source_target_pairs={{0,8},{8,16},{16,24},{24,32},{32,40},{40,48},{48,56},{56,64},{64,7... | collective-permute-start | bytes 589832 | tf_op jit(solution)/shard_map/ppermute | solution.py:41
  95.5 4.0 %collective-permute-start.30 = (bf16[2,32,256]{2,1,0:T(8,128)(2,1)S(1)}, bf16[2,32,256]{2,1,0:T(8,128)(2,1)S(1)}, u32[]{:S(2)}, u32[]{:S(2)}) collective-permute-start(bf16[2,32,256]{2,1,0:T(8,128)(2,1)S(1)} %add_convert_fusion.part0), channel_id=1, source_target_pairs={{0,192},{8,200},{16,208},{24,216},{32,224},{40,232},{48,240},{56,2... | collective-permute-start | bytes 98312 | tf_op jit(solution)/shard_map/ppermute | solution.py:36
  97.3 5.3 %collective-permute-start.29 = (bf16[2,32,256]{2,1,0:T(8,128)(2,1)S(1)}, bf16[2,32,256]{2,1,0:T(8,128)(2,1)S(1)}, u32[]{:S(2)}, u32[]{:S(2)}) collective-permute-start(bf16[2,32,256]{2,1,0:T(8,128)(2,1)S(1)} %add_convert_fusion.part0), channel_id=1, source_target_pairs={{0,128},{8,136},{16,144},{24,152},{32,160},{40,168},{48,176},{56,1... | collective-permute-start | bytes 98312 | tf_op jit(solution)/shard_map/ppermute | solution.py:36
  97.3 5.3 %collective-permute-start.28 = (bf16[2,32,256]{2,1,0:T(8,128)(2,1)S(1)}, bf16[2,32,256]{2,1,0:T(8,128)(2,1)S(1)}, u32[]{:S(2)}, u32[]{:S(2)}) collective-permute-start(bf16[2,32,256]{2,1,0:T(8,128)(2,1)S(1)} %add_convert_fusion.part0), channel_id=1, source_target_pairs={{0,64},{8,72},{16,80},{24,88},{32,96},{40,104},{48,112},{56,120},{... | collective-permute-start | bytes 98312 | tf_op jit(solution)/shard_map/ppermute | solution.py:36
  103.1 1.4 %collective-permute-start.31 = (bf16[2,128,256]{2,1,0:T(8,128)(2,1)S(1)}, bf16[2,128,256]{2,1,0:T(8,128)(2,1)S(1)}, u32[]{:S(2)}, u32[]{:S(2)}) collective-permute-start(bf16[2,128,256]{2,1,0:T(8,128)(2,1)S(1)} %shard_map.79.own), channel_id=1, source_target_pairs={{0,8},{8,0},{16,24},{24,16},{32,40},{40,32},{48,56},{56,48},{64,72... | collective-permute-start | bytes 393224 | tf_op jit(solution)/shard_map/ppermute | solution.py:36
